TPU v7x, 512 devices: a whole 4x4x16 slice. The times are simulated.
512 devices in a mesh: dp: 4 (over z_lo), tm: 16 (over x, z_hi), expert: 8 (over y, core).
Axes of the slice: x: 4, y: 4, z: 16 (z_hi: 4, z_lo: 4; z = z_hi * 4 + z_lo), core: 2. Of those that a mesh axis runs over, the one named last changes fastest.
Arguments:
- decoder_in: bfloat16 [4, 16384, 2048], P('dp', ('tm', 'expert')), may hold values from -6 to 6
- enc_keys: bfloat16 [4, 16384, 2048], P('dp', ('tm', 'expert')), may hold values from -4 to 4
- enc_values: bfloat16 [4, 16384, 2048], P('dp', ('tm', 'expert')), may hold values from -4 to 4
- win_start: int32 [4, 16384], P('dp', ('tm', 'expert')), may hold values from 0 to 16383, as said below
- win_end: int32 [4, 16384], P('dp', ('tm', 'expert')), may hold values from 1 to 16384, as said below
- routes: int32 [4, 16384, 2], P('dp', ('tm', 'expert')), may hold values from 0 to 31, as said below
- gate_probs: float32 [4, 16384, 2], P('dp', ('tm', 'expert')), may hold values from 0.1 to 1
- w_up: bfloat16 [8, 2048, 2048], P('expert', 'tm', 'dp'), may hold values from -0.125 to 0.125
- w_down: bfloat16 [8, 2048, 2048], P('expert', 'dp', 'tm'), may hold values from -0.09375 to 0.09375
- cotangent: bfloat16 [4, 16384, 2048], P('dp', ('tm', 'expert')), may hold values from -6 to 6
Outputs:
- block_out: bfloat16 [4, 16384, 2048], P('dp', ('tm', 'expert'))
- grad_in: bfloat16 [4, 16384, 2048], P('dp', ('tm', 'expert'))
- grad_keys: bfloat16 [4, 16384, 2048], P('dp', ('tm', 'expert'))
- grad_values: bfloat16 [4, 16384, 2048], P('dp', ('tm', 'expert'))
Inputs may be any that keep to these rules, and one draw needn't show every extreme that they name: `win_start`: starts never fall along the tokens of a recording, and each token's window holds its own position and no frame more than 16 positions before the first token of its block of 128; in every draw and recording some token's window starts exactly 16 frames before its block. `win_end`: ends never fall along the tokens of a recording and lie after the token's own position, at most 16 frames past the last token of its block of 128; in every draw and recording some token's window ends exactly 16 frames past its block. `routes`: the two ids of a token differ. In each aligned block of 128 tokens any id below 4 is named at most 10 times; in every draw, for every recording and every index of tm, one id below 4 is named exactly 10 times in each of the 8 blocks of that index.
All inputs are finite; a program needn't handle non-finite values.
Results may differ from a plain program's by a relative error of at most 0.0063.
Values may be sent and summed in bfloat16 or wider, within the bound.
No kernel may reach another device: no remote copies, remote signals or barrier semaphores. Data moves between devices by JAX's collectives and lax.ppermute only.
A program may use at most 64 MiB of HBM per device.

v0:
```python
import math

import jax
import jax.numpy as jnp
from jax import lax
from jax.sharding import PartitionSpec as P

HEADS = 16
HD = 128
HALO = 16
SLOT_LIMIT = 10


NORM_EPS = 1e-06
ROOT_HALF = 1.0 / math.sqrt(2.0)
INV_ROOT_TWOPI = 1.0 / math.sqrt(2.0 * math.pi)


def with_halo(cells, sides, width):
    for axis, dim in sides:
        count = lax.axis_size(axis)
        ends = count - 1
        head = lax.slice_in_dim(cells, 0, width, axis=dim)
        tail = lax.slice_in_dim(cells, cells.shape[dim] - width, cells.shape[dim], axis=dim)
        cells = jnp.concatenate(
            [
                lax.ppermute(tail, axis, [(i, (i + 1) % count) for i in range(ends)]),
                cells,
                lax.ppermute(head, axis, [((i + 1) % count, i) for i in range(ends)]),
            ],
            axis=dim,
        )
    return cells


def gelu_parts(pre_act):
    gauss_cdf = 0.5 * (1.0 + jax.scipy.special.erf(pre_act * ROOT_HALF))
    slope = gauss_cdf + pre_act * jnp.exp(-0.5 * pre_act * pre_act) * INV_ROOT_TWOPI
    return (pre_act * gauss_cdf, slope)


def fetch_slices(up_local, down_local):
    return (
        lax.all_gather(up_local, "tm", axis=1, tiled=True),
        lax.all_gather(down_local, "tm", axis=2, tiled=True),
    )


def send_slots(slot_rows):
    experts, capacity, feat_width = slot_rows.shape
    copies = lax.axis_size("dp")
    spread = jnp.broadcast_to(slot_rows[None, :, None], (copies, experts, 2, capacity, feat_width))
    spread = spread.reshape(copies * experts * 2, capacity, feat_width)
    arrived = lax.all_to_all(spread, ("dp", "expert"), split_axis=0, concat_axis=0, tiled=True)
    return arrived.reshape(-1, feat_width)


def return_slots(results, capacity):
    feat_width = results.shape[-1]
    groups = results.shape[0] // capacity
    returned = lax.all_to_all(
        results.reshape(groups, capacity, feat_width),
        ("dp", "expert"),
        split_axis=0,
        concat_axis=0,
        tiled=True,
    )
    copies = lax.axis_size("dp")
    returned = returned.reshape(copies, groups // (2 * copies), 2, capacity, feat_width).astype(
        jnp.float32
    )
    return jnp.sum(returned, axis=(0, 2))


def shards(
    decoder_in,
    enc_keys,
    enc_values,
    win_start,
    win_end,
    routes,
    gate_probs,
    w_up,
    w_down,
    cotangent,
):
    tok_rows = decoder_in.shape[1]
    feat_width = decoder_in.shape[2]
    key_span = tok_rows + 2 * HALO
    experts = lax.axis_size("expert") // 2
    slot_count = experts * SLOT_LIMIT
    position = lax.axis_index(("tm", "expert"))
    key_value = jnp.stack([enc_keys[0], enc_values[0]])
    framed = with_halo(key_value, ((("tm", "expert"), 1),), HALO)
    first_frame = position * tok_rows - HALO
    frame = first_frame + jnp.arange(key_span, dtype=jnp.int32)
    inside = (frame[None, :] >= win_start[0][:, None]) & (frame[None, :] < win_end[0][:, None])
    key_heads = framed[0].reshape(key_span, HEADS, HD)
    val_heads = framed[1].reshape(key_span, HEADS, HD)
    input_f32 = decoder_in[0].astype(jnp.float32)
    heads_in = input_f32.reshape(tok_rows, HEADS, HD)
    scale_q = lax.rsqrt(jnp.mean(heads_in * heads_in, axis=-1, keepdims=True) + NORM_EPS)
    normed = heads_in * scale_q
    query_low = normed.astype(jnp.bfloat16)
    scores = jnp.einsum(
        "thd,fhd->htf", query_low, key_heads, preferred_element_type=jnp.float32
    ) * (1.0 / math.sqrt(HD))
    weights = jnp.exp(scores) * inside[None].astype(jnp.float32)
    att_probs = weights / jnp.sum(weights, axis=-1, keepdims=True)
    probs_low = att_probs.astype(jnp.bfloat16)
    context = jnp.einsum(
        "htf,fhd->thd", probs_low, val_heads, preferred_element_type=jnp.float32
    ).reshape(tok_rows, feat_width)
    hidden = input_f32 + context
    scale_h = lax.rsqrt(jnp.mean(hidden * hidden, axis=-1, keepdims=True) + NORM_EPS)
    normed_h = hidden * scale_h
    normed_low = normed_h.astype(jnp.bfloat16)
    flat_ids = routes[0].reshape(2 * tok_rows)
    member = flat_ids[:, None] == jnp.arange(experts, dtype=jnp.int32)[None, :]
    earlier = jnp.arange(2 * tok_rows)[:, None] > jnp.arange(2 * tok_rows)[None, :]
    earlier_count = jnp.dot(
        earlier.astype(jnp.bfloat16),
        member.astype(jnp.bfloat16),
        preferred_element_type=jnp.float32,
    )
    slot_place = member[:, :, None] & (
        earlier_count[:, :, None] == jnp.arange(SLOT_LIMIT, dtype=jnp.float32)[None, None, :]
    )
    slot_place = slot_place.astype(jnp.float32).reshape(tok_rows, 2, slot_count)
    slot_table = jnp.sum(slot_place, axis=1)
    weighted = jnp.sum(slot_place * gate_probs[0][:, :, None], axis=1)
    slot_in = lax.dot_general(
        slot_table.astype(jnp.bfloat16),
        normed_low,
        (((0,), (0,)), ((), ())),
        preferred_element_type=jnp.float32,
    )
    slot_in = slot_in.astype(jnp.bfloat16).reshape(experts, SLOT_LIMIT, feat_width)
    gathered_in = send_slots(slot_in)
    up_slice, down_slice = fetch_slices(w_up, w_down)
    up_one = up_slice[0]
    down_one = down_slice[0]
    pre_act = jnp.dot(gathered_in, up_one, preferred_element_type=jnp.float32)
    gelu_val, gelu_slope = gelu_parts(pre_act)
    partial_value = jnp.dot(
        gelu_val.astype(jnp.bfloat16), down_one, preferred_element_type=jnp.float32
    ).astype(jnp.bfloat16)
    slot_out = return_slots(partial_value, SLOT_LIMIT).reshape(slot_count, feat_width)
    moe_mixed = jnp.dot(weighted, slot_out, precision=lax.Precision.HIGHEST)
    block_out = (hidden + moe_mixed).astype(jnp.bfloat16)
    grad_out = cotangent[0].astype(jnp.float32)
    slot_grad = lax.dot_general(
        weighted, grad_out, (((0,), (0,)), ((), ())), precision=lax.Precision.HIGHEST
    )
    slot_grad = slot_grad.astype(jnp.bfloat16).reshape(experts, SLOT_LIMIT, feat_width)
    gathered_grad = send_slots(slot_grad)
    grad_gelu = lax.dot_general(
        gathered_grad, down_one, (((1,), (1,)), ((), ())), preferred_element_type=jnp.float32
    )
    grad_act = (grad_gelu * gelu_slope).astype(jnp.bfloat16)
    part_back = lax.dot_general(
        grad_act, up_one, (((1,), (1,)), ((), ())), preferred_element_type=jnp.float32
    ).astype(jnp.bfloat16)
    slot_back = return_slots(part_back, SLOT_LIMIT).reshape(slot_count, feat_width)
    grad_norm = jnp.dot(slot_table, slot_back, precision=lax.Precision.HIGHEST)
    grad_hidden = grad_out + scale_h * (
        grad_norm - normed_h * jnp.mean(grad_norm * normed_h, axis=-1, keepdims=True)
    )
    grad_low = grad_hidden.astype(jnp.bfloat16).reshape(tok_rows, HEADS, HD)
    grad_probs = jnp.einsum("thd,fhd->htf", grad_low, val_heads, preferred_element_type=jnp.float32)
    grad_scores = (
        att_probs
        * (grad_probs - jnp.sum(att_probs * grad_probs, axis=-1, keepdims=True))
        * (1.0 / math.sqrt(HD))
    )
    scores_low = grad_scores.astype(jnp.bfloat16)
    grad_query = jnp.einsum(
        "htf,fhd->thd", scores_low, key_heads, preferred_element_type=jnp.float32
    )
    grad_key = jnp.einsum(
        "htf,thd->fhd", scores_low, query_low, preferred_element_type=jnp.float32
    ).reshape(key_span, feat_width)
    grad_value = jnp.einsum(
        "htf,thd->fhd", probs_low, grad_low, preferred_element_type=jnp.float32
    ).reshape(key_span, feat_width)
    grad_piece = scale_q * (
        grad_query - normed * jnp.mean(grad_query * normed, axis=-1, keepdims=True)
    )
    grad_in = (grad_hidden + grad_piece.reshape(tok_rows, feat_width)).astype(jnp.bfloat16)
    local_grads = jnp.stack([grad_key, grad_value])
    grad_edges = jnp.concatenate([local_grads[:, :HALO], local_grads[:, key_span - HALO :]], axis=1)
    received = with_halo(grad_edges.astype(jnp.bfloat16), ((("tm", "expert"), 1),), HALO).astype(
        grad_edges.dtype
    )
    own_grads = local_grads[:, HALO : HALO + tok_rows]
    own_grads = own_grads.at[:, :HALO].add(received[:, :HALO])
    own_grads = own_grads.at[:, tok_rows - HALO :].add(received[:, 3 * HALO :])
    own_low = own_grads.astype(jnp.bfloat16)
    return (block_out[None], grad_in[None], own_low[0][None], own_low[1][None])


def solution(mesh):
    return jax.shard_map(
        shards,
        mesh=mesh,
        in_specs=(
            P("dp", ("tm", "expert"), None),
            P("dp", ("tm", "expert"), None),
            P("dp", ("tm", "expert"), None),
            P("dp", ("tm", "expert")),
            P("dp", ("tm", "expert")),
            P("dp", ("tm", "expert"), None),
            P("dp", ("tm", "expert"), None),
            P("expert", "tm", "dp"),
            P("expert", "dp", "tm"),
            P("dp", ("tm", "expert"), None),
        ),
        out_specs=(
            P("dp", ("tm", "expert"), None),
            P("dp", ("tm", "expert"), None),
            P("dp", ("tm", "expert"), None),
            P("dp", ("tm", "expert"), None),
        ),
        check_vma=False,
    )
```

profile of v0, /device:TPU:6, one launch (start us, length us, event | category | flops | bytes accessed | tf_op | source)
XLA Modules:
  0.0 401.9 jit_solution(17397559584007037871)
XLA Ops:
  7.2 0.8 copy.28
  8.5 0.8 copy.30
  9.3 0.3 and.27
  9.9 0.3 eq.43
  10.2 0.3 eq.44
  10.7 0.4 convert_reduce_fusion.2
  11.1 0.6 copy-done.10
  11.8 0.4 convolution_convert_fusion.2
  12.2 1.6 broadcast_in_dim.16
  13.8 9.2 %all-to-all-start.2 = ((bf16[32,10,2048]{2,1,0:T(8,128)(2,1)}), bf16[32,10,2048]{2,1,0:T(8,128)(2,1)}, u32[]{:S(2)}, u32[]{:S(2)}) async-start(bf16[32,10,2048]{2,1,0:T(8,128)(2,1)} %bitcast.13), calls=%async_computation.2 | async-start | bytes 4194304 | tf_op jit(solution)/shard_map/all_to_all | solution.py:54
  23.0 0.7 all-gather.3.cloned.1.call-update
  24.1 12.4 %collective-permute-start.1 = (bf16[2,16,2048]{2,1,0:T(8,128)(2,1)S(1)}, bf16[2,16,2048]{2,1,0:T(8,128)(2,1)S(1)}, u32[]{:S(2)}, u32[]{:S(2)}) collective-permute-start(bf16[2,16,2048]{2,1,0:T(8,128)(2,1)S(1)} %get-tuple-element.39), channel_id=1, source_target_pairs={{1,0},{2,1},{3,2},{4,3},{5,4},{6,5},{7,6},{8,7},{9,8},{10,9},{11,1... | collective-permute-start | bytes 393224 | tf_op jit(solution)/shard_map/ppermute | solution.py:29
  36.5 1.9 collective-permute-start
  39.3 42.0 %collective-permute-done = bf16[2,16,2048]{2,1,0:T(8,128)(2,1)S(1)} collective-permute-done((bf16[2,16,2048]{2,1,0:T(8,128)(2,1)S(1)}, bf16[2,16,2048]{2,1,0:T(8,128)(2,1)S(1)}, u32[]{:S(2)}, u32[]{:S(2)}) %collective-permute-start) | collective-permute-done | bytes 131104 | tf_op jit(solution)/shard_map/ppermute | solution.py:27
  81.8 1.5 fusion.13
  83.3 3.3 fusion.27
  86.5 1.6 copy.27
  88.1 1.0 convolution_convert_fusion.3
  89.1 1.0 broadcast_in_dim.12
  90.1 1.6 broadcast_in_dim.13
  91.7 16.0 %all-to-all-start = ((bf16[32,10,2048]{2,1,0:T(8,128)(2,1)}), bf16[32,10,2048]{2,1,0:T(8,128)(2,1)}, u32[]{:S(2)}, u32[]{:S(2)}) async-start(bf16[32,10,2048]{2,1,0:T(8,128)(2,1)} %bitcast.93), calls=%async_computation | async-start | bytes 4194304 | tf_op jit(solution)/shard_map/all_to_all | solution.py:54
  107.8 0.7 all-gather.5.cloned.1.call-update
  108.5 3.6 reshape.241
  112.1 65.6 %all-to-all-done = bf16[32,10,2048]{2,1,0:T(8,128)(2,1)} async-done(((bf16[32,10,2048]{2,1,0:T(8,128)(2,1)}), bf16[32,10,2048]{2,1,0:T(8,128)(2,1)}, u32[]{:S(2)}, u32[]{:S(2)}) %all-to-all-start) | async-done | bytes 1310752 | tf_op jit(solution)/shard_map/all_to_all | solution.py:54
  177.7 3.6 reshape.237
  181.3 3.7 fusion.7
  185.0 61.1 %all-gather.5.cloned.1.call-done = bf16[1,512,2048]{2,1,0:T(8,128)(2,1)} async-done(((bf16[1,512,128]{2,1,0:T(8,128)(2,1)}), bf16[1,512,2048]{2,1,0:T(8,128)(2,1)}) %all-gather.5.cloned.1.call-update) | async-done | bytes 2097168 | tf_op jit(solution)/shard_map/all_gather | solution.py:45
  246.1 5.6 %convolution_convert_fusion = bf16[320,2048]{1,0:T(8,128)(2,1)} fusion(bf16[1,2048,512]{2,1,0:T(8,128)(2,1)} %all-gather.3.cloned.1.call-done, bf16[320,2048]{1,0:T(8,128)(2,1)} %reshape.241, bf16[1,512,2048]{2,1,0:T(8,128)(2,1)} %all-gather.5.cloned.1.call-done, f32[320,512]{1,0:T(8,128)} %fusion.7), kind=kOutput, calls=%fused_computation.3 | convolution fusion | flops 1344471040 | bytes 7471104 | tf_op jit(solution)/shard_map/dot_general | solution.py:161
  251.7 3.4 reshape.242
  255.0 7.6 %all-to-all-start.3 = ((bf16[32,10,2048]{2,1,0:T(8,128)(2,1)}), bf16[32,10,2048]{2,1,0:T(8,128)(2,1)}, u32[]{:S(2)}, u32[]{:S(2)}) async-start(bf16[32,10,2048]{2,1,0:T(8,128)(2,1)} %reshape.242), calls=%async_computation.3 | async-start | bytes 4194304 | tf_op jit(solution)/shard_map/all_to_all | solution.py:61
  262.6 3.7 convolution_convert_fusion.1
  266.3 3.3 reshape.238
  269.7 41.7 %all-to-all-done.3 = bf16[32,10,2048]{2,1,0:T(8,128)(2,1)} async-done(((bf16[32,10,2048]{2,1,0:T(8,128)(2,1)}), bf16[32,10,2048]{2,1,0:T(8,128)(2,1)}, u32[]{:S(2)}, u32[]{:S(2)}) %all-to-all-start.3) | async-done | bytes 1310752 | tf_op jit(solution)/shard_map/all_to_all | solution.py:61
  311.4 6.0 %all-to-all-start.1 = ((bf16[32,10,2048]{2,1,0:T(8,128)(2,1)}), bf16[32,10,2048]{2,1,0:T(8,128)(2,1)}, u32[]{:S(2)}, u32[]{:S(2)}) async-start(bf16[32,10,2048]{2,1,0:T(8,128)(2,1)} %reshape.238), calls=%async_computation.1 | async-start | bytes 4194304 | tf_op jit(solution)/shard_map/all_to_all | solution.py:61
  317.4 3.0 fusion.36
  320.3 2.8 convert_reduce_fusion
  323.2 1.8 reshape.243
  325.0 2.2 multiply_reduce_fusion.2
  327.2 1.4 convert_bitcast_fusion
  328.6 0.8 copy-done.7
  329.3 1.6 fusion.39
  330.9 4.3 %convolution_bitcast_fusion.1 = f32[160,16,128]{2,0,1:T(8,128)} fusion(f32[16,128,160]{1,2,0:T(8,128)} %fusion.36, f32[16,128,160]{1,2,0:T(8,128)} %fusion.39, f32[128,16,128]{0,2,1:T(8,128)S(1)} %bitcast.90, f32[128,16]{0,1:T(8,128)S(1)} %add_rsqrt_fusion), kind=kOutput, calls=%fused_computation.17 | convolution fusion | flops 86050976 | bytes 4988928 | tf_op jit(solution)/shard_map/htf,thd->fhd/dot_general | solution.py:180
  335.2 3.2 copy.36
  338.4 2.4 stack_reshape.6
  340.8 3.3 convolution_bitcast_fusion
  344.1 3.2 copy.38
  347.3 2.5 stack_reshape.7
  349.7 1.5 constant_dynamic-update-slice_fusion.3
  351.5 1.6 slice.103
  353.2 0.5 copy-done
  353.7 1.2 convert.10
  354.9 4.4 %multiply_reduce_fusion.1 = (f32[128,16]{0,1:T(8,128)S(1)}, f32[128,16,128]{0,2,1:T(8,128)}) fusion(f32[128,16,128]{0,2,1:T(8,128)S(1)} %bitcast.91, f32[128,16]{0,1:T(8,128)S(1)} %add_rsqrt_fusion, f32[16,128,160]{1,2,0:T(8,128)} %fusion.36, f32[16,128,160]{1,2,0:T(8,128)} %fusion.39, bf16[160,16,128]{2,1,0:T(8,128)(2,1)S(1)} %bitcast.96), kind=kOutput, calls=%fused_computation.37 | convolution fusion | flops 86311072 | bytes 5390336 | tf_op jit(solution)/shard_map/htf,fhd->thd/dot_general | solution.py:177
  359.4 6.6 %all-to-all-done.1 = bf16[32,10,2048]{2,1,0:T(8,128)(2,1)} async-done(((bf16[32,10,2048]{2,1,0:T(8,128)(2,1)}), bf16[32,10,2048]{2,1,0:T(8,128)(2,1)}, u32[]{:S(2)}, u32[]{:S(2)}) %all-to-all-start.1) | async-done | bytes 1310752 | tf_op jit(solution)/shard_map/all_to_all | solution.py:61
  366.0 2.0 convert_reduce_fusion.1
  368.1 2.4 subtract_multiply_fusion
  370.5 2.7 copy.34
  373.1 1.0 fusion.68
  374.1 3.3 collective-permute-start.3
  377.4 1.9 collective-permute-start.2
  379.4 2.2 fusion.45
  381.5 1.8 fusion.2
  383.3 9.5 %collective-permute-done.2 = bf16[2,16,2048]{2,1,0:T(8,128)(2,1)S(1)} collective-permute-done((bf16[2,16,2048]{2,1,0:T(8,128)(2,1)S(1)}, bf16[2,16,2048]{2,1,0:T(8,128)(2,1)S(1)}, u32[]{:S(2)}, u32[]{:S(2)}) %collective-permute-start.2) | collective-permute-done | bytes 131104 | tf_op jit(solution)/shard_map/ppermute | solution.py:27
  392.8 1.0 fusion.57
  394.0 1.0 fusion.69
  (65 shorter events, 3.1 us)
Async XLA Ops:
  7.2 4.6 %copy-start.8 = (bf16[1,128,2048]{2,1,0:T(8,128)(2,1)S(1)}, bf16[1,128,2048]{2,1,0:T(8,128)(2,1)}, u32[]{:S(2)}) copy-start(bf16[1,128,2048]{2,1,0:T(8,128)(2,1)} %param.23) | copy-start | bytes 1572868
  11.1 0.6 copy-start.10
  11.1 77.0 %copy-start.12 = (f32[128,40]{1,0:T(8,128)}, f32[128,40]{1,0:T(8,128)S(1)}, u32[]{:S(2)}) copy-start(f32[128,40]{1,0:T(8,128)S(1)} %get-tuple-element.28) | copy-start | bytes 61444
  13.8 9.9 %copy-start.14 = (bf16[1,128,2048]{2,1,0:T(8,128)(2,1)S(1)}, bf16[1,128,2048]{2,1,0:T(8,128)(2,1)}, u32[]{:S(2)}) copy-start(bf16[1,128,2048]{2,1,0:T(8,128)(2,1)} %param.15) | copy-start | bytes 1572868
  13.8 76.3 %all-to-all-start.2 = ((bf16[32,10,2048]{2,1,0:T(8,128)(2,1)}), bf16[32,10,2048]{2,1,0:T(8,128)(2,1)}, u32[]{:S(2)}, u32[]{:S(2)}) async-start(bf16[32,10,2048]{2,1,0:T(8,128)(2,1)} %bitcast.13), calls=%async_computation.2 | async-start | bytes 4194304 | tf_op jit(solution)/shard_map/all_to_all | solution.py:54
  23.0 1.0 copy-start.15
  23.0 158.3 %all-gather.3.cloned.1.call-start = ((), (), s32[]{:S(2)}) async-start(), calls=%async_computation.4 | async-start | bytes 2228224 | tf_op jit(solution)/shard_map/all_gather | solution.py:44
  23.7 14.7 %copy-start.1 = (bf16[1,128,2048]{2,1,0:T(8,128)(2,1)S(1)}, bf16[1,128,2048]{2,1,0:T(8,128)(2,1)}, u32[]{:S(2)}) copy-start(bf16[1,128,2048]{2,1,0:T(8,128)(2,1)} %param.14) | copy-start | bytes 1572868
  24.1 15.2 %collective-permute-start.1 = (bf16[2,16,2048]{2,1,0:T(8,128)(2,1)S(1)}, bf16[2,16,2048]{2,1,0:T(8,128)(2,1)S(1)}, u32[]{:S(2)}, u32[]{:S(2)}) collective-permute-start(bf16[2,16,2048]{2,1,0:T(8,128)(2,1)S(1)} %get-tuple-element.39), channel_id=1, source_target_pairs={{1,0},{2,1},{3,2},{4,3},{5,4},{6,5},{7,6},{8,7},{9,8},{10,9},{11,1... | collective-permute-start | bytes 393224 | tf_op jit(solution)/shard_map/ppermute | solution.py:29
  36.5 44.7 %collective-permute-start = (bf16[2,16,2048]{2,1,0:T(8,128)(2,1)S(1)}, bf16[2,16,2048]{2,1,0:T(8,128)(2,1)S(1)}, u32[]{:S(2)}, u32[]{:S(2)}) collective-permute-start(bf16[2,16,2048]{2,1,0:T(8,128)(2,1)S(1)} %get-tuple-element.38), channel_id=1, source_target_pairs={{0,1},{1,2},{2,3},{3,4},{4,5},{5,6},{6,7},{7,8},{8,9},{9,10},{10,1... | collective-permute-start | bytes 393224 | tf_op jit(solution)/shard_map/ppermute | solution.py:27
  38.5 0.7 copy-start.16
  38.5 0.7 copy-start.17
  81.8 1.5 copy-start.5
  91.7 86.0 %all-to-all-start = ((bf16[32,10,2048]{2,1,0:T(8,128)(2,1)}), bf16[32,10,2048]{2,1,0:T(8,128)(2,1)}, u32[]{:S(2)}, u32[]{:S(2)}) async-start(bf16[32,10,2048]{2,1,0:T(8,128)(2,1)} %bitcast.93), calls=%async_computation | async-start | bytes 4194304 | tf_op jit(solution)/shard_map/all_to_all | solution.py:54
  107.7 138.4 %all-gather.5.cloned.1.call-start = ((), (), s32[]{:S(2)}) async-start(), calls=%async_computation.5 | async-start | bytes 2228224 | tf_op jit(solution)/shard_map/all_gather | solution.py:45
  255.0 56.3 %all-to-all-start.3 = ((bf16[32,10,2048]{2,1,0:T(8,128)(2,1)}), bf16[32,10,2048]{2,1,0:T(8,128)(2,1)}, u32[]{:S(2)}, u32[]{:S(2)}) async-start(bf16[32,10,2048]{2,1,0:T(8,128)(2,1)} %reshape.242), calls=%async_computation.3 | async-start | bytes 4194304 | tf_op jit(solution)/shard_map/all_to_all | solution.py:61
  311.4 54.6 %all-to-all-start.1 = ((bf16[32,10,2048]{2,1,0:T(8,128)(2,1)}), bf16[32,10,2048]{2,1,0:T(8,128)(2,1)}, u32[]{:S(2)}, u32[]{:S(2)}) async-start(bf16[32,10,2048]{2,1,0:T(8,128)(2,1)} %reshape.238), calls=%async_computation.1 | async-start | bytes 4194304 | tf_op jit(solution)/shard_map/all_to_all | solution.py:61
  320.3 4.6 %copy-start.13 = (f32[128,40]{1,0:T(8,128)S(1)}, f32[128,40]{1,0:T(8,128)}, u32[]{:S(2)}) copy-start(f32[128,40]{1,0:T(8,128)} %copy-done.12) | copy-start | bytes 61444
  325.0 2.2 copy-start.9
  327.2 2.2 copy-start.6
  328.6 0.8 copy-start.7
  349.7 1.7 copy-start.3
  351.5 2.2 copy-start
  370.5 8.9 %copy-start.4 = (f32[128,2048]{1,0:T(8,128)S(1)}, f32[128,2048]{1,0:T(8,128)}, u32[]{:S(2)}) copy-start(f32[128,2048]{1,0:T(8,128)} %get-tuple-element.31) | copy-start | bytes 3145732
  374.1 9.2 %collective-permute-start.3 = (bf16[2,16,2048]{2,1,0:T(8,128)(2,1)S(1)}, bf16[2,16,2048]{2,1,0:T(8,128)(2,1)S(1)}, u32[]{:S(2)}, u32[]{:S(2)}) collective-permute-start(bf16[2,16,2048]{2,1,0:T(8,128)(2,1)S(1)} %get-tuple-element.33), channel_id=1, source_target_pairs={{1,0},{2,1},{3,2},{4,3},{5,4},{6,5},{7,6},{8,7},{9,8},{10,9},{11,1... | collective-permute-start | bytes 393224 | tf_op jit(solution)/shard_map/ppermute | solution.py:29
  377.4 15.4 %collective-permute-start.2 = (bf16[2,16,2048]{2,1,0:T(8,128)(2,1)S(1)}, bf16[2,16,2048]{2,1,0:T(8,128)(2,1)S(1)}, u32[]{:S(2)}, u32[]{:S(2)}) collective-permute-start(bf16[2,16,2048]{2,1,0:T(8,128)(2,1)S(1)} %get-tuple-element.32), channel_id=1, source_target_pairs={{0,1},{1,2},{2,3},{3,4},{4,5},{5,6},{6,7},{7,8},{8,9},{9,10},{10,1... | collective-permute-start | bytes 393224 | tf_op jit(solution)/shard_map/ppermute | solution.py:27
  379.4 2.2 copy-start.11
  381.5 11.3 %copy-start.2 = (f32[2,128,2048]{2,1,0:T(8,128)S(1)}, f32[2,128,2048]{2,1,0:T(8,128)}, u32[]{:S(2)}) copy-start(f32[2,128,2048]{2,1,0:T(8,128)} %slice.103) | copy-start | bytes 6291460
Sparse Core Ops, SparseCore 0:
  26.9 105.8 all-gather.2
  135.7 110.3 all-gather.4
where the time goes:
time: 403 us; the launch traced here: 402 us
  waiting for transfers between devices  228 us (57%)
  starting transfers between devices  58.4 us (14%)
  local copies, waits for them, and re-layouts  47.2 us (12%)
  matrix products  36.9 us (9%)
  other arithmetic  17 us (4%)
  between operations  14.5 us (4%)
    all_to_all x2, waiting for transfers between devices, send_slots(): lax.all_to_all(spread, ('dp', 'expert'), split_axis=0, concat_axis=0, til...  65.6 us
    all_gather x1, waiting for transfers between devices, fetch_slices(): lax.all_gather(down_local, 'tm', axis=2, tiled=True)  61.1 us
    ppermute x2, waiting for transfers between devices, with_halo(): lax.ppermute(tail, axis, [(i, (i + 1) % count) for i in range(ends)])  51.5 us
    all_to_all x2, waiting for transfers between devices, return_slots(): lax.all_to_all(results.reshape(groups, capacity, feat_width), ('dp', 'exp...  48.3 us
    all_to_all x2, starting transfers between devices, send_slots(): lax.all_to_all(spread, ('dp', 'expert'), split_axis=0, concat_axis=0, til...  25.2 us
    ppermute x2, starting transfers between devices, with_halo(): lax.ppermute(head, axis, [((i + 1) % count, i) for i in range(ends)])  15.7 us
    all_to_all x2, starting transfers between devices, return_slots(): lax.all_to_all(results.reshape(groups, capacity, feat_width), ('dp', 'exp...  13.6 us
  transfers between devices with their start and end apart: 10, of which 6 were waited for; matrix products, arithmetic and copies ran while one was open for 18% of the time, Pallas kernels for 0%

commit v1 on v0

v1 whole, which is shorter than its diff:
```python
import math

import jax
import jax.numpy as jnp
from jax import lax
from jax.experimental import pallas as pl
from jax.experimental.pallas import tpu as pltpu
from jax.sharding import Mesh, PartitionSpec as P

HEADS = 16
HD = 128
HALO = 16
SLOT_LIMIT = 10
EXPERTS = 4
SLOTS = EXPERTS * SLOT_LIMIT
LANES = 128

NORM_EPS = 1e-06
ROOT_HALF = 1.0 / math.sqrt(2.0)
INV_ROOT_TWOPI = 1.0 / math.sqrt(2.0 * math.pi)
INV_ROOT_HD = 1.0 / math.sqrt(HD)

BF = jnp.bfloat16
F32 = jnp.float32
VMEM_LIMIT = 56 * 1024 * 1024

NT = (((1,), (1,)), ((), ()))
TN = (((0,), (0,)), ((), ()))


def mm(a, b, dims=(((1,), (0,)), ((), ()))):
    return lax.dot_general(a, b, dims, preferred_element_type=F32)


def call(body, outs, args, scratch=(), flops=10**8, aliases=None):
    nbytes = sum(math.prod(a.shape) * a.dtype.itemsize for a in args)
    nbytes += sum(math.prod(o.shape) * o.dtype.itemsize for o in outs)
    return pl.pallas_call(
        body,
        out_shape=outs,
        in_specs=[pl.BlockSpec(memory_space=pltpu.VMEM)] * len(args),
        out_specs=[pl.BlockSpec(memory_space=pltpu.VMEM)] * len(outs),
        scratch_shapes=list(scratch),
        input_output_aliases=aliases or {},
        compiler_params=pltpu.CompilerParams(vmem_limit_bytes=VMEM_LIMIT),
        cost_estimate=pl.CostEstimate(flops=flops, bytes_accessed=nbytes, transcendentals=0),
    )(*args)


def shaped(shape, dtype):
    return jax.ShapeDtypeStruct(shape, dtype)


def slot_table(routes_ref):
    tokens = routes_ref.shape[1]
    first, second = routes_ref[0:1, :], routes_ref[1:2, :]
    slot = lax.broadcasted_iota(jnp.int32, (SLOTS, tokens), 0)
    expert = jnp.zeros_like(slot)
    for e in range(1, EXPERTS):
        expert = expert + (slot >= e * SLOT_LIMIT).astype(jnp.int32)
    rank = (slot - expert * SLOT_LIMIT).astype(F32)
    is_first = first == expert
    member = is_first | (second == expert)
    before = lax.broadcasted_iota(jnp.int32, (tokens, tokens), 0)
    after = lax.broadcasted_iota(jnp.int32, (tokens, tokens), 1)
    earlier = mm(
        jnp.where(member, 1.0, 0.0).astype(BF), jnp.where(before < after, 1.0, 0.0).astype(BF)
    )
    table = jnp.where(member & (earlier == rank), 1.0, 0.0)
    return table, is_first


def slot_gates(table, is_first, gates_ref):
    gate = jnp.where(is_first, gates_ref[0:1, :], gates_ref[1:2, :])
    return jnp.sum(table * gate, axis=1, keepdims=True)


def to_travel(rows, scratch, row_count, base=0):
    for c in range(rows.shape[1] // LANES):
        scratch[pl.ds(base + c, row_count, stride=16), :] = rows[:, c * LANES : (c + 1) * LANES]


def from_travel(scratch, row_count, c, base=0):
    return scratch[pl.ds(base + c, row_count, stride=16), :]


def scatter_slots(table, rows):
    high = rows.astype(BF)
    low = (rows - high.astype(F32)).astype(BF)
    table_low = table.astype(BF)
    return mm(table_low, high, TN) + mm(table_low, low, TN)


def grad_slots_kernel(routes, gates, cot, out, scratch):
    table, is_first = slot_table(routes)
    gate = slot_gates(table, is_first, gates)
    rows = mm(table.astype(BF), cot[...]) * gate
    to_travel(rows, scratch, SLOTS)
    sent = scratch[...].astype(BF)
    for d in range(out.shape[0]):
        out[d] = sent


def query_of(x):
    scale = lax.rsqrt(jnp.mean(x * x, axis=-1, keepdims=True) + NORM_EPS)
    return x * scale, scale


def attend_kernel(
    routes, bounds, dec, keys, values, halo_lo, halo_hi,
    sent, hidden, probs, k_all, v_all, scratch,
):
    tokens = dec.shape[0]
    span = tokens + 2 * HALO
    for all_ref, own, i in ((k_all, keys, 0), (v_all, values, 1)):
        all_ref[0:HALO, :] = halo_lo[i]
        all_ref[HALO : HALO + tokens, :] = own[...]
        all_ref[HALO + tokens : span, :] = halo_hi[i]
    frame = lax.broadcasted_iota(jnp.int32, (tokens, span), 1)
    inside = (frame >= bounds[:, 0:1]) & (frame < bounds[:, 1:2])
    square = jnp.zeros((tokens, 1), F32)
    for h in range(HEADS):
        cols = slice(h * HD, (h + 1) * HD)
        x = dec[:, cols].astype(F32)
        query = query_of(x)[0].astype(BF)
        scores = mm(query, k_all[:, cols], NT) * INV_ROOT_HD
        weights = jnp.where(inside, jnp.exp(scores), 0.0)
        att = weights / jnp.sum(weights, axis=-1, keepdims=True)
        probs[h] = att
        mixed = x + mm(att.astype(BF), v_all[:, cols])
        hidden[:, cols] = mixed
        square = square + jnp.sum(mixed * mixed, axis=-1, keepdims=True)
    scale_h = lax.rsqrt(square * (1.0 / (HEADS * HD)) + NORM_EPS)
    table = slot_table(routes)[0].astype(BF)
    rows = mm(table, (hidden[...] * scale_h).astype(BF))
    to_travel(rows, scratch, SLOTS)
    low = scratch[...].astype(BF)
    for d in range(sent.shape[0]):
        sent[d] = low


def rows_kernel(own, other, out, scratch):
    half = own.shape[0] // 16
    for i, ref in enumerate((own, other)):
        scratch[...] = ref[...].astype(F32)
        for c in range(out.shape[1] // LANES):
            out[i * half : (i + 1) * half, c * LANES : (c + 1) * LANES] = from_travel(
                scratch, half, c
            ).astype(BF)


def gelu_parts(pre_act):
    gauss_cdf = 0.5 * (1.0 + lax.erf(pre_act * ROOT_HALF))
    slope = gauss_cdf + pre_act * jnp.exp(-0.5 * pre_act * pre_act) * INV_ROOT_TWOPI
    return (pre_act * gauss_cdf, slope)


def send_halves(lhs, rhs_of, outs, scratches):
    half = lhs.shape[0] // 2
    for c in range(0, 16, 2):
        part = rhs_of(lhs, c)
        for i, scratch in enumerate(scratches):
            for k in range(2):
                scratch[pl.ds(c + k, half, stride=16), :] = part[
                    i * half : (i + 1) * half, k * LANES : (k + 1) * LANES
                ]
    for out, scratch in zip(outs, scratches):
        out[...] = scratch[...].astype(BF)


def expert_back_kernel(place, rows_in, rows_grad, *refs):
    pieces, (own, other, gelu, up, down, sc_own, sc_other) = refs[:-7], refs[-7:]
    assemble(place, pieces, up, down)
    pre_act = mm(rows_in[...], up[...])
    value, slope = gelu_parts(pre_act)
    gelu[...] = value.astype(BF)
    grad_act = (mm(rows_grad[...], down[...], NT) * slope).astype(BF)
    send_halves(
        grad_act,
        lambda lhs, c: mm(lhs, up[c * LANES : (c + 2) * LANES, :], NT),
        (own, other),
        (sc_own, sc_other),
    )


def expert_out_kernel(gelu, down, own, other, sc_own, sc_other):
    send_halves(
        gelu[...],
        lambda lhs, c: mm(lhs, down[:, c * LANES : (c + 2) * LANES]),
        (own, other),
        (sc_own, sc_other),
    )


def assemble(place, pieces, up, down):
    (whole,) = pieces
    block = LANES
    for tm in range(16):
        up[tm * block : (tm + 1) * block, :] = whole[tm, 0:block, :]
        for q in range(4):
            down[q * block : (q + 1) * block, tm * block : (tm + 1) * block] = whole[
                tm, block : 2 * block, q * block : (q + 1) * block
            ]


def slot_sum(back, scratch):
    total = back[0].astype(F32)
    for d in range(1, back.shape[0]):
        total = total + back[d].astype(F32)
    scratch[...] = total
    return jnp.concatenate([from_travel(scratch, SLOTS, c) for c in range(16)], axis=1)


def out_kernel(routes, gates, back, hidden, out, scratch):
    table, is_first = slot_table(routes)
    rows = slot_sum(back, scratch) * slot_gates(table, is_first, gates)
    out[...] = (hidden[...] + scatter_slots(table, rows)).astype(BF)


def attend_back_kernel(
    routes, back, cot, hidden, dec, probs, keys, values, halo_lo, halo_hi,
    grad_in, grad_k, grad_v, edge, send, k_all, v_all, scratch, grad_h,
):
    tokens = dec.shape[0]
    span = tokens + 2 * HALO
    for all_ref, own, i in ((k_all, keys, 0), (v_all, values, 1)):
        all_ref[0:HALO, :] = halo_lo[i]
        all_ref[HALO : HALO + tokens, :] = own[...]
        all_ref[HALO + tokens : span, :] = halo_hi[i]
    table, _ = slot_table(routes)
    grad_norm = scatter_slots(table, slot_sum(back, scratch))
    mixed = hidden[...]
    scale_h = lax.rsqrt(jnp.mean(mixed * mixed, axis=-1, keepdims=True) + NORM_EPS)
    normed = mixed * scale_h
    grad_h[...] = cot[...].astype(F32) + scale_h * (
        grad_norm - normed * jnp.mean(grad_norm * normed, axis=-1, keepdims=True)
    )
    for h in range(HEADS):
        cols = slice(h * HD, (h + 1) * HD)
        grad_hidden = grad_h[:, cols]
        grad_low = grad_hidden.astype(BF)
        att = probs[h]
        grad_probs = mm(grad_low, v_all[:, cols], NT)
        inner = jnp.sum(att * grad_probs, axis=-1, keepdims=True)
        scores_low = (att * (grad_probs - inner) * INV_ROOT_HD).astype(BF)
        query, scale_q = query_of(dec[:, cols].astype(F32))
        grad_query = mm(scores_low, k_all[:, cols])
        piece = scale_q * (
            grad_query - query * jnp.mean(grad_query * query, axis=-1, keepdims=True)
        )
        grad_in[:, cols] = (grad_hidden + piece).astype(BF)
        both = (
            mm(scores_low, query.astype(BF), TN),
            mm(att.astype(BF), grad_low, TN),
        )
        for i, (grad, ref) in enumerate(zip(both, (grad_k, grad_v))):
            ref[:, cols] = grad[HALO : HALO + tokens, :].astype(BF)
            edge[i, 0, :, cols] = grad[HALO : 2 * HALO, :]
            edge[i, 1, :, cols] = grad[tokens : HALO + tokens, :]
            send[0, i, :, cols] = grad[0:HALO, :].astype(BF)
            send[1, i, :, cols] = grad[HALO + tokens : span, :].astype(BF)


def shift(value, axis, step):
    count = lax.axis_size(axis)
    return lax.ppermute(value, axis, [(i, (i + step) % count) for i in range(count)])


def neighbours(tail, head):
    axes = ("x", "zh", "y", "core")
    count = lax.axis_size(axes)
    return (
        lax.ppermute(tail, axes, [(i, i + 1) for i in range(count - 1)]),
        lax.ppermute(head, axes, [(i + 1, i) for i in range(count - 1)]),
    )


def exchange(sent):
    shape = sent.shape
    got = lax.all_to_all(
        sent.reshape(-1, 160, LANES), ("dp", "y"), split_axis=0, concat_axis=0, tiled=True
    )
    return got.reshape(shape)


def gather_weights(up_local, down_local):
    turned = down_local.reshape(4, LANES, LANES).transpose(1, 0, 2).reshape(LANES, 4 * LANES)
    packed = jnp.concatenate([up_local, turned], axis=0)
    whole = lax.all_gather(packed, ("x", "zh"), axis=0, tiled=True)
    return (whole.reshape(16, 2 * LANES, 4 * LANES),)


def slot_rows(got):
    mine = got.reshape(-1, LANES)
    other = shift(mine, "core", 1)
    count = mine.shape[0]
    return call(
        rows_kernel,
        [shaped((2 * count // 16, 16 * LANES), BF)],
        (mine, other),
        scratch=[pltpu.VMEM((count, LANES), F32)],
    )[0]


def send_back(own, other):
    total = own.astype(F32) + shift(other, "core", 1).astype(F32)
    return exchange(total.astype(BF).reshape(4, EXPERTS * 160, LANES))


def shards(
    decoder_in, enc_keys, enc_values, win_start, win_end, routes, gate_probs, w_up, w_down, cotangent
):
    dec, keys, values, cot = decoder_in[0], enc_keys[0], enc_values[0], cotangent[0]
    tokens, feat = dec.shape
    span = tokens + 2 * HALO
    position = lax.axis_index(("x", "zh", "y", "core"))
    place = jnp.stack([lax.axis_index("x"), lax.axis_index("zh")]).astype(jnp.int32)
    bounds = jnp.stack([win_start[0], win_end[0]], axis=1) - (position * tokens - HALO)
    routes_t = routes[0].T
    gates_t = gate_probs[0].T

    pieces = gather_weights(w_up[0], w_down[0])
    halo_lo, halo_hi = neighbours(
        jnp.stack([keys[tokens - HALO :], values[tokens - HALO :]]),
        jnp.stack([keys[:HALO], values[:HALO]]),
    )

    travel = (4, EXPERTS * 160, LANES)
    (grad_sent,) = call(
        grad_slots_kernel,
        [shaped(travel, BF)],
        (routes_t, gates_t, cot),
        scratch=[pltpu.VMEM(travel[1:], F32)],
    )
    grad_rows = slot_rows(exchange(grad_sent))

    in_sent, hidden, probs = call(
        attend_kernel,
        [shaped(travel, BF), shaped((tokens, feat), F32), shaped((HEADS, tokens, span), F32)],
        (routes_t, bounds, dec, keys, values, halo_lo, halo_hi),
        scratch=[
            pltpu.VMEM((span, feat), BF),
            pltpu.VMEM((span, feat), BF),
            pltpu.VMEM(travel[1:], F32),
        ],
    )
    in_rows = slot_rows(exchange(in_sent))

    rows, units = in_rows.shape[0], 4 * LANES
    half = (rows // 2 * 16, LANES)
    back_own, back_other, gelu, up_full, down_full = call(
        expert_back_kernel,
        [
            shaped(half, BF),
            shaped(half, BF),
            shaped((rows, units), BF),
            shaped((feat, units), BF),
            shaped((units, feat), BF),
        ],
        (place, in_rows, grad_rows, *pieces),
        scratch=[pltpu.VMEM(half, F32), pltpu.VMEM(half, F32)],
    )
    back = send_back(back_own, back_other)
    value_own, value_other = call(
        expert_out_kernel,
        [shaped(half, BF), shaped(half, BF)],
        (gelu, down_full),
        scratch=[pltpu.VMEM(half, F32), pltpu.VMEM(half, F32)],
    )
    result = send_back(value_own, value_other)

    grad_in, grad_k, grad_v, edge, send = call(
        attend_back_kernel,
        [
            shaped((tokens, feat), BF),
            shaped((tokens, feat), BF),
            shaped((tokens, feat), BF),
            shaped((2, 2, HALO, feat), F32),
            shaped((2, 2, HALO, feat), BF),
        ],
        (routes_t, back, cot, hidden, dec, probs, keys, values, halo_lo, halo_hi),
        scratch=[
            pltpu.VMEM((span, feat), BF),
            pltpu.VMEM((span, feat), BF),
            pltpu.VMEM(travel[1:], F32),
            pltpu.VMEM((tokens, feat), F32),
        ],
    )
    from_lo, from_hi = neighbours(send[1], send[0])
    (block_out,) = call(
        out_kernel,
        [shaped((tokens, feat), BF)],
        (routes_t, gates_t, result, hidden),
        scratch=[pltpu.VMEM(travel[1:], F32)],
    )
    grads = []
    for i, grad in enumerate((grad_k, grad_v)):
        low = (edge[i, 0] + from_lo[i].astype(F32)).astype(BF)
        high = (edge[i, 1] + from_hi[i].astype(F32)).astype(BF)
        grad = lax.dynamic_update_slice(grad, low, (0, 0))
        grad = lax.dynamic_update_slice(grad, high, (tokens - HALO, 0))
        grads.append(grad)
    return (block_out[None], grad_in[None], grads[0][None], grads[1][None])


def solution(mesh):
    fine = Mesh(mesh.devices.reshape(4, 4, 4, 4, 2), ("dp", "x", "zh", "y", "core"))
    time = ("x", "zh", "y", "core")
    wide = P("dp", time, None)
    return jax.shard_map(
        shards,
        mesh=fine,
        in_specs=(
            wide,
            wide,
            wide,
            P("dp", time),
            P("dp", time),
            wide,
            wide,
            P(("y", "core"), ("x", "zh"), "dp"),
            P(("y", "core"), "dp", ("x", "zh")),
            wide,
        ),
        out_specs=(wide, wide, wide, wide),
        check_vma=False,
    )
```

time: 403 us -> 248 us (0.62)
  the two profiles are of different devices: /device:TPU:6 before, /device:TPU:59 now
where the time goes in v1:
time: 248 us; the launch traced here: 247 us
  waiting for transfers between devices  100 us (40%)
  starting transfers between devices  76.9 us (31%)
  Pallas kernels  40.6 us (16%)
  between operations  14.2 us (6%)
  other arithmetic  8.47 us (3%)
  local copies, waits for them, and re-layouts  6.32 us (3%)
    all_to_all x4, waiting for transfers between devices, exchange(): lax.all_to_all(sent.reshape(-1, 160, LANES), ('dp', 'y'), split_axis=0, c...  59.7 us
    pallas_call x8, Pallas kernels, call(): pl.pallas_call(body, out_shape=outs, in_specs=[pl.BlockSpec(memory_space=...  40.6 us
    all_to_all x4, starting transfers between devices, exchange(): lax.all_to_all(sent.reshape(-1, 160, LANES), ('dp', 'y'), split_axis=0, c...  35.1 us
    ppermute x2, starting transfers between devices, neighbours(): lax.ppermute(tail, axes, [(i, i + 1) for i in range(count - 1)])  19.5 us
    ppermute x4, starting transfers between devices, shift(): lax.ppermute(value, axis, [(i, (i + step) % count) for i in range(count)])  18.5 us
    ppermute x2, waiting for transfers between devices, neighbours(): lax.ppermute(tail, axes, [(i, i + 1) for i in range(count - 1)])  17.2 us
    all_gather x1, waiting for transfers between devices, gather_weights(): whole = lax.all_gather(packed, ('x', 'zh'), axis=0, tiled=True)  10.6 us
    ppermute x2, waiting for transfers between devices, neighbours(): lax.ppermute(head, axes, [(i + 1, i) for i in range(count - 1)])  8.81 us
  transfers between devices with their start and end apart: 13, of which 7 were waited for; matrix products, arithmetic and copies ran while one was open for 2% of the time, Pallas kernels for 14%

profile of v1, /device:TPU:59, one launch (start us, length us, event | category | flops | bytes accessed | tf_op | source)
XLA Modules:
  0.0 246.7 jit_solution(14324898943056956089)
XLA Ops:
  7.2 0.0 all-gather.2.cloned.1.call-start
  7.2 0.9 copy.24
  8.1 1.6 pad_maximum_fusion
  9.8 0.0 all-gather.2.cloned.1.call-update
  9.8 2.3 shard_map.131
  12.1 0.0 copy-start.9
  12.1 0.0 copy-start.10
  12.1 7.9 %all-to-all-start.1 = ((bf16[16,160,128]{2,1,0:T(8,128)(2,1)}), bf16[16,160,128]{2,1,0:T(8,128)(2,1)S(1)}, u32[]{:S(2)}, u32[]{:S(2)}) async-start(bf16[16,160,128]{2,1,0:T(8,128)(2,1)} %bitcast.74), calls=%async_computation.1 | async-start | bytes 1310720 | tf_op jit(solution)/shard_map/all_to_all | solution.py:280
  20.0 1.0 fusion.8
  21.0 9.9 %collective-permute-start = (bf16[2,16,2048]{2,1,0:T(8,128)(2,1)S(1)}, bf16[2,16,2048]{2,1,0:T(8,128)(2,1)S(1)}, u32[]{:S(2)}, u32[]{:S(2)}) collective-permute-start(bf16[2,16,2048]{2,1,0:T(8,128)(2,1)S(1)} %pad_maximum_fusion.1), channel_id=1, source_target_pairs={{0,1},{1,2},{2,3},{3,4},{4,5},{5,6},{6,7},{7,8},{8,9},{9,10},{10,1... | collective-permute-start | bytes 393224 | tf_op jit(solution)/shard_map/ppermute | solution.py:273
  30.9 1.9 collective-permute-start.1
  32.9 0.0 copy-done.9
  32.9 0.0 copy-done.10
  32.9 0.1 copy.19
  33.0 0.6 broadcast_subtract_fusion.bounds
  33.7 17.2 %collective-permute-done.halo_lo = bf16[2,16,2048]{2,1,0:T(8,128)(2,1)S(1)} collective-permute-done((bf16[2,16,2048]{2,1,0:T(8,128)(2,1)S(1)}, bf16[2,16,2048]{2,1,0:T(8,128)(2,1)S(1)}, u32[]{:S(2)}, u32[]{:S(2)}) %collective-permute-start) | collective-permute-done | bytes 131104 | tf_op jit(solution)/shard_map/ppermute | solution.py:273
  50.9 0.0 copy-start.6
  50.9 0.0 collective-permute-done.1.halo_hi
  50.9 0.0 copy-start.7
  50.9 0.6 copy-done.6
  51.5 0.0 copy-done.7
  51.6 7.3 %shard_map.129 = (bf16[4,640,128]{2,1,0:T(8,128)(2,1)}, f32[128,2048]{1,0:T(8,128)}, f32[16,128,160]{2,1,0:T(8,128)}) custom-call(s32[2,128]{1,0:T(2,128)} %bitcast.85, s32[128,2]{1,0:T(8,128)} %broadcast_subtract_fusion.bounds, bf16[128,2048]{1,0:T(8,128)(2,1)} %bitcast.75, bf16[128,2048]{1,0:T(8,128)(2,1)} %bitcast.64, bf16[128,2048]{1,0:T(8,128)(2,1)} %bitcast.66, ...), custom_call_target="tpu_custom_call" | custom-call | flops 100000000 | bytes 4851712 | tf_op jit(solution)/shard_map/pallas_call | solution.py:38
  58.9 0.0 all-to-all-done.1
  58.9 0.0 copy-start
  58.9 16.1 %all-to-all-start = ((bf16[16,160,128]{2,1,0:T(8,128)(2,1)}), bf16[16,160,128]{2,1,0:T(8,128)(2,1)S(1)}, u32[]{:S(2)}, u32[]{:S(2)}) async-start(bf16[16,160,128]{2,1,0:T(8,128)(2,1)} %bitcast.79), calls=%async_computation | async-start | bytes 1310720 | tf_op jit(solution)/shard_map/all_to_all | solution.py:280
  75.0 5.7 %collective-permute-start.3 = (bf16[2560,128]{1,0:T(8,128)(2,1)S(1)}, bf16[2560,128]{1,0:T(8,128)(2,1)S(1)}, u32[]{:S(2)}, u32[]{:S(2)}) collective-permute-start(bf16[2560,128]{1,0:T(8,128)(2,1)S(1)} %bitcast.68), channel_id=1, source_target_pairs={{0,1},{1,0},{2,3},{3,2},{4,5},{5,4},{6,7},{7,6},{8,9},{9,8},{10,11... | collective-permute-start | bytes 1966088 | tf_op jit(solution)/shard_map/ppermute | solution.py:266
  80.6 54.9 %all-to-all-done = bf16[16,160,128]{2,1,0:T(8,128)(2,1)S(1)} async-done(((bf16[16,160,128]{2,1,0:T(8,128)(2,1)}), bf16[16,160,128]{2,1,0:T(8,128)(2,1)S(1)}, u32[]{:S(2)}, u32[]{:S(2)}) %all-to-all-start) | async-done | bytes 655392 | tf_op jit(solution)/shard_map/all_to_all | solution.py:280
  135.5 0.0 copy-start.3
  135.5 7.1 %collective-permute-start.2 = (bf16[2560,128]{1,0:T(8,128)(2,1)S(1)}, bf16[2560,128]{1,0:T(8,128)(2,1)S(1)}, u32[]{:S(2)}, u32[]{:S(2)}) collective-permute-start(bf16[2560,128]{1,0:T(8,128)(2,1)S(1)} %bitcast.72), channel_id=1, source_target_pairs={{0,1},{1,0},{2,3},{3,2},{4,5},{5,4},{6,7},{7,6},{8,9},{9,8},{10,11... | collective-permute-start | bytes 1966088 | tf_op jit(solution)/shard_map/ppermute | solution.py:266
  142.7 0.6 pad_add_fusion.1.place
  143.3 0.0 collective-permute-done.3.other
  143.3 0.0 copy-done
  143.3 0.9 copy-done.4
  144.2 3.5 %shard_map.132.rows_grad = bf16[320,2048]{1,0:T(8,128)(2,1)} custom-call(bf16[2560,128]{1,0:T(8,128)(2,1)} %bitcast.69, bf16[2560,128]{1,0:T(8,128)(2,1)} %copy-done.4), custom_call_target="tpu_custom_call" | custom-call | flops 100000000 | bytes 2621440 | tf_op jit(solution)/shard_map/pallas_call | solution.py:38
  147.6 0.0 copy-done.3
  147.6 0.0 collective-permute-done.2.other
  147.6 0.8 copy-done.5
  148.5 3.5 %shard_map.130.rows_in = bf16[320,2048]{1,0:T(8,128)(2,1)} custom-call(bf16[2560,128]{1,0:T(8,128)(2,1)} %bitcast.73, bf16[2560,128]{1,0:T(8,128)(2,1)} %copy-done.5), custom_call_target="tpu_custom_call" | custom-call | flops 100000000 | bytes 2621440 | tf_op jit(solution)/shard_map/pallas_call | solution.py:38
  152.0 10.6 %all-gather.2.cloned.1.call-done = bf16[4096,512]{1,0:T(8,128)(2,1)} async-done(((bf16[256,512]{1,0:T(8,128)(2,1)}), bf16[4096,512]{1,0:T(8,128)(2,1)}) %all-gather.2.cloned.1.call-update) | async-done | bytes 4194320 | tf_op jit(solution)/shard_map/all_gather | solution.py:289
  162.6 7.0 %shard_map.133 = (bf16[2560,128]{1,0:T(8,128)(2,1)}, bf16[2560,128]{1,0:T(8,128)(2,1)}, bf16[320,512]{1,0:T(8,128)(2,1)}, bf16[2048,512]{1,0:T(8,128)(2,1)}, bf16[512,2048]{1,0:T(8,128)(2,1)}) custom-call(s32[2]{0:T(128)} %pad_add_fusion.1.place, bf16[320,2048]{1,0:T(8,128)(2,1)} %shard_map.130.rows_in, bf16[320,2048]{1,0:T(8,128)(2,1)} %shard_map.132.rows_grad, ...), custom_call_target="tpu_custom_call" | custom-call | flops 100000000 | bytes 12648456 | tf_op jit(solution)/shard_map/pallas_call | solution.py:38
  169.6 2.8 %collective-permute-start.5 = (bf16[2560,128]{1,0:T(8,128)(2,1)}, bf16[2560,128]{1,0:T(8,128)(2,1)S(1)}, u32[]{:S(2)}, u32[]{:S(2)}) collective-permute-start(bf16[2560,128]{1,0:T(8,128)(2,1)} %get-tuple-element.25), channel_id=1, source_target_pairs={{0,1},{1,0},{2,3},{3,2},{4,5},{5,4},{6,7},{7,6},{8,9},{9,8},{10,11... | collective-permute-start | bytes 1966088 | tf_op jit(solution)/shard_map/ppermute | solution.py:266
  172.4 1.9 collective-permute-done.5
  174.3 2.1 add_convert_fusion
  176.5 5.2 %all-to-all-start.3 = ((bf16[16,160,128]{2,1,0:T(8,128)(2,1)}), bf16[16,160,128]{2,1,0:T(8,128)(2,1)S(1)}, u32[]{:S(2)}, u32[]{:S(2)}) async-start(bf16[16,160,128]{2,1,0:T(8,128)(2,1)} %bitcast.25), calls=%async_computation.3 | async-start | bytes 1310720 | tf_op jit(solution)/shard_map/all_to_all | solution.py:280
  181.6 4.0 %shard_map.134 = (bf16[2560,128]{1,0:T(8,128)(2,1)}, bf16[2560,128]{1,0:T(8,128)(2,1)}) custom-call(bf16[320,512]{1,0:T(8,128)(2,1)} %get-tuple-element.19.gelu, bf16[512,2048]{1,0:T(8,128)(2,1)} %get-tuple-element.20.down), custom_call_target="tpu_custom_call" | custom-call | flops 100000000 | bytes 3735552 | tf_op jit(solution)/shard_map/pallas_call | solution.py:38
  185.6 2.8 %collective-permute-start.4 = (bf16[2560,128]{1,0:T(8,128)(2,1)}, bf16[2560,128]{1,0:T(8,128)(2,1)S(1)}, u32[]{:S(2)}, u32[]{:S(2)}) collective-permute-start(bf16[2560,128]{1,0:T(8,128)(2,1)} %get-tuple-element.22), channel_id=1, source_target_pairs={{0,1},{1,0},{2,3},{3,2},{4,5},{5,4},{6,7},{7,6},{8,9},{9,8},{10,11... | collective-permute-start | bytes 1966088 | tf_op jit(solution)/shard_map/ppermute | solution.py:266
  188.4 1.9 collective-permute-done.4
  190.4 2.1 add_convert_fusion.1
  192.5 4.8 %all-to-all-done.3 = bf16[16,160,128]{2,1,0:T(8,128)(2,1)S(1)} async-done(((bf16[16,160,128]{2,1,0:T(8,128)(2,1)}), bf16[16,160,128]{2,1,0:T(8,128)(2,1)S(1)}, u32[]{:S(2)}, u32[]{:S(2)}) %all-to-all-start.3) | async-done | bytes 655392 | tf_op jit(solution)/shard_map/all_to_all | solution.py:280
  197.3 6.0 %all-to-all-start.2 = ((bf16[16,160,128]{2,1,0:T(8,128)(2,1)}), bf16[16,160,128]{2,1,0:T(8,128)(2,1)S(1)}, u32[]{:S(2)}, u32[]{:S(2)}) async-start(bf16[16,160,128]{2,1,0:T(8,128)(2,1)} %bitcast.22), calls=%async_computation.2 | async-start | bytes 1310720 | tf_op jit(solution)/shard_map/all_to_all | solution.py:280
  203.2 0.0 copy-done.1
  203.2 10.1 %shard_map.136 = (bf16[128,2048]{1,0:T(8,128)(2,1)}, bf16[128,2048]{1,0:T(8,128)(2,1)}, bf16[128,2048]{1,0:T(8,128)(2,1)}, f32[2,2,16,2048]{3,2,1,0:T(8,128)}, bf16[2,2,16,2048]{3,2,1,0:T(8,128)(2,1)}) custom-call(s32[2,128]{1,0:T(2,128)} %bitcast.86, bf16[4,640,128]{2,1,0:T(8,128)(2,1)} %bitcast.70, bf16[128,2048]{1,0:T(8,128)(2,1)} %bitcast.78, ...), custom_call_target="tpu_custom_call" | custom-call | flops 100000000 | bytes 7734272 | tf_op jit(solution)/shard_map/pallas_call | solution.py:38
  213.3 1.0 slice_bitcast_fusion
  214.4 9.6 %collective-permute-start.6 = (bf16[2,16,2048]{2,1,0:T(8,128)(2,1)S(1)}, bf16[2,16,2048]{2,1,0:T(8,128)(2,1)S(1)}, u32[]{:S(2)}, u32[]{:S(2)}) collective-permute-start(bf16[2,16,2048]{2,1,0:T(8,128)(2,1)S(1)} %get-tuple-element.41), channel_id=1, source_target_pairs={{0,1},{1,2},{2,3},{3,4},{4,5},{5,6},{6,7},{7,8},{8,9},{9,10},{10,1... | collective-permute-start | bytes 393224 | tf_op jit(solution)/shard_map/ppermute | solution.py:273
  224.0 1.9 collective-permute-start.7
  225.9 0.0 all-to-all-done.2
  225.9 0.0 copy-start.2
  225.9 0.8 copy-done.2
  226.8 2.9 %shard_map.135 = bf16[128,2048]{1,0:T(8,128)(2,1)} custom-call(s32[2,128]{1,0:T(2,128)} %bitcast.87, f32[2,128]{1,0:T(2,128)} %bitcast.89, bf16[4,640,128]{2,1,0:T(8,128)(2,1)} %bitcast.71, f32[128,2048]{1,0:T(8,128)} %get-tuple-element.23.hidden), custom_call_target="tpu_custom_call" | custom-call | flops 100000000 | bytes 2230272 | tf_op jit(solution)/shard_map/pallas_call | solution.py:38
  229.7 0.0 collective-permute-done.6
  229.7 0.0 copy-done.8
  229.7 0.7 fusion.6
  230.4 8.8 %collective-permute-done.7 = bf16[2,16,2048]{2,1,0:T(8,128)(2,1)S(1)} collective-permute-done((bf16[2,16,2048]{2,1,0:T(8,128)(2,1)S(1)}, bf16[2,16,2048]{2,1,0:T(8,128)(2,1)S(1)}, u32[]{:S(2)}, u32[]{:S(2)}) %collective-permute-start.7) | collective-permute-done | bytes 131104 | tf_op jit(solution)/shard_map/ppermute | solution.py:274
  239.2 0.7 fusion.7
  (7 shorter events, 0.0 us)
Async XLA Ops:
  7.2 155.4 %all-gather.2.cloned.1.call-start = ((), (), s32[]{:S(2)}) async-start(), calls=%async_computation.4 | async-start | bytes 4456448 | tf_op jit(solution)/shard_map/all_gather | solution.py:289
  12.1 20.8 %copy-start.9 = (s32[1,128]{1,0:T(1,128)S(1)}, s32[1,128]{1,0:T(1,128)}, u32[]{:S(2)}) copy-start(s32[1,128]{1,0:T(1,128)} %param.14) | copy-start | bytes 1540
  12.1 20.8 %copy-start.10 = (s32[1,128]{1,0:T(1,128)S(1)}, s32[1,128]{1,0:T(1,128)}, u32[]{:S(2)}) copy-start(s32[1,128]{1,0:T(1,128)} %param.13) | copy-start | bytes 1540
  12.1 46.8 %all-to-all-start.1 = ((bf16[16,160,128]{2,1,0:T(8,128)(2,1)}), bf16[16,160,128]{2,1,0:T(8,128)(2,1)S(1)}, u32[]{:S(2)}, u32[]{:S(2)}) async-start(bf16[16,160,128]{2,1,0:T(8,128)(2,1)} %bitcast.74), calls=%async_computation.1 | async-start | bytes 1310720 | tf_op jit(solution)/shard_map/all_to_all | solution.py:280
  21.0 29.9 %collective-permute-start = (bf16[2,16,2048]{2,1,0:T(8,128)(2,1)S(1)}, bf16[2,16,2048]{2,1,0:T(8,128)(2,1)S(1)}, u32[]{:S(2)}, u32[]{:S(2)}) collective-permute-start(bf16[2,16,2048]{2,1,0:T(8,128)(2,1)S(1)} %pad_maximum_fusion.1), channel_id=1, source_target_pairs={{0,1},{1,2},{2,3},{3,4},{4,5},{5,6},{6,7},{7,8},{8,9},{9,10},{10,1... | collective-permute-start | bytes 393224 | tf_op jit(solution)/shard_map/ppermute | solution.py:273
  30.9 20.0 %collective-permute-start.1 = (bf16[2,16,2048]{2,1,0:T(8,128)(2,1)S(1)}, bf16[2,16,2048]{2,1,0:T(8,128)(2,1)S(1)}, u32[]{:S(2)}, u32[]{:S(2)}) collective-permute-start(bf16[2,16,2048]{2,1,0:T(8,128)(2,1)S(1)} %pad_maximum_fusion.2), channel_id=1, source_target_pairs={{1,0},{2,1},{3,2},{4,3},{5,4},{6,5},{7,6},{8,7},{9,8},{10,9},{11,1... | collective-permute-start | bytes 393224 | tf_op jit(solution)/shard_map/ppermute | solution.py:274
  50.9 0.6 copy-start.6
  50.9 0.7 copy-start.7
  58.9 84.4 %copy-start = (bf16[16,160,128]{2,1,0:T(8,128)(2,1)}, bf16[16,160,128]{2,1,0:T(8,128)(2,1)S(1)}, u32[]{:S(2)}) copy-start(bf16[16,160,128]{2,1,0:T(8,128)(2,1)S(1)} %all-to-all-done.1) | copy-start | bytes 1966084
  58.9 76.6 %all-to-all-start = ((bf16[16,160,128]{2,1,0:T(8,128)(2,1)}), bf16[16,160,128]{2,1,0:T(8,128)(2,1)S(1)}, u32[]{:S(2)}, u32[]{:S(2)}) async-start(bf16[16,160,128]{2,1,0:T(8,128)(2,1)} %bitcast.79), calls=%async_computation | async-start | bytes 1310720 | tf_op jit(solution)/shard_map/all_to_all | solution.py:280
  75.0 68.3 %collective-permute-start.3 = (bf16[2560,128]{1,0:T(8,128)(2,1)S(1)}, bf16[2560,128]{1,0:T(8,128)(2,1)S(1)}, u32[]{:S(2)}, u32[]{:S(2)}) collective-permute-start(bf16[2560,128]{1,0:T(8,128)(2,1)S(1)} %bitcast.68), channel_id=1, source_target_pairs={{0,1},{1,0},{2,3},{3,2},{4,5},{5,4},{6,7},{7,6},{8,9},{9,8},{10,11... | collective-permute-start | bytes 1966088 | tf_op jit(solution)/shard_map/ppermute | solution.py:266
  135.5 12.1 %copy-start.3 = (bf16[16,160,128]{2,1,0:T(8,128)(2,1)}, bf16[16,160,128]{2,1,0:T(8,128)(2,1)S(1)}, u32[]{:S(2)}) copy-start(bf16[16,160,128]{2,1,0:T(8,128)(2,1)S(1)} %all-to-all-done) | copy-start | bytes 1966084
  135.5 12.1 %collective-permute-start.2 = (bf16[2560,128]{1,0:T(8,128)(2,1)S(1)}, bf16[2560,128]{1,0:T(8,128)(2,1)S(1)}, u32[]{:S(2)}, u32[]{:S(2)}) collective-permute-start(bf16[2560,128]{1,0:T(8,128)(2,1)S(1)} %bitcast.72), channel_id=1, source_target_pairs={{0,1},{1,0},{2,3},{3,2},{4,5},{5,4},{6,7},{7,6},{8,9},{9,8},{10,11... | collective-permute-start | bytes 1966088 | tf_op jit(solution)/shard_map/ppermute | solution.py:266
  143.3 0.9 copy-start.4
  147.6 0.9 copy-start.5
  169.6 4.7 %collective-permute-start.5 = (bf16[2560,128]{1,0:T(8,128)(2,1)}, bf16[2560,128]{1,0:T(8,128)(2,1)S(1)}, u32[]{:S(2)}, u32[]{:S(2)}) collective-permute-start(bf16[2560,128]{1,0:T(8,128)(2,1)} %get-tuple-element.25), channel_id=1, source_target_pairs={{0,1},{1,0},{2,3},{3,2},{4,5},{5,4},{6,7},{7,6},{8,9},{9,8},{10,11... | collective-permute-start | bytes 1966088 | tf_op jit(solution)/shard_map/ppermute | solution.py:266
  176.5 20.8 %all-to-all-start.3 = ((bf16[16,160,128]{2,1,0:T(8,128)(2,1)}), bf16[16,160,128]{2,1,0:T(8,128)(2,1)S(1)}, u32[]{:S(2)}, u32[]{:S(2)}) async-start(bf16[16,160,128]{2,1,0:T(8,128)(2,1)} %bitcast.25), calls=%async_computation.3 | async-start | bytes 1310720 | tf_op jit(solution)/shard_map/all_to_all | solution.py:280
  185.6 4.8 %collective-permute-start.4 = (bf16[2560,128]{1,0:T(8,128)(2,1)}, bf16[2560,128]{1,0:T(8,128)(2,1)S(1)}, u32[]{:S(2)}, u32[]{:S(2)}) collective-permute-start(bf16[2560,128]{1,0:T(8,128)(2,1)} %get-tuple-element.22), channel_id=1, source_target_pairs={{0,1},{1,0},{2,3},{3,2},{4,5},{5,4},{6,7},{7,6},{8,9},{9,8},{10,11... | collective-permute-start | bytes 1966088 | tf_op jit(solution)/shard_map/ppermute | solution.py:266
  197.3 6.0 %copy-start.1 = (bf16[16,160,128]{2,1,0:T(8,128)(2,1)}, bf16[16,160,128]{2,1,0:T(8,128)(2,1)S(1)}, u32[]{:S(2)}) copy-start(bf16[16,160,128]{2,1,0:T(8,128)(2,1)S(1)} %all-to-all-done.3) | copy-start | bytes 1966084
  197.3 28.6 %all-to-all-start.2 = ((bf16[16,160,128]{2,1,0:T(8,128)(2,1)}), bf16[16,160,128]{2,1,0:T(8,128)(2,1)S(1)}, u32[]{:S(2)}, u32[]{:S(2)}) async-start(bf16[16,160,128]{2,1,0:T(8,128)(2,1)} %bitcast.22), calls=%async_computation.2 | async-start | bytes 1310720 | tf_op jit(solution)/shard_map/all_to_all | solution.py:280
  213.3 16.4 %copy-start.8 = (f32[2,2,16,2048]{3,2,1,0:T(8,128)S(1)}, f32[2,2,16,2048]{3,2,1,0:T(8,128)}, u32[]{:S(2)}) copy-start(f32[2,2,16,2048]{3,2,1,0:T(8,128)} %get-tuple-element.29) | copy-start | bytes 1572868
  214.4 15.3 %collective-permute-start.6 = (bf16[2,16,2048]{2,1,0:T(8,128)(2,1)S(1)}, bf16[2,16,2048]{2,1,0:T(8,128)(2,1)S(1)}, u32[]{:S(2)}, u32[]{:S(2)}) collective-permute-start(bf16[2,16,2048]{2,1,0:T(8,128)(2,1)S(1)} %get-tuple-element.41), channel_id=1, source_target_pairs={{0,1},{1,2},{2,3},{3,4},{4,5},{5,6},{6,7},{7,8},{8,9},{9,10},{10,1... | collective-permute-start | bytes 393224 | tf_op jit(solution)/shard_map/ppermute | solution.py:273
  224.0 15.2 %collective-permute-start.7 = (bf16[2,16,2048]{2,1,0:T(8,128)(2,1)S(1)}, bf16[2,16,2048]{2,1,0:T(8,128)(2,1)S(1)}, u32[]{:S(2)}, u32[]{:S(2)}) collective-permute-start(bf16[2,16,2048]{2,1,0:T(8,128)(2,1)S(1)} %get-tuple-element.40), channel_id=1, source_target_pairs={{1,0},{2,1},{3,2},{4,3},{5,4},{6,5},{7,6},{8,7},{9,8},{10,9},{11,1... | collective-permute-start | bytes 393224 | tf_op jit(solution)/shard_map/ppermute | solution.py:274
  225.9 0.8 copy-start.2
Sparse Core Ops, SparseCore 0:
  11.6 150.9 all-gather.1

commit v2 on v1

--- a/solution.py
+++ b/solution.py
@@ -14,6 +14,7 @@
 EXPERTS = 4
 SLOTS = EXPERTS * SLOT_LIMIT
 LANES = 128
+TRAVEL_ROWS = SLOT_LIMIT * 16
 
 NORM_EPS = 1e-06
 ROOT_HALF = 1.0 / math.sqrt(2.0)
@@ -32,16 +33,16 @@
     return lax.dot_general(a, b, dims, preferred_element_type=F32)
 
 
-def call(body, outs, args, scratch=(), flops=10**8, aliases=None):
+def call(body, outs, args, scratch=(), flops=10**8, scalars=0):
     nbytes = sum(math.prod(a.shape) * a.dtype.itemsize for a in args)
     nbytes += sum(math.prod(o.shape) * o.dtype.itemsize for o in outs)
     return pl.pallas_call(
         body,
         out_shape=outs,
-        in_specs=[pl.BlockSpec(memory_space=pltpu.VMEM)] * len(args),
+        in_specs=[pl.BlockSpec(memory_space=pltpu.SMEM)] * scalars
+        + [pl.BlockSpec(memory_space=pltpu.VMEM)] * (len(args) - scalars),
         out_specs=[pl.BlockSpec(memory_space=pltpu.VMEM)] * len(outs),
         scratch_shapes=list(scratch),
-        input_output_aliases=aliases or {},
         compiler_params=pltpu.CompilerParams(vmem_limit_bytes=VMEM_LIMIT),
         cost_estimate=pl.CostEstimate(flops=flops, bytes_accessed=nbytes, transcendentals=0),
     )(*args)
@@ -51,14 +52,14 @@
     return jax.ShapeDtypeStruct(shape, dtype)
 
 
-def slot_table(routes_ref):
+def slot_table(routes_ref, stride=SLOT_LIMIT):
     tokens = routes_ref.shape[1]
     first, second = routes_ref[0:1, :], routes_ref[1:2, :]
-    slot = lax.broadcasted_iota(jnp.int32, (SLOTS, tokens), 0)
+    slot = lax.broadcasted_iota(jnp.int32, (EXPERTS * stride, tokens), 0)
     expert = jnp.zeros_like(slot)
     for e in range(1, EXPERTS):
-        expert = expert + (slot >= e * SLOT_LIMIT).astype(jnp.int32)
-    rank = (slot - expert * SLOT_LIMIT).astype(F32)
+        expert = expert + (slot >= e * stride).astype(jnp.int32)
+    rank = (slot - expert * stride).astype(F32)
     is_first = first == expert
     member = is_first | (second == expert)
     before = lax.broadcasted_iota(jnp.int32, (tokens, tokens), 0)
@@ -75,11 +76,6 @@
     return jnp.sum(table * gate, axis=1, keepdims=True)
 
 
-def to_travel(rows, scratch, row_count, base=0):
-    for c in range(rows.shape[1] // LANES):
-        scratch[pl.ds(base + c, row_count, stride=16), :] = rows[:, c * LANES : (c + 1) * LANES]
-
-
 def from_travel(scratch, row_count, c, base=0):
     return scratch[pl.ds(base + c, row_count, stride=16), :]
 
@@ -91,14 +87,13 @@
     return mm(table_low, high, TN) + mm(table_low, low, TN)
 
 
-def grad_slots_kernel(routes, gates, cot, out, scratch):
-    table, is_first = slot_table(routes)
-    gate = slot_gates(table, is_first, gates)
-    rows = mm(table.astype(BF), cot[...]) * gate
-    to_travel(rows, scratch, SLOTS)
-    sent = scratch[...].astype(BF)
-    for d in range(out.shape[0]):
-        out[d] = sent
+def slots_to_travel(rows, scratch, kind):
+    for e in range(EXPERTS):
+        base = (2 * e + kind) * TRAVEL_ROWS
+        for c in range(16):
+            scratch[pl.ds(base + c, SLOT_LIMIT, stride=16), :] = rows[
+                e * 16 : e * 16 + SLOT_LIMIT, c * LANES : (c + 1) * LANES
+            ]
 
 
 def query_of(x):
@@ -107,7 +102,7 @@
 
 
 def attend_kernel(
-    routes, bounds, dec, keys, values, halo_lo, halo_hi,
+    routes, gates, bounds, dec, cot, keys, values, halo_lo, halo_hi,
     sent, hidden, probs, k_all, v_all, scratch,
 ):
     tokens = dec.shape[0]
@@ -116,35 +111,41 @@
         all_ref[0:HALO, :] = halo_lo[i]
         all_ref[HALO : HALO + tokens, :] = own[...]
         all_ref[HALO + tokens : span, :] = halo_hi[i]
-    frame = lax.broadcasted_iota(jnp.int32, (tokens, span), 1)
-    inside = (frame >= bounds[:, 0:1]) & (frame < bounds[:, 1:2])
+    frame = lax.broadcasted_iota(jnp.int32, (span, tokens), 0)
+    inside = (frame >= bounds[0:1, :]) & (frame < bounds[1:2, :])
     square = jnp.zeros((tokens, 1), F32)
     for h in range(HEADS):
         cols = slice(h * HD, (h + 1) * HD)
         x = dec[:, cols].astype(F32)
         query = query_of(x)[0].astype(BF)
-        scores = mm(query, k_all[:, cols], NT) * INV_ROOT_HD
+        scores = mm(k_all[:, cols], query, NT) * INV_ROOT_HD
         weights = jnp.where(inside, jnp.exp(scores), 0.0)
-        att = weights / jnp.sum(weights, axis=-1, keepdims=True)
+        att = weights * (1.0 / jnp.sum(weights, axis=0, keepdims=True))
         probs[h] = att
-        mixed = x + mm(att.astype(BF), v_all[:, cols])
+        mixed = x + mm(att.astype(BF), v_all[:, cols], TN)
         hidden[:, cols] = mixed
         square = square + jnp.sum(mixed * mixed, axis=-1, keepdims=True)
     scale_h = lax.rsqrt(square * (1.0 / (HEADS * HD)) + NORM_EPS)
-    table = slot_table(routes)[0].astype(BF)
-    rows = mm(table, (hidden[...] * scale_h).astype(BF))
-    to_travel(rows, scratch, SLOTS)
+    table, is_first = slot_table(routes, 16)
+    gate = slot_gates(table, is_first, gates)
+    table = table.astype(BF)
+    slots_to_travel(mm(table, (hidden[...] * scale_h).astype(BF)), scratch, 0)
+    slots_to_travel(mm(table, cot[...]) * gate, scratch, 1)
     low = scratch[...].astype(BF)
     for d in range(sent.shape[0]):
         sent[d] = low
 
 
-def rows_kernel(own, other, out, scratch):
-    half = own.shape[0] // 16
-    for i, ref in enumerate((own, other)):
-        scratch[...] = ref[...].astype(F32)
-        for c in range(out.shape[1] // LANES):
-            out[i * half : (i + 1) * half, c * LANES : (c + 1) * LANES] = from_travel(
+def rows_kernel(got, out, scratch):
+    half = out.shape[0] // 2
+    for kind in range(2):
+        for j in range(got.shape[0]):
+            start = kind * TRAVEL_ROWS
+            scratch[j * TRAVEL_ROWS : (j + 1) * TRAVEL_ROWS, :] = got[
+                j, start : start + TRAVEL_ROWS, :
+            ].astype(F32)
+        for c in range(16):
+            out[kind * half : (kind + 1) * half, c * LANES : (c + 1) * LANES] = from_travel(
                 scratch, half, c
             ).astype(BF)
 
@@ -168,9 +169,14 @@
         out[...] = scratch[...].astype(BF)
 
 
-def expert_back_kernel(place, rows_in, rows_grad, *refs):
-    pieces, (own, other, gelu, up, down, sc_own, sc_other) = refs[:-7], refs[-7:]
+def expert_back_kernel(place, rows_own, rows_other, *refs):
+    pieces, refs = refs[:-9], refs[-9:]
+    own, other, gelu, up, down, sc_own, sc_other, rows_in, rows_grad = refs
     assemble(place, pieces, up, down)
+    half = rows_own.shape[0] // 2
+    for i, ref in enumerate((rows_own, rows_other)):
+        rows_in[i * half : (i + 1) * half, :] = ref[0:half, :]
+        rows_grad[i * half : (i + 1) * half, :] = ref[half : 2 * half, :]
     pre_act = mm(rows_in[...], up[...])
     value, slope = gelu_parts(pre_act)
     gelu[...] = value.astype(BF)
@@ -193,14 +199,32 @@
 
 
 def assemble(place, pieces, up, down):
-    (whole,) = pieces
-    block = LANES
-    for tm in range(16):
-        up[tm * block : (tm + 1) * block, :] = whole[tm, 0:block, :]
-        for q in range(4):
-            down[q * block : (q + 1) * block, tm * block : (tm + 1) * block] = whole[
-                tm, block : 2 * block, q * block : (q + 1) * block
-            ]
+    x, zh = place[0], place[1]
+
+    def put(part, block, x, zh):
+        start = pl.multiple_of(((x & 3) * 4 + (zh & 3)) * LANES, LANES)
+        if part == 0:
+            up[pl.ds(start, LANES), :] = block[...]
+        else:
+            for q in range(4):
+                cols = slice(q * LANES, (q + 1) * LANES)
+                down[cols, pl.ds(start, LANES)] = block[:, cols]
+
+    def put_ring(refs, first_zh):
+        own, before, after, low, high = refs
+        count = own.shape[0] // LANES
+        for i in range(count):
+            rows = pl.ds(i * LANES, LANES)
+            for ref, step in ((own, 0), (before, 3), (after, 1)):
+                put(i % 2, ref.at[rows], x + step, first_zh + i // 2)
+            far, j = (low, i) if 2 * i < count else (high, i - count // 2)
+            put(i % 2, far.at[pl.ds(j * LANES, LANES)], x + 2, first_zh + i // 2)
+
+    put_ring(pieces[0:5], zh)
+    put_ring(pieces[5:10], zh + 1)
+    for i in range(4):
+        for part in range(2):
+            put(part, pieces[10].at[i, pl.ds(part * LANES, LANES)], i, zh + 3)
 
 
 def slot_sum(back, scratch):
@@ -240,18 +264,18 @@
         grad_hidden = grad_h[:, cols]
         grad_low = grad_hidden.astype(BF)
         att = probs[h]
-        grad_probs = mm(grad_low, v_all[:, cols], NT)
-        inner = jnp.sum(att * grad_probs, axis=-1, keepdims=True)
+        grad_probs = mm(v_all[:, cols], grad_low, NT)
+        inner = jnp.sum(att * grad_probs, axis=0, keepdims=True)
         scores_low = (att * (grad_probs - inner) * INV_ROOT_HD).astype(BF)
         query, scale_q = query_of(dec[:, cols].astype(F32))
-        grad_query = mm(scores_low, k_all[:, cols])
+        grad_query = mm(scores_low, k_all[:, cols], TN)
         piece = scale_q * (
             grad_query - query * jnp.mean(grad_query * query, axis=-1, keepdims=True)
         )
         grad_in[:, cols] = (grad_hidden + piece).astype(BF)
         both = (
-            mm(scores_low, query.astype(BF), TN),
-            mm(att.astype(BF), grad_low, TN),
+            mm(scores_low, query.astype(BF)),
+            mm(att.astype(BF), grad_low),
         )
         for i, (grad, ref) in enumerate(zip(both, (grad_k, grad_v))):
             ref[:, cols] = grad[HALO : HALO + tokens, :].astype(BF)
@@ -276,35 +300,48 @@
 
 
 def exchange(sent):
-    shape = sent.shape
-    got = lax.all_to_all(
-        sent.reshape(-1, 160, LANES), ("dp", "y"), split_axis=0, concat_axis=0, tiled=True
-    )
-    return got.reshape(shape)
-
-
-def gather_weights(up_local, down_local):
+    axes = ("dp", "zh", "y", "core")
+    dp, zh, y, core = (lax.axis_size(axis) for axis in axes)
+    groups = []
+    for c in range(core):
+        for run in range(zh):
+            members = []
+            for step in range(dp):
+                z = (run * dp + step + 2 * c) % (dp * zh)
+                members += [((z % dp * zh + z // dp) * y + i) * core + c for i in range(y)]
+            groups.append(members)
+    return lax.all_to_all(
+        sent, axes, split_axis=0, concat_axis=0, axis_index_groups=groups, tiled=True
+    )
+
+
+def pack_weights(up_local, down_local):
     turned = down_local.reshape(4, LANES, LANES).transpose(1, 0, 2).reshape(LANES, 4 * LANES)
-    packed = jnp.concatenate([up_local, turned], axis=0)
-    whole = lax.all_gather(packed, ("x", "zh"), axis=0, tiled=True)
-    return (whole.reshape(16, 2 * LANES, 4 * LANES),)
+    return jnp.concatenate([up_local, turned], axis=0)
+
+
+def ring_sides(block):
+    return shift(block, "x", 1), shift(block, "x", -1)
+
+
+def ring_opposite(before, after):
+    half = before.shape[0] // 2
+    return shift(before[:half], "x", 1), shift(after[half:], "x", -1)
 
 
 def slot_rows(got):
-    mine = got.reshape(-1, LANES)
-    other = shift(mine, "core", 1)
-    count = mine.shape[0]
+    count = got.shape[0] * SLOT_LIMIT
     return call(
         rows_kernel,
-        [shaped((2 * count // 16, 16 * LANES), BF)],
-        (mine, other),
-        scratch=[pltpu.VMEM((count, LANES), F32)],
+        [shaped((2 * count, 16 * LANES), BF)],
+        (got,),
+        scratch=[pltpu.VMEM((count * 16, LANES), F32)],
     )[0]
 
 
 def send_back(own, other):
     total = own.astype(F32) + shift(other, "core", 1).astype(F32)
-    return exchange(total.astype(BF).reshape(4, EXPERTS * 160, LANES))
+    return exchange(total.astype(BF).reshape(16, TRAVEL_ROWS, LANES)).reshape(4, -1, LANES)
 
 
 def shards(
@@ -315,38 +352,50 @@
     span = tokens + 2 * HALO
     position = lax.axis_index(("x", "zh", "y", "core"))
     place = jnp.stack([lax.axis_index("x"), lax.axis_index("zh")]).astype(jnp.int32)
-    bounds = jnp.stack([win_start[0], win_end[0]], axis=1) - (position * tokens - HALO)
+    bounds = jnp.stack([win_start[0], win_end[0]], axis=0) - (position * tokens - HALO)
     routes_t = routes[0].T
     gates_t = gate_probs[0].T
 
-    pieces = gather_weights(w_up[0], w_down[0])
+    packed = pack_weights(w_up[0], w_down[0])
+    column = lax.all_gather(packed, "zh", axis=0, tiled=True)
     halo_lo, halo_hi = neighbours(
         jnp.stack([keys[tokens - HALO :], values[tokens - HALO :]]),
         jnp.stack([keys[:HALO], values[:HALO]]),
     )
-
-    travel = (4, EXPERTS * 160, LANES)
-    (grad_sent,) = call(
-        grad_slots_kernel,
-        [shaped(travel, BF)],
-        (routes_t, gates_t, cot),
-        scratch=[pltpu.VMEM(travel[1:], F32)],
-    )
-    grad_rows = slot_rows(exchange(grad_sent))
-
-    in_sent, hidden, probs = call(
+    for_x, halo_lo, halo_hi = lax.optimization_barrier((packed, halo_lo, halo_hi))
+    own_sides = ring_sides(for_x)
+    own_opposite = ring_opposite(*own_sides)
+
+    travel = (4, 2 * EXPERTS * TRAVEL_ROWS, LANES)
+    sent, hidden, probs = call(
         attend_kernel,
-        [shaped(travel, BF), shaped((tokens, feat), F32), shaped((HEADS, tokens, span), F32)],
-        (routes_t, bounds, dec, keys, values, halo_lo, halo_hi),
+        [shaped(travel, BF), shaped((tokens, feat), F32), shaped((HEADS, span, tokens), F32)],
+        (routes_t, gates_t, bounds, dec, cot, keys, values, halo_lo, halo_hi),
         scratch=[
             pltpu.VMEM((span, feat), BF),
             pltpu.VMEM((span, feat), BF),
             pltpu.VMEM(travel[1:], F32),
         ],
     )
-    in_rows = slot_rows(exchange(in_sent))
-
-    rows, units = in_rows.shape[0], 4 * LANES
+    sent, column, own_sides, own_opposite = lax.optimization_barrier(
+        (sent, column, own_sides, own_opposite)
+    )
+    got = exchange(sent.reshape(16, 2 * TRAVEL_ROWS, LANES))
+    block = packed.shape[0]
+    nexts = [
+        lax.dynamic_slice_in_dim(column, (place[1] + step) % 4 * block, block, 0)
+        for step in range(1, 4)
+    ]
+    two, last = jnp.concatenate(nexts[:2], axis=0), nexts[2]
+    last_x = lax.all_gather(last, "x", axis=0)
+    two_sides = ring_sides(two)
+    two_opposite = ring_opposite(*two_sides)
+    got, two_sides = lax.optimization_barrier((got, two_sides))
+    own_rows = slot_rows(got)
+    other_rows = shift(own_rows, "core", 1)
+    pieces = (packed, *own_sides, *own_opposite, two, *two_sides, *two_opposite, last_x)
+
+    rows, units = own_rows.shape[0], 4 * LANES
     half = (rows // 2 * 16, LANES)
     back_own, back_other, gelu, up_full, down_full = call(
         expert_back_kernel,
@@ -357,8 +406,14 @@
             shaped((feat, units), BF),
             shaped((units, feat), BF),
         ],
-        (place, in_rows, grad_rows, *pieces),
-        scratch=[pltpu.VMEM(half, F32), pltpu.VMEM(half, F32)],
+        (place, own_rows, other_rows, *pieces),
+        scratch=[
+            pltpu.VMEM(half, F32),
+            pltpu.VMEM(half, F32),
+            pltpu.VMEM((rows, feat), BF),
+            pltpu.VMEM((rows, feat), BF),
+        ],
+        scalars=1,
     )
     back = send_back(back_own, back_other)
     value_own, value_other = call(
@@ -382,7 +437,7 @@
         scratch=[
             pltpu.VMEM((span, feat), BF),
             pltpu.VMEM((span, feat), BF),
-            pltpu.VMEM(travel[1:], F32),
+            pltpu.VMEM((SLOTS * 16, LANES), F32),
             pltpu.VMEM((tokens, feat), F32),
         ],
     )
@@ -391,7 +446,7 @@
         out_kernel,
         [shaped((tokens, feat), BF)],
         (routes_t, gates_t, result, hidden),
-        scratch=[pltpu.VMEM(travel[1:], F32)],
+        scratch=[pltpu.VMEM((SLOTS * 16, LANES), F32)],
     )
     grads = []
     for i, grad in enumerate((grad_k, grad_v)):

time: 248 us -> 207 us (0.83)
  the two profiles are of different devices: /device:TPU:59 before, /device:TPU:57 now
where the time goes in v2:
time: 207 us; the launch traced here: 205 us
  starting transfers between devices  78.5 us (38%)
  waiting for transfers between devices  62.4 us (30%)
  Pallas kernels  34.4 us (17%)
  between operations  14.5 us (7%)
  other arithmetic  8.45 us (4%)
  local copies, waits for them, and re-layouts  7.15 us (3%)
    pallas_call x6, Pallas kernels, call(): pl.pallas_call(body, out_shape=outs, in_specs=[pl.BlockSpec(memory_space=...  34.4 us
    ppermute x11, starting transfers between devices, shift(): lax.ppermute(value, axis, [(i, (i + step) % count) for i in range(count)])  33.8 us
    all_to_all x3, starting transfers between devices, exchange(): lax.all_to_all(sent, axes, split_axis=0, concat_axis=0, axis_index_groups...  29.3 us
    ppermute x11, waiting for transfers between devices, shift(): lax.ppermute(value, axis, [(i, (i + step) % count) for i in range(count)])  27.8 us
    ppermute x2, waiting for transfers between devices, neighbours(): lax.ppermute(head, axes, [(i + 1, i) for i in range(count - 1)])  16.1 us
    all_gather x1, waiting for transfers between devices, shards(): column = lax.all_gather(packed, 'zh', axis=0, tiled=True)  13.3 us
    ppermute x2, starting transfers between devices, neighbours(): lax.ppermute(tail, axes, [(i, i + 1) for i in range(count - 1)])  11.4 us
    convert_element_type x2, other arithmetic, send_back(): total.astype(BF).reshape(16, TRAVEL_ROWS, LANES)  4.22 us
  transfers between devices with their start and end apart: 20, of which 13 were waited for; matrix products, arithmetic and copies ran while one was open for 3% of the time, Pallas kernels for 13%

profile of v2, /device:TPU:57, one launch (start us, length us, event | category | flops | bytes accessed | tf_op | source)
XLA Modules:
  0.0 205.3 jit_solution(17541263801348448093)
XLA Ops:
  7.2 0.0 all-gather.4.cloned.1.call-start
  7.2 1.0 copy.14
  8.2 0.0 copy-start.18
  8.2 0.0 copy-start.19
  8.3 1.6 pad_maximum_fusion.1.refs_0_
  9.9 0.0 all-gather.4.cloned.1.call-update
  9.9 1.0 fusion.8
  11.0 9.0 %collective-permute-start = (bf16[2,16,2048]{2,1,0:T(8,128)(2,1)S(1)}, bf16[2,16,2048]{2,1,0:T(8,128)(2,1)S(1)}, u32[]{:S(2)}, u32[]{:S(2)}) collective-permute-start(bf16[2,16,2048]{2,1,0:T(8,128)(2,1)S(1)} %pad_maximum_fusion.2), channel_id=1, source_target_pairs={{0,1},{1,2},{2,3},{3,4},{4,5},{5,6},{6,7},{7,8},{8,9},{9,10},{10,1... | collective-permute-start | bytes 393224 | tf_op jit(solution)/shard_map/ppermute | solution.py:297
  20.0 1.9 collective-permute-start.1
  21.9 2.0 collective-permute-done.halo_lo
  23.9 8.5 %collective-permute-done.1.halo_hi = bf16[2,16,2048]{2,1,0:T(8,128)(2,1)S(1)} collective-permute-done((bf16[2,16,2048]{2,1,0:T(8,128)(2,1)S(1)}, bf16[2,16,2048]{2,1,0:T(8,128)(2,1)S(1)}, u32[]{:S(2)}, u32[]{:S(2)}) %collective-permute-start.1) | collective-permute-done | bytes 131104 | tf_op jit(solution)/shard_map/ppermute | solution.py:298
  32.4 4.7 %collective-permute-start.3 = (bf16[256,512]{1,0:T(8,128)(2,1)S(1)}, bf16[256,512]{1,0:T(8,128)(2,1)S(1)}, u32[]{:S(2)}, u32[]{:S(2)}) collective-permute-start(bf16[256,512]{1,0:T(8,128)(2,1)S(1)} %copy-done.3), channel_id=1, source_target_pairs={{0,96},{32,0},{64,32},{96,64},{1,97},{33,1},{65,33},{97,65},{2,98}... | collective-permute-start | bytes 786440 | tf_op jit(solution)/shard_map/ppermute | solution.py:290
  37.1 1.9 collective-permute-start.2
  39.0 2.8 %collective-permute-done.3.refs_2_ = bf16[256,512]{1,0:T(8,128)(2,1)S(1)} collective-permute-done((bf16[256,512]{1,0:T(8,128)(2,1)S(1)}, bf16[256,512]{1,0:T(8,128)(2,1)S(1)}, u32[]{:S(2)}, u32[]{:S(2)}) %collective-permute-start.3) | collective-permute-done | bytes 262176 | tf_op jit(solution)/shard_map/ppermute | solution.py:290
  41.8 5.4 %collective-permute-start.5 = (bf16[128,512]{1,0:T(8,128)(2,1)S(1)}, bf16[128,512]{1,0:T(8,128)(2,1)S(1)}, u32[]{:S(2)}, u32[]{:S(2)}) collective-permute-start(bf16[128,512]{1,0:T(8,128)(2,1)S(1)} %slice.77), channel_id=1, source_target_pairs={{0,96},{32,0},{64,32},{96,64},{1,97},{33,1},{65,33},{97,65},{2,98}... | collective-permute-start | bytes 393224 | tf_op jit(solution)/shard_map/ppermute | solution.py:290
  47.2 0.0 collective-permute-done.2.refs_1_
  47.3 1.9 collective-permute-start.4
  49.2 0.6 add_subtract_fusion.bounds
  49.8 8.0 %shard_map.129 = (bf16[4,1280,128]{2,1,0:T(8,128)(2,1)}, f32[128,2048]{1,0:T(8,128)}, f32[16,160,128]{2,1,0:T(8,128)}) custom-call(s32[2,128]{1,0:T(2,128)} %bitcast.74, f32[2,128]{1,0:T(2,128)} %bitcast.77, s32[2,128]{1,0:T(2,128)} %add_subtract_fusion.bounds, bf16[128,2048]{1,0:T(8,128)(2,1)} %bitcast.63, bf16[128,2048]{1,0:T(8,128)(2,1)} %bitcast.65, ...), custom_call_target="tpu_custom_call" | custom-call | flops 100000000 | bytes 6032384 | tf_op jit(solution)/shard_map/pallas_call | solution.py:39
  57.8 0.0 collective-permute-done.5.refs_4_
  57.9 0.0 collective-permute-done.4.refs_3_
  57.9 13.3 %all-gather.4.cloned.1.call-done = bf16[1024,512]{1,0:T(8,128)(2,1)} async-done(((bf16[256,512]{1,0:T(8,128)(2,1)}), bf16[1024,512]{1,0:T(8,128)(2,1)}) %all-gather.4.cloned.1.call-update) | async-done | bytes 1048592 | tf_op jit(solution)/shard_map/all_gather | solution.py:360
  71.2 10.3 %all-to-all-start = ((bf16[16,320,128]{2,1,0:T(8,128)(2,1)}), bf16[16,320,128]{2,1,0:T(8,128)(2,1)S(1)}, u32[]{:S(2)}, u32[]{:S(2)}) async-start(bf16[16,320,128]{2,1,0:T(8,128)(2,1)} %bitcast.67), calls=%async_computation | async-start | bytes 2621440 | tf_op jit(solution)/shard_map/all_to_all | solution.py:313
  81.5 0.0 all-gather.6.cloned.1.call-start
  81.6 0.8 constant_dynamic-slice_fusion
  82.4 0.0 copy-start.4
  82.4 4.3 %collective-permute-start.7 = (bf16[512,512]{1,0:T(8,128)(2,1)S(1)}, bf16[512,512]{1,0:T(8,128)(2,1)S(1)}, u32[]{:S(2)}, u32[]{:S(2)}) collective-permute-start(bf16[512,512]{1,0:T(8,128)(2,1)S(1)} %pad_maximum_fusion.refs_5_), channel_id=1, source_target_pairs={{0,96},{32,0},{64,32},{96,64},{1,97},{33,1},{65,33},{97,65},{2,98}... | collective-permute-start | bytes 1572872 | tf_op jit(solution)/shard_map/ppermute | solution.py:290
  86.8 1.9 collective-permute-start.6
  88.7 0.0 all-gather.6.cloned.1.call-update
  88.7 8.2 %collective-permute-done.7.refs_7_ = bf16[512,512]{1,0:T(8,128)(2,1)S(1)} collective-permute-done((bf16[512,512]{1,0:T(8,128)(2,1)S(1)}, bf16[512,512]{1,0:T(8,128)(2,1)S(1)}, u32[]{:S(2)}, u32[]{:S(2)}) %collective-permute-start.7) | collective-permute-done | bytes 524320 | tf_op jit(solution)/shard_map/ppermute | solution.py:290
  96.9 5.0 %collective-permute-done.6.refs_6_ = bf16[512,512]{1,0:T(8,128)(2,1)S(1)} collective-permute-done((bf16[512,512]{1,0:T(8,128)(2,1)S(1)}, bf16[512,512]{1,0:T(8,128)(2,1)S(1)}, u32[]{:S(2)}, u32[]{:S(2)}) %collective-permute-start.6) | collective-permute-done | bytes 524320 | tf_op jit(solution)/shard_map/ppermute | solution.py:290
  101.9 2.0 all-to-all-done.got
  103.9 1.1 copy-done
  105.0 3.5 %shard_map.130.rows_own = bf16[320,2048]{1,0:T(8,128)(2,1)} custom-call(bf16[16,320,128]{2,1,0:T(8,128)(2,1)} %copy-done), custom_call_target="tpu_custom_call" | custom-call | flops 100000000 | bytes 2621440 | tf_op jit(solution)/shard_map/pallas_call | solution.py:39
  108.5 2.3 %collective-permute-start.8 = (bf16[320,2048]{1,0:T(8,128)(2,1)}, bf16[320,2048]{1,0:T(8,128)(2,1)S(1)}, u32[]{:S(2)}, u32[]{:S(2)}) collective-permute-start(bf16[320,2048]{1,0:T(8,128)(2,1)} %shard_map.130.rows_own), channel_id=1, source_target_pairs={{0,1},{1,0},{2,3},{3,2},{4,5},{5,4},{6,7},{7,6},{8,9},{9,8},{10,11... | collective-permute-start | bytes 3932168 | tf_op jit(solution)/shard_map/ppermute | solution.py:290
  110.8 3.9 %collective-permute-start.10 = (bf16[256,512]{1,0:T(8,128)(2,1)S(1)}, bf16[256,512]{1,0:T(8,128)(2,1)S(1)}, u32[]{:S(2)}, u32[]{:S(2)}) collective-permute-start(bf16[256,512]{1,0:T(8,128)(2,1)S(1)} %slice.79), channel_id=1, source_target_pairs={{0,96},{32,0},{64,32},{96,64},{1,97},{33,1},{65,33},{97,65},{2,98}... | collective-permute-start | bytes 786440 | tf_op jit(solution)/shard_map/ppermute | solution.py:290
  114.8 1.9 collective-permute-start.9
  116.7 0.6 pad_add_fusion.place
  117.3 3.4 %collective-permute-done.10.refs_9_ = bf16[256,512]{1,0:T(8,128)(2,1)S(1)} collective-permute-done((bf16[256,512]{1,0:T(8,128)(2,1)S(1)}, bf16[256,512]{1,0:T(8,128)(2,1)S(1)}, u32[]{:S(2)}, u32[]{:S(2)}) %collective-permute-start.10) | collective-permute-done | bytes 262176 | tf_op jit(solution)/shard_map/ppermute | solution.py:290
  120.7 4.3 %collective-permute-done.9.refs_8_ = bf16[256,512]{1,0:T(8,128)(2,1)S(1)} collective-permute-done((bf16[256,512]{1,0:T(8,128)(2,1)S(1)}, bf16[256,512]{1,0:T(8,128)(2,1)S(1)}, u32[]{:S(2)}, u32[]{:S(2)}) %collective-permute-start.9) | collective-permute-done | bytes 262176 | tf_op jit(solution)/shard_map/ppermute | solution.py:290
  124.9 0.0 collective-permute-done.8.rows_other
  125.0 0.7 copy-done.15
  125.7 0.5 copy-done.5
  126.2 7.5 %shard_map.131 = (bf16[2560,128]{1,0:T(8,128)(2,1)}, bf16[2560,128]{1,0:T(8,128)(2,1)}, bf16[320,512]{1,0:T(8,128)(2,1)}, bf16[2048,512]{1,0:T(8,128)(2,1)}, bf16[512,2048]{1,0:T(8,128)(2,1)}) custom-call(s32[2]{0:T(128)} %pad_add_fusion.place, bf16[320,2048]{1,0:T(8,128)(2,1)} %shard_map.130.rows_own, bf16[320,2048]{1,0:T(8,128)(2,1)} %copy-done.5, ...), custom_call_target="tpu_custom_call" | custom-call | flops 100000000 | bytes 12648456 | tf_op jit(solution)/shard_map/pallas_call | solution.py:39
  133.7 3.6 %collective-permute-start.12 = (bf16[2560,128]{1,0:T(8,128)(2,1)}, bf16[2560,128]{1,0:T(8,128)(2,1)S(1)}, u32[]{:S(2)}, u32[]{:S(2)}) collective-permute-start(bf16[2560,128]{1,0:T(8,128)(2,1)} %get-tuple-element.49), channel_id=1, source_target_pairs={{0,1},{1,0},{2,3},{3,2},{4,5},{5,4},{6,7},{7,6},{8,9},{9,8},{10,11... | collective-permute-start | bytes 1966088 | tf_op jit(solution)/shard_map/ppermute | solution.py:290
  137.2 1.9 collective-permute-done.12
  139.2 2.1 %add_convert_fusion = bf16[2560,128]{1,0:T(8,128)(2,1)} fusion(bf16[2560,128]{1,0:T(8,128)(2,1)S(1)} %collective-permute-done.12, bf16[2560,128]{1,0:T(8,128)(2,1)} %get-tuple-element.48), kind=kLoop, calls=%fused_computation | loop fusion | flops 1310720 | bytes 1966080 | tf_op jit(solution)/shard_map/convert_element_type | solution.py:344
  141.3 10.3 %all-to-all-start.2 = ((bf16[16,160,128]{2,1,0:T(8,128)(2,1)}), bf16[16,160,128]{2,1,0:T(8,128)(2,1)S(1)}, u32[]{:S(2)}, u32[]{:S(2)}) async-start(bf16[16,160,128]{2,1,0:T(8,128)(2,1)} %bitcast.20), calls=%async_computation.2 | async-start | bytes 1310720 | tf_op jit(solution)/shard_map/all_to_all | solution.py:313
  151.6 4.0 %shard_map.132 = (bf16[2560,128]{1,0:T(8,128)(2,1)}, bf16[2560,128]{1,0:T(8,128)(2,1)}) custom-call(bf16[320,512]{1,0:T(8,128)(2,1)} %get-tuple-element.43.gelu, bf16[512,2048]{1,0:T(8,128)(2,1)} %get-tuple-element.44.down), custom_call_target="tpu_custom_call" | custom-call | flops 100000000 | bytes 3735552 | tf_op jit(solution)/shard_map/pallas_call | solution.py:39
  155.5 1.9 collective-permute-start.11
  157.4 2.3 %collective-permute-done.11 = bf16[2560,128]{1,0:T(8,128)(2,1)S(1)} collective-permute-done((bf16[2560,128]{1,0:T(8,128)(2,1)}, bf16[2560,128]{1,0:T(8,128)(2,1)S(1)}, u32[]{:S(2)}, u32[]{:S(2)}) %collective-permute-start.11) | collective-permute-done | bytes 655392 | tf_op jit(solution)/shard_map/ppermute | solution.py:290
  159.7 2.1 %add_convert_fusion.1 = bf16[2560,128]{1,0:T(8,128)(2,1)} fusion(bf16[2560,128]{1,0:T(8,128)(2,1)S(1)} %collective-permute-done.11, bf16[2560,128]{1,0:T(8,128)(2,1)} %get-tuple-element.45), kind=kLoop, calls=%fused_computation.1 | loop fusion | flops 1310720 | bytes 1966080 | tf_op jit(solution)/shard_map/convert_element_type | solution.py:344
  161.8 1.2 all-to-all-done.2
  163.1 8.7 %all-to-all-start.1 = ((bf16[16,160,128]{2,1,0:T(8,128)(2,1)}), bf16[16,160,128]{2,1,0:T(8,128)(2,1)S(1)}, u32[]{:S(2)}, u32[]{:S(2)}) async-start(bf16[16,160,128]{2,1,0:T(8,128)(2,1)} %bitcast.17), calls=%async_computation.1 | async-start | bytes 1310720 | tf_op jit(solution)/shard_map/all_to_all | solution.py:313
  171.7 8.5 %shard_map.134 = (bf16[128,2048]{1,0:T(8,128)(2,1)}, bf16[128,2048]{1,0:T(8,128)(2,1)}, bf16[128,2048]{1,0:T(8,128)(2,1)}, f32[2,2,16,2048]{3,2,1,0:T(8,128)}, bf16[2,2,16,2048]{3,2,1,0:T(8,128)(2,1)}) custom-call(s32[2,128]{1,0:T(2,128)} %bitcast.75, bf16[4,640,128]{2,1,0:T(8,128)(2,1)} %bitcast.62, bf16[128,2048]{1,0:T(8,128)(2,1)} %bitcast.66, ...), custom_call_target="tpu_custom_call" | custom-call | flops 100000000 | bytes 7734272 | tf_op jit(solution)/shard_map/pallas_call | solution.py:39
  180.3 1.0 slice_bitcast_fusion
  181.3 2.3 %collective-permute-start.13 = (bf16[2,16,2048]{2,1,0:T(8,128)(2,1)S(1)}, bf16[2,16,2048]{2,1,0:T(8,128)(2,1)S(1)}, u32[]{:S(2)}, u32[]{:S(2)}) collective-permute-start(bf16[2,16,2048]{2,1,0:T(8,128)(2,1)S(1)} %get-tuple-element.68), channel_id=1, source_target_pairs={{0,1},{1,2},{2,3},{3,4},{4,5},{5,6},{6,7},{7,8},{8,9},{9,10},{10,1... | collective-permute-start | bytes 393224 | tf_op jit(solution)/shard_map/ppermute | solution.py:297
  183.6 2.0 collective-permute-start.14
  185.7 0.0 all-to-all-done.1
  185.7 0.9 copy-done.1
  186.5 2.9 %shard_map.133 = bf16[128,2048]{1,0:T(8,128)(2,1)} custom-call(s32[2,128]{1,0:T(2,128)} %bitcast.76, f32[2,128]{1,0:T(2,128)} %bitcast.78, bf16[4,640,128]{2,1,0:T(8,128)(2,1)} %bitcast.61, f32[128,2048]{1,0:T(8,128)} %get-tuple-element.47.hidden), custom_call_target="tpu_custom_call" | custom-call | flops 100000000 | bytes 2230272 | tf_op jit(solution)/shard_map/pallas_call | solution.py:39
  189.5 0.7 fusion.6
  190.1 7.6 %collective-permute-done.14 = bf16[2,16,2048]{2,1,0:T(8,128)(2,1)S(1)} collective-permute-done((bf16[2,16,2048]{2,1,0:T(8,128)(2,1)S(1)}, bf16[2,16,2048]{2,1,0:T(8,128)(2,1)S(1)}, u32[]{:S(2)}, u32[]{:S(2)}) %collective-permute-start.14) | collective-permute-done | bytes 131104 | tf_op jit(solution)/shard_map/ppermute | solution.py:298
  197.8 0.7 fusion.7
  (43 shorter events, 0.2 us)
Async XLA Ops:
  7.2 64.0 %all-gather.4.cloned.1.call-start = ((), (), s32[]{:S(2)}) async-start(), calls=%async_computation.3 | async-start | bytes 1310720 | tf_op jit(solution)/shard_map/all_gather | solution.py:360
  8.2 41.0 %copy-start.18 = (s32[1,128]{1,0:T(1,128)S(1)}, s32[1,128]{1,0:T(1,128)}, u32[]{:S(2)}) copy-start(s32[1,128]{1,0:T(1,128)} %param.14) | copy-start | bytes 1540
  8.2 41.0 %copy-start.19 = (s32[1,128]{1,0:T(1,128)S(1)}, s32[1,128]{1,0:T(1,128)}, u32[]{:S(2)}) copy-start(s32[1,128]{1,0:T(1,128)} %param.13) | copy-start | bytes 1540
  9.9 22.5 %copy-start.3 = (bf16[256,512]{1,0:T(8,128)(2,1)S(1)}, bf16[256,512]{1,0:T(8,128)(2,1)}, u32[]{:S(2)}) copy-start(bf16[256,512]{1,0:T(8,128)(2,1)} %pad_maximum_fusion.1.refs_0_) | copy-start | bytes 786436
  11.0 13.0 %collective-permute-start = (bf16[2,16,2048]{2,1,0:T(8,128)(2,1)S(1)}, bf16[2,16,2048]{2,1,0:T(8,128)(2,1)S(1)}, u32[]{:S(2)}, u32[]{:S(2)}) collective-permute-start(bf16[2,16,2048]{2,1,0:T(8,128)(2,1)S(1)} %pad_maximum_fusion.2), channel_id=1, source_target_pairs={{0,1},{1,2},{2,3},{3,4},{4,5},{5,6},{6,7},{7,8},{8,9},{9,10},{10,1... | collective-permute-start | bytes 393224 | tf_op jit(solution)/shard_map/ppermute | solution.py:297
  20.0 12.4 %collective-permute-start.1 = (bf16[2,16,2048]{2,1,0:T(8,128)(2,1)S(1)}, bf16[2,16,2048]{2,1,0:T(8,128)(2,1)S(1)}, u32[]{:S(2)}, u32[]{:S(2)}) collective-permute-start(bf16[2,16,2048]{2,1,0:T(8,128)(2,1)S(1)} %pad_maximum_fusion.3), channel_id=1, source_target_pairs={{1,0},{2,1},{3,2},{4,3},{5,4},{6,5},{7,6},{8,7},{9,8},{10,9},{11,1... | collective-permute-start | bytes 393224 | tf_op jit(solution)/shard_map/ppermute | solution.py:298
  23.9 25.9 %copy-start.11 = (bf16[2,16,2048]{2,1,0:T(8,128)(2,1)}, bf16[2,16,2048]{2,1,0:T(8,128)(2,1)S(1)}, u32[]{:S(2)}) copy-start(bf16[2,16,2048]{2,1,0:T(8,128)(2,1)S(1)} %collective-permute-done.halo_lo) | copy-start | bytes 393220
  32.4 17.4 %copy-start.12 = (bf16[2,16,2048]{2,1,0:T(8,128)(2,1)}, bf16[2,16,2048]{2,1,0:T(8,128)(2,1)S(1)}, u32[]{:S(2)}) copy-start(bf16[2,16,2048]{2,1,0:T(8,128)(2,1)S(1)} %collective-permute-done.1.halo_hi) | copy-start | bytes 393220
  32.4 9.4 %collective-permute-start.3 = (bf16[256,512]{1,0:T(8,128)(2,1)S(1)}, bf16[256,512]{1,0:T(8,128)(2,1)S(1)}, u32[]{:S(2)}, u32[]{:S(2)}) collective-permute-start(bf16[256,512]{1,0:T(8,128)(2,1)S(1)} %copy-done.3), channel_id=1, source_target_pairs={{0,96},{32,0},{64,32},{96,64},{1,97},{33,1},{65,33},{97,65},{2,98}... | collective-permute-start | bytes 786440 | tf_op jit(solution)/shard_map/ppermute | solution.py:290
  37.1 10.2 %collective-permute-start.2 = (bf16[256,512]{1,0:T(8,128)(2,1)S(1)}, bf16[256,512]{1,0:T(8,128)(2,1)S(1)}, u32[]{:S(2)}, u32[]{:S(2)}) collective-permute-start(bf16[256,512]{1,0:T(8,128)(2,1)S(1)} %copy-done.3), channel_id=1, source_target_pairs={{0,32},{32,64},{64,96},{96,0},{1,33},{33,65},{65,97},{97,1},{2,34}... | collective-permute-start | bytes 786440 | tf_op jit(solution)/shard_map/ppermute | solution.py:290
  41.8 16.1 %copy-start.8 = (bf16[256,512]{1,0:T(8,128)(2,1)}, bf16[256,512]{1,0:T(8,128)(2,1)S(1)}, u32[]{:S(2)}) copy-start(bf16[256,512]{1,0:T(8,128)(2,1)S(1)} %collective-permute-done.3.refs_2_) | copy-start | bytes 786436
  41.8 16.1 %collective-permute-start.5 = (bf16[128,512]{1,0:T(8,128)(2,1)S(1)}, bf16[128,512]{1,0:T(8,128)(2,1)S(1)}, u32[]{:S(2)}, u32[]{:S(2)}) collective-permute-start(bf16[128,512]{1,0:T(8,128)(2,1)S(1)} %slice.77), channel_id=1, source_target_pairs={{0,96},{32,0},{64,32},{96,64},{1,97},{33,1},{65,33},{97,65},{2,98}... | collective-permute-start | bytes 393224 | tf_op jit(solution)/shard_map/ppermute | solution.py:290
  47.2 10.6 %copy-start.9 = (bf16[256,512]{1,0:T(8,128)(2,1)}, bf16[256,512]{1,0:T(8,128)(2,1)S(1)}, u32[]{:S(2)}) copy-start(bf16[256,512]{1,0:T(8,128)(2,1)S(1)} %collective-permute-done.2.refs_1_) | copy-start | bytes 786436
  47.3 10.6 %collective-permute-start.4 = (bf16[128,512]{1,0:T(8,128)(2,1)S(1)}, bf16[128,512]{1,0:T(8,128)(2,1)S(1)}, u32[]{:S(2)}, u32[]{:S(2)}) collective-permute-start(bf16[128,512]{1,0:T(8,128)(2,1)S(1)} %slice.76), channel_id=1, source_target_pairs={{0,32},{32,64},{64,96},{96,0},{1,33},{33,65},{65,97},{97,1},{2,34}... | collective-permute-start | bytes 393224 | tf_op jit(solution)/shard_map/ppermute | solution.py:290
  57.8 13.4 %copy-start.16 = (bf16[128,512]{1,0:T(8,128)(2,1)}, bf16[128,512]{1,0:T(8,128)(2,1)S(1)}, u32[]{:S(2)}) copy-start(bf16[128,512]{1,0:T(8,128)(2,1)S(1)} %collective-permute-done.5.refs_4_) | copy-start | bytes 393220
  57.9 13.3 %copy-start.17 = (bf16[128,512]{1,0:T(8,128)(2,1)}, bf16[128,512]{1,0:T(8,128)(2,1)S(1)}, u32[]{:S(2)}) copy-start(bf16[128,512]{1,0:T(8,128)(2,1)S(1)} %collective-permute-done.4.refs_3_) | copy-start | bytes 393220
  71.2 10.4 %copy-start.10 = (bf16[1024,512]{1,0:T(8,128)(2,1)S(1)}, bf16[1024,512]{1,0:T(8,128)(2,1)}, u32[]{:S(2)}) copy-start(bf16[1024,512]{1,0:T(8,128)(2,1)} %all-gather.4.cloned.1.call-done) | copy-start | bytes 3145732
  71.2 32.7 %all-to-all-start = ((bf16[16,320,128]{2,1,0:T(8,128)(2,1)}), bf16[16,320,128]{2,1,0:T(8,128)(2,1)S(1)}, u32[]{:S(2)}, u32[]{:S(2)}) async-start(bf16[16,320,128]{2,1,0:T(8,128)(2,1)} %bitcast.67), calls=%async_computation | async-start | bytes 2621440 | tf_op jit(solution)/shard_map/all_to_all | solution.py:313
  81.5 43.4 %all-gather.6.cloned.1.call-start = ((), (), s32[]{:S(2)}) async-start(), calls=%async_computation.4 | async-start | bytes 1310720 | tf_op jit(solution)/shard_map/all_gather | solution.py:390
  82.4 42.5 %copy-start.4 = (bf16[512,512]{1,0:T(8,128)(2,1)}, bf16[512,512]{1,0:T(8,128)(2,1)S(1)}, u32[]{:S(2)}) copy-start(bf16[512,512]{1,0:T(8,128)(2,1)S(1)} %pad_maximum_fusion.refs_5_) | copy-start | bytes 1572868
  82.4 14.4 %collective-permute-start.7 = (bf16[512,512]{1,0:T(8,128)(2,1)S(1)}, bf16[512,512]{1,0:T(8,128)(2,1)S(1)}, u32[]{:S(2)}, u32[]{:S(2)}) collective-permute-start(bf16[512,512]{1,0:T(8,128)(2,1)S(1)} %pad_maximum_fusion.refs_5_), channel_id=1, source_target_pairs={{0,96},{32,0},{64,32},{96,64},{1,97},{33,1},{65,33},{97,65},{2,98}... | collective-permute-start | bytes 1572872 | tf_op jit(solution)/shard_map/ppermute | solution.py:290
  86.8 15.1 %collective-permute-start.6 = (bf16[512,512]{1,0:T(8,128)(2,1)S(1)}, bf16[512,512]{1,0:T(8,128)(2,1)S(1)}, u32[]{:S(2)}, u32[]{:S(2)}) collective-permute-start(bf16[512,512]{1,0:T(8,128)(2,1)S(1)} %pad_maximum_fusion.refs_5_), channel_id=1, source_target_pairs={{0,32},{32,64},{64,96},{96,0},{1,33},{33,65},{65,97},{97,1},{2,34}... | collective-permute-start | bytes 1572872 | tf_op jit(solution)/shard_map/ppermute | solution.py:290
  96.9 28.1 %copy-start.6 = (bf16[512,512]{1,0:T(8,128)(2,1)}, bf16[512,512]{1,0:T(8,128)(2,1)S(1)}, u32[]{:S(2)}) copy-start(bf16[512,512]{1,0:T(8,128)(2,1)S(1)} %collective-permute-done.7.refs_7_) | copy-start | bytes 1572868
  101.9 23.1 %copy-start.7 = (bf16[512,512]{1,0:T(8,128)(2,1)}, bf16[512,512]{1,0:T(8,128)(2,1)S(1)}, u32[]{:S(2)}) copy-start(bf16[512,512]{1,0:T(8,128)(2,1)S(1)} %collective-permute-done.6.refs_6_) | copy-start | bytes 1572868
  103.9 1.1 copy-start
  108.5 16.5 %collective-permute-start.8 = (bf16[320,2048]{1,0:T(8,128)(2,1)}, bf16[320,2048]{1,0:T(8,128)(2,1)S(1)}, u32[]{:S(2)}, u32[]{:S(2)}) collective-permute-start(bf16[320,2048]{1,0:T(8,128)(2,1)} %shard_map.130.rows_own), channel_id=1, source_target_pairs={{0,1},{1,0},{2,3},{3,2},{4,5},{5,4},{6,7},{7,6},{8,9},{9,8},{10,11... | collective-permute-start | bytes 3932168 | tf_op jit(solution)/shard_map/ppermute | solution.py:290
  110.8 9.9 %collective-permute-start.10 = (bf16[256,512]{1,0:T(8,128)(2,1)S(1)}, bf16[256,512]{1,0:T(8,128)(2,1)S(1)}, u32[]{:S(2)}, u32[]{:S(2)}) collective-permute-start(bf16[256,512]{1,0:T(8,128)(2,1)S(1)} %slice.79), channel_id=1, source_target_pairs={{0,96},{32,0},{64,32},{96,64},{1,97},{33,1},{65,33},{97,65},{2,98}... | collective-permute-start | bytes 786440 | tf_op jit(solution)/shard_map/ppermute | solution.py:290
  114.8 10.2 %collective-permute-start.9 = (bf16[256,512]{1,0:T(8,128)(2,1)S(1)}, bf16[256,512]{1,0:T(8,128)(2,1)S(1)}, u32[]{:S(2)}, u32[]{:S(2)}) collective-permute-start(bf16[256,512]{1,0:T(8,128)(2,1)S(1)} %slice.78), channel_id=1, source_target_pairs={{0,32},{32,64},{64,96},{96,0},{1,33},{33,65},{65,97},{97,1},{2,34}... | collective-permute-start | bytes 786440 | tf_op jit(solution)/shard_map/ppermute | solution.py:290
  120.7 4.3 %copy-start.14 = (bf16[256,512]{1,0:T(8,128)(2,1)}, bf16[256,512]{1,0:T(8,128)(2,1)S(1)}, u32[]{:S(2)}) copy-start(bf16[256,512]{1,0:T(8,128)(2,1)S(1)} %collective-permute-done.10.refs_9_) | copy-start | bytes 786436
  124.9 0.7 copy-start.15
  124.9 1.3 copy-start.5
  133.7 5.5 %collective-permute-start.12 = (bf16[2560,128]{1,0:T(8,128)(2,1)}, bf16[2560,128]{1,0:T(8,128)(2,1)S(1)}, u32[]{:S(2)}, u32[]{:S(2)}) collective-permute-start(bf16[2560,128]{1,0:T(8,128)(2,1)} %get-tuple-element.49), channel_id=1, source_target_pairs={{0,1},{1,0},{2,3},{3,2},{4,5},{5,4},{6,7},{7,6},{8,9},{9,8},{10,11... | collective-permute-start | bytes 1966088 | tf_op jit(solution)/shard_map/ppermute | solution.py:290
  141.3 21.8 %all-to-all-start.2 = ((bf16[16,160,128]{2,1,0:T(8,128)(2,1)}), bf16[16,160,128]{2,1,0:T(8,128)(2,1)S(1)}, u32[]{:S(2)}, u32[]{:S(2)}) async-start(bf16[16,160,128]{2,1,0:T(8,128)(2,1)} %bitcast.20), calls=%async_computation.2 | async-start | bytes 1310720 | tf_op jit(solution)/shard_map/all_to_all | solution.py:313
  155.5 4.2 %collective-permute-start.11 = (bf16[2560,128]{1,0:T(8,128)(2,1)}, bf16[2560,128]{1,0:T(8,128)(2,1)S(1)}, u32[]{:S(2)}, u32[]{:S(2)}) collective-permute-start(bf16[2560,128]{1,0:T(8,128)(2,1)} %get-tuple-element.46), channel_id=1, source_target_pairs={{0,1},{1,0},{2,3},{3,2},{4,5},{5,4},{6,7},{7,6},{8,9},{9,8},{10,11... | collective-permute-start | bytes 1966088 | tf_op jit(solution)/shard_map/ppermute | solution.py:290
  163.1 8.7 %copy-start.2 = (bf16[16,160,128]{2,1,0:T(8,128)(2,1)}, bf16[16,160,128]{2,1,0:T(8,128)(2,1)S(1)}, u32[]{:S(2)}) copy-start(bf16[16,160,128]{2,1,0:T(8,128)(2,1)S(1)} %all-to-all-done.2) | copy-start | bytes 1966084
  163.1 22.6 %all-to-all-start.1 = ((bf16[16,160,128]{2,1,0:T(8,128)(2,1)}), bf16[16,160,128]{2,1,0:T(8,128)(2,1)S(1)}, u32[]{:S(2)}, u32[]{:S(2)}) async-start(bf16[16,160,128]{2,1,0:T(8,128)(2,1)} %bitcast.17), calls=%async_computation.1 | async-start | bytes 1310720 | tf_op jit(solution)/shard_map/all_to_all | solution.py:313
  180.3 9.2 %copy-start.13 = (f32[2,2,16,2048]{3,2,1,0:T(8,128)S(1)}, f32[2,2,16,2048]{3,2,1,0:T(8,128)}, u32[]{:S(2)}) copy-start(f32[2,2,16,2048]{3,2,1,0:T(8,128)} %get-tuple-element.53) | copy-start | bytes 1572868
  181.3 8.2 %collective-permute-start.13 = (bf16[2,16,2048]{2,1,0:T(8,128)(2,1)S(1)}, bf16[2,16,2048]{2,1,0:T(8,128)(2,1)S(1)}, u32[]{:S(2)}, u32[]{:S(2)}) collective-permute-start(bf16[2,16,2048]{2,1,0:T(8,128)(2,1)S(1)} %get-tuple-element.68), channel_id=1, source_target_pairs={{0,1},{1,2},{2,3},{3,4},{4,5},{5,6},{6,7},{7,8},{8,9},{9,10},{10,1... | collective-permute-start | bytes 393224 | tf_op jit(solution)/shard_map/ppermute | solution.py:297
  183.6 14.1 %collective-permute-start.14 = (bf16[2,16,2048]{2,1,0:T(8,128)(2,1)S(1)}, bf16[2,16,2048]{2,1,0:T(8,128)(2,1)S(1)}, u32[]{:S(2)}, u32[]{:S(2)}) collective-permute-start(bf16[2,16,2048]{2,1,0:T(8,128)(2,1)S(1)} %get-tuple-element.67), channel_id=1, source_target_pairs={{1,0},{2,1},{3,2},{4,3},{5,4},{6,5},{7,6},{8,7},{9,8},{10,9},{11,1... | collective-permute-start | bytes 393224 | tf_op jit(solution)/shard_map/ppermute | solution.py:298
  185.7 0.9 copy-start.1
Sparse Core Ops, SparseCore 0:
  10.1 61.0 all-gather.3
  88.8 26.4 all-gather.5

commit v3 on v2

--- a/solution.py
+++ b/solution.py
@@ -136,18 +136,11 @@
         sent[d] = low
 
 
-def rows_kernel(got, out, scratch):
-    half = out.shape[0] // 2
+def rows_kernel(got, out):
+    half, feat = out.shape[0] // 2, out.shape[1]
     for kind in range(2):
-        for j in range(got.shape[0]):
-            start = kind * TRAVEL_ROWS
-            scratch[j * TRAVEL_ROWS : (j + 1) * TRAVEL_ROWS, :] = got[
-                j, start : start + TRAVEL_ROWS, :
-            ].astype(F32)
-        for c in range(16):
-            out[kind * half : (kind + 1) * half, c * LANES : (c + 1) * LANES] = from_travel(
-                scratch, half, c
-            ).astype(BF)
+        rows = got[:, kind * TRAVEL_ROWS : (kind + 1) * TRAVEL_ROWS, :]
+        out[kind * half : (kind + 1) * half, :] = rows.reshape(half, 16, LANES).reshape(half, feat)
 
 
 def gelu_parts(pre_act):
@@ -156,22 +149,17 @@
     return (pre_act * gauss_cdf, slope)
 
 
-def send_halves(lhs, rhs_of, outs, scratches):
+def send_halves(lhs, rhs_of, outs, scratch):
     half = lhs.shape[0] // 2
     for c in range(0, 16, 2):
-        part = rhs_of(lhs, c)
-        for i, scratch in enumerate(scratches):
-            for k in range(2):
-                scratch[pl.ds(c + k, half, stride=16), :] = part[
-                    i * half : (i + 1) * half, k * LANES : (k + 1) * LANES
-                ]
-    for out, scratch in zip(outs, scratches):
-        out[...] = scratch[...].astype(BF)
+        scratch[:, c * LANES : (c + 2) * LANES] = rhs_of(lhs, c).astype(BF)
+    for i, out in enumerate(outs):
+        out[...] = scratch[i * half : (i + 1) * half, :].reshape(out.shape)
 
 
 def expert_back_kernel(place, rows_own, rows_other, *refs):
-    pieces, refs = refs[:-9], refs[-9:]
-    own, other, gelu, up, down, sc_own, sc_other, rows_in, rows_grad = refs
+    pieces, refs = refs[:-8], refs[-8:]
+    own, other, gelu, up, down, scratch, rows_in, rows_grad = refs
     assemble(place, pieces, up, down)
     half = rows_own.shape[0] // 2
     for i, ref in enumerate((rows_own, rows_other)):
@@ -185,16 +173,16 @@
         grad_act,
         lambda lhs, c: mm(lhs, up[c * LANES : (c + 2) * LANES, :], NT),
         (own, other),
-        (sc_own, sc_other),
-    )
-
-
-def expert_out_kernel(gelu, down, own, other, sc_own, sc_other):
+        scratch,
+    )
+
+
+def expert_out_kernel(gelu, down, own, other, scratch):
     send_halves(
         gelu[...],
         lambda lhs, c: mm(lhs, down[:, c * LANES : (c + 2) * LANES]),
         (own, other),
-        (sc_own, sc_other),
+        scratch,
     )
 
 
@@ -243,7 +231,7 @@
 
 def attend_back_kernel(
     routes, back, cot, hidden, dec, probs, keys, values, halo_lo, halo_hi,
-    grad_in, grad_k, grad_v, edge, send, k_all, v_all, scratch, grad_h,
+    grad_in, grad_k, grad_v, edge, send_lo, send_hi, k_all, v_all, scratch, grad_h,
 ):
     tokens = dec.shape[0]
     span = tokens + 2 * HALO
@@ -281,8 +269,8 @@
             ref[:, cols] = grad[HALO : HALO + tokens, :].astype(BF)
             edge[i, 0, :, cols] = grad[HALO : 2 * HALO, :]
             edge[i, 1, :, cols] = grad[tokens : HALO + tokens, :]
-            send[0, i, :, cols] = grad[0:HALO, :].astype(BF)
-            send[1, i, :, cols] = grad[HALO + tokens : span, :].astype(BF)
+            send_lo[i, :, cols] = grad[0:HALO, :].astype(BF)
+            send_hi[i, :, cols] = grad[HALO + tokens : span, :].astype(BF)
 
 
 def shift(value, axis, step):
@@ -331,17 +319,12 @@
 
 def slot_rows(got):
     count = got.shape[0] * SLOT_LIMIT
-    return call(
-        rows_kernel,
-        [shaped((2 * count, 16 * LANES), BF)],
-        (got,),
-        scratch=[pltpu.VMEM((count * 16, LANES), F32)],
-    )[0]
+    return call(rows_kernel, [shaped((2 * count, 16 * LANES), BF)], (got,))[0]
 
 
 def send_back(own, other):
-    total = own.astype(F32) + shift(other, "core", 1).astype(F32)
-    return exchange(total.astype(BF).reshape(16, TRAVEL_ROWS, LANES)).reshape(4, -1, LANES)
+    total = own + shift(other, "core", 1)
+    return exchange(total.reshape(16, TRAVEL_ROWS, LANES)).reshape(4, -1, LANES)
 
 
 def shards(
@@ -396,7 +379,7 @@
     pieces = (packed, *own_sides, *own_opposite, two, *two_sides, *two_opposite, last_x)
 
     rows, units = own_rows.shape[0], 4 * LANES
-    half = (rows // 2 * 16, LANES)
+    half = (rows // 2, 16, LANES)
     back_own, back_other, gelu, up_full, down_full = call(
         expert_back_kernel,
         [
@@ -408,8 +391,7 @@
         ],
         (place, own_rows, other_rows, *pieces),
         scratch=[
-            pltpu.VMEM(half, F32),
-            pltpu.VMEM(half, F32),
+            pltpu.VMEM((rows, feat), BF),
             pltpu.VMEM((rows, feat), BF),
             pltpu.VMEM((rows, feat), BF),
         ],
@@ -420,18 +402,19 @@
         expert_out_kernel,
         [shaped(half, BF), shaped(half, BF)],
         (gelu, down_full),
-        scratch=[pltpu.VMEM(half, F32), pltpu.VMEM(half, F32)],
+        scratch=[pltpu.VMEM((rows, feat), BF)],
     )
     result = send_back(value_own, value_other)
 
-    grad_in, grad_k, grad_v, edge, send = call(
+    grad_in, grad_k, grad_v, edge, send_lo, send_hi = call(
         attend_back_kernel,
         [
             shaped((tokens, feat), BF),
             shaped((tokens, feat), BF),
             shaped((tokens, feat), BF),
             shaped((2, 2, HALO, feat), F32),
-            shaped((2, 2, HALO, feat), BF),
+            shaped((2, HALO, feat), BF),
+            shaped((2, HALO, feat), BF),
         ],
         (routes_t, back, cot, hidden, dec, probs, keys, values, halo_lo, halo_hi),
         scratch=[
@@ -441,7 +424,7 @@
             pltpu.VMEM((tokens, feat), F32),
         ],
     )
-    from_lo, from_hi = neighbours(send[1], send[0])
+    from_lo, from_hi = neighbours(send_hi, send_lo)
     (block_out,) = call(
         out_kernel,
         [shaped((tokens, feat), BF)],

time: 207 us -> 205 us (level)
    convert_element_type x2 -> x0, other arithmetic: 4.22 us -> none  [send_back(): total.astype(BF).reshape(16, TRAVEL_ROWS, LANES)]
    add x0 -> x2, other arithmetic: none -> 4.19 us  [send_back(): total = own + shift(other, 'core', 1)]
where the time goes in v3:
time: 205 us; the launch traced here: 203 us
  starting transfers between devices  78.6 us (38%)
  waiting for transfers between devices  62.9 us (31%)
  Pallas kernels  32.7 us (16%)
  between operations  14.5 us (7%)
  other arithmetic  8.47 us (4%)
  local copies, waits for them, and re-layouts  6.1 us (3%)
    ppermute x11, starting transfers between devices, shift(): lax.ppermute(value, axis, [(i, (i + step) % count) for i in range(count)])  33.8 us
    pallas_call x6, Pallas kernels, call(): pl.pallas_call(body, out_shape=outs, in_specs=[pl.BlockSpec(memory_space=...  32.7 us
    all_to_all x3, starting transfers between devices, exchange(): lax.all_to_all(sent, axes, split_axis=0, concat_axis=0, axis_index_groups...  29.3 us
    ppermute x11, waiting for transfers between devices, shift(): lax.ppermute(value, axis, [(i, (i + step) % count) for i in range(count)])  27.7 us
    ppermute x2, waiting for transfers between devices, neighbours(): lax.ppermute(head, axes, [(i + 1, i) for i in range(count - 1)])  16.3 us
    all_gather x1, waiting for transfers between devices, shards(): column = lax.all_gather(packed, 'zh', axis=0, tiled=True)  13.3 us
    ppermute x2, starting transfers between devices, neighbours(): lax.ppermute(tail, axes, [(i, i + 1) for i in range(count - 1)])  11.5 us
    add x2, other arithmetic, send_back(): total = own + shift(other, 'core', 1)  4.19 us
  transfers between devices with their start and end apart: 20, of which 13 were waited for; matrix products, arithmetic and copies ran while one was open for 3% of the time, Pallas kernels for 13%

profile of v3, /device:TPU:57, one launch (start us, length us, event | category | flops | bytes accessed | tf_op | source)
XLA Modules:
  0.0 203.3 jit_solution(14708326614980143002)
XLA Ops:
  7.2 0.0 all-gather.4.cloned.1.call-start
  7.2 1.0 copy.14
  8.2 0.0 copy-start.18
  8.2 0.0 copy-start.19
  8.3 1.6 pad_maximum_fusion.1.refs_0_
  9.9 0.0 all-gather.4.cloned.1.call-update
  9.9 1.0 fusion.8
  11.0 9.0 %collective-permute-start = (bf16[2,16,2048]{2,1,0:T(8,128)(2,1)S(1)}, bf16[2,16,2048]{2,1,0:T(8,128)(2,1)S(1)}, u32[]{:S(2)}, u32[]{:S(2)}) collective-permute-start(bf16[2,16,2048]{2,1,0:T(8,128)(2,1)S(1)} %pad_maximum_fusion.2), channel_id=1, source_target_pairs={{0,1},{1,2},{2,3},{3,4},{4,5},{5,6},{6,7},{7,8},{8,9},{9,10},{10,1... | collective-permute-start | bytes 393224 | tf_op jit(solution)/shard_map/ppermute | solution.py:285
  20.0 1.9 collective-permute-start.1
  22.0 2.0 collective-permute-done.halo_lo
  23.9 8.5 %collective-permute-done.1.halo_hi = bf16[2,16,2048]{2,1,0:T(8,128)(2,1)S(1)} collective-permute-done((bf16[2,16,2048]{2,1,0:T(8,128)(2,1)S(1)}, bf16[2,16,2048]{2,1,0:T(8,128)(2,1)S(1)}, u32[]{:S(2)}, u32[]{:S(2)}) %collective-permute-start.1) | collective-permute-done | bytes 131104 | tf_op jit(solution)/shard_map/ppermute | solution.py:286
  32.4 4.7 %collective-permute-start.3 = (bf16[256,512]{1,0:T(8,128)(2,1)S(1)}, bf16[256,512]{1,0:T(8,128)(2,1)S(1)}, u32[]{:S(2)}, u32[]{:S(2)}) collective-permute-start(bf16[256,512]{1,0:T(8,128)(2,1)S(1)} %copy-done.3), channel_id=1, source_target_pairs={{0,96},{32,0},{64,32},{96,64},{1,97},{33,1},{65,33},{97,65},{2,98}... | collective-permute-start | bytes 786440 | tf_op jit(solution)/shard_map/ppermute | solution.py:278
  37.1 1.9 collective-permute-start.2
  39.0 2.8 %collective-permute-done.3.refs_2_ = bf16[256,512]{1,0:T(8,128)(2,1)S(1)} collective-permute-done((bf16[256,512]{1,0:T(8,128)(2,1)S(1)}, bf16[256,512]{1,0:T(8,128)(2,1)S(1)}, u32[]{:S(2)}, u32[]{:S(2)}) %collective-permute-start.3) | collective-permute-done | bytes 262176 | tf_op jit(solution)/shard_map/ppermute | solution.py:278
  41.8 5.4 %collective-permute-start.5 = (bf16[128,512]{1,0:T(8,128)(2,1)S(1)}, bf16[128,512]{1,0:T(8,128)(2,1)S(1)}, u32[]{:S(2)}, u32[]{:S(2)}) collective-permute-start(bf16[128,512]{1,0:T(8,128)(2,1)S(1)} %slice.69), channel_id=1, source_target_pairs={{0,96},{32,0},{64,32},{96,64},{1,97},{33,1},{65,33},{97,65},{2,98}... | collective-permute-start | bytes 393224 | tf_op jit(solution)/shard_map/ppermute | solution.py:278
  47.2 0.0 collective-permute-done.2.refs_1_
  47.3 1.9 collective-permute-start.4
  49.2 0.6 add_subtract_fusion.bounds
  49.8 8.0 %shard_map.129 = (bf16[4,1280,128]{2,1,0:T(8,128)(2,1)}, f32[128,2048]{1,0:T(8,128)}, f32[16,160,128]{2,1,0:T(8,128)}) custom-call(s32[2,128]{1,0:T(2,128)} %bitcast.70, f32[2,128]{1,0:T(2,128)} %bitcast.73, s32[2,128]{1,0:T(2,128)} %add_subtract_fusion.bounds, bf16[128,2048]{1,0:T(8,128)(2,1)} %bitcast.59, bf16[128,2048]{1,0:T(8,128)(2,1)} %bitcast.61, ...), custom_call_target="tpu_custom_call" | custom-call | flops 100000000 | bytes 6032384 | tf_op jit(solution)/shard_map/pallas_call | solution.py:39
  57.8 0.0 collective-permute-done.5.refs_4_
  57.9 0.0 collective-permute-done.4.refs_3_
  57.9 13.3 %all-gather.4.cloned.1.call-done = bf16[1024,512]{1,0:T(8,128)(2,1)} async-done(((bf16[256,512]{1,0:T(8,128)(2,1)}), bf16[1024,512]{1,0:T(8,128)(2,1)}) %all-gather.4.cloned.1.call-update) | async-done | bytes 1048592 | tf_op jit(solution)/shard_map/all_gather | solution.py:343
  71.2 10.3 %all-to-all-start = ((bf16[16,320,128]{2,1,0:T(8,128)(2,1)}), bf16[16,320,128]{2,1,0:T(8,128)(2,1)S(1)}, u32[]{:S(2)}, u32[]{:S(2)}) async-start(bf16[16,320,128]{2,1,0:T(8,128)(2,1)} %bitcast.63), calls=%async_computation | async-start | bytes 2621440 | tf_op jit(solution)/shard_map/all_to_all | solution.py:301
  81.5 0.0 all-gather.6.cloned.1.call-start
  81.6 0.8 constant_dynamic-slice_fusion
  82.4 0.0 copy-start.4
  82.4 4.3 %collective-permute-start.7 = (bf16[512,512]{1,0:T(8,128)(2,1)S(1)}, bf16[512,512]{1,0:T(8,128)(2,1)S(1)}, u32[]{:S(2)}, u32[]{:S(2)}) collective-permute-start(bf16[512,512]{1,0:T(8,128)(2,1)S(1)} %pad_maximum_fusion.refs_5_), channel_id=1, source_target_pairs={{0,96},{32,0},{64,32},{96,64},{1,97},{33,1},{65,33},{97,65},{2,98}... | collective-permute-start | bytes 1572872 | tf_op jit(solution)/shard_map/ppermute | solution.py:278
  86.8 1.9 collective-permute-start.6
  88.7 0.0 all-gather.6.cloned.1.call-update
  88.7 8.2 %collective-permute-done.7.refs_7_ = bf16[512,512]{1,0:T(8,128)(2,1)S(1)} collective-permute-done((bf16[512,512]{1,0:T(8,128)(2,1)S(1)}, bf16[512,512]{1,0:T(8,128)(2,1)S(1)}, u32[]{:S(2)}, u32[]{:S(2)}) %collective-permute-start.7) | collective-permute-done | bytes 524320 | tf_op jit(solution)/shard_map/ppermute | solution.py:278
  96.9 4.9 %collective-permute-done.6.refs_6_ = bf16[512,512]{1,0:T(8,128)(2,1)S(1)} collective-permute-done((bf16[512,512]{1,0:T(8,128)(2,1)S(1)}, bf16[512,512]{1,0:T(8,128)(2,1)S(1)}, u32[]{:S(2)}, u32[]{:S(2)}) %collective-permute-start.6) | collective-permute-done | bytes 524320 | tf_op jit(solution)/shard_map/ppermute | solution.py:278
  101.9 2.0 all-to-all-done.got
  103.8 1.1 copy-done
  105.0 2.6 %shard_map.130.rows_own = bf16[320,2048]{1,0:T(8,128)(2,1)} custom-call(bf16[16,320,128]{2,1,0:T(8,128)(2,1)} %copy-done), custom_call_target="tpu_custom_call" | custom-call | flops 100000000 | bytes 2621440 | tf_op jit(solution)/shard_map/pallas_call | solution.py:39
  107.6 2.3 %collective-permute-start.8 = (bf16[320,2048]{1,0:T(8,128)(2,1)}, bf16[320,2048]{1,0:T(8,128)(2,1)S(1)}, u32[]{:S(2)}, u32[]{:S(2)}) collective-permute-start(bf16[320,2048]{1,0:T(8,128)(2,1)} %shard_map.130.rows_own), channel_id=1, source_target_pairs={{0,1},{1,0},{2,3},{3,2},{4,5},{5,4},{6,7},{7,6},{8,9},{9,8},{10,11... | collective-permute-start | bytes 3932168 | tf_op jit(solution)/shard_map/ppermute | solution.py:278
  109.9 3.9 %collective-permute-start.10 = (bf16[256,512]{1,0:T(8,128)(2,1)S(1)}, bf16[256,512]{1,0:T(8,128)(2,1)S(1)}, u32[]{:S(2)}, u32[]{:S(2)}) collective-permute-start(bf16[256,512]{1,0:T(8,128)(2,1)S(1)} %slice.71), channel_id=1, source_target_pairs={{0,96},{32,0},{64,32},{96,64},{1,97},{33,1},{65,33},{97,65},{2,98}... | collective-permute-start | bytes 786440 | tf_op jit(solution)/shard_map/ppermute | solution.py:278
  113.9 1.9 collective-permute-start.9
  115.8 0.7 pad_add_fusion.place
  116.5 4.2 %collective-permute-done.10.refs_9_ = bf16[256,512]{1,0:T(8,128)(2,1)S(1)} collective-permute-done((bf16[256,512]{1,0:T(8,128)(2,1)S(1)}, bf16[256,512]{1,0:T(8,128)(2,1)S(1)}, u32[]{:S(2)}, u32[]{:S(2)}) %collective-permute-start.10) | collective-permute-done | bytes 262176 | tf_op jit(solution)/shard_map/ppermute | solution.py:278
  120.6 3.4 %collective-permute-done.9.refs_8_ = bf16[256,512]{1,0:T(8,128)(2,1)S(1)} collective-permute-done((bf16[256,512]{1,0:T(8,128)(2,1)S(1)}, bf16[256,512]{1,0:T(8,128)(2,1)S(1)}, u32[]{:S(2)}, u32[]{:S(2)}) %collective-permute-start.9) | collective-permute-done | bytes 262176 | tf_op jit(solution)/shard_map/ppermute | solution.py:278
  124.1 0.0 collective-permute-done.8.rows_other
  124.1 0.7 copy-done.15
  124.8 0.5 copy-done.5
  125.3 7.0 %shard_map.131 = (bf16[160,16,128]{2,1,0:T(8,128)(2,1)}, bf16[160,16,128]{2,1,0:T(8,128)(2,1)}, bf16[320,512]{1,0:T(8,128)(2,1)}, bf16[2048,512]{1,0:T(8,128)(2,1)}, bf16[512,2048]{1,0:T(8,128)(2,1)}) custom-call(s32[2]{0:T(128)} %pad_add_fusion.place, bf16[320,2048]{1,0:T(8,128)(2,1)} %shard_map.130.rows_own, bf16[320,2048]{1,0:T(8,128)(2,1)} %copy-done.5, ...), custom_call_target="tpu_custom_call" | custom-call | flops 100000000 | bytes 12648456 | tf_op jit(solution)/shard_map/pallas_call | solution.py:39
  132.4 3.6 %collective-permute-start.12 = (bf16[160,16,128]{2,1,0:T(8,128)(2,1)}, bf16[160,16,128]{2,1,0:T(8,128)(2,1)S(1)}, u32[]{:S(2)}, u32[]{:S(2)}) collective-permute-start(bf16[160,16,128]{2,1,0:T(8,128)(2,1)} %get-tuple-element.50), channel_id=1, source_target_pairs={{0,1},{1,0},{2,3},{3,2},{4,5},{5,4},{6,7},{7,6},{8,9},{9,8},{10,11... | collective-permute-start | bytes 1966088 | tf_op jit(solution)/shard_map/ppermute | solution.py:278
  135.9 1.9 collective-permute-done.12
  137.8 2.1 %add.73 = bf16[160,16,128]{2,1,0:T(8,128)(2,1)} add(bf16[160,16,128]{2,1,0:T(8,128)(2,1)} %get-tuple-element.49, bf16[160,16,128]{2,1,0:T(8,128)(2,1)S(1)} %collective-permute-done.12) | non-fusion elementwise | flops 327680 | bytes 1966080 | tf_op jit(solution)/shard_map/add | solution.py:326
  139.9 10.3 %all-to-all-start.2 = ((bf16[16,160,128]{2,1,0:T(8,128)(2,1)}), bf16[16,160,128]{2,1,0:T(8,128)(2,1)S(1)}, u32[]{:S(2)}, u32[]{:S(2)}) async-start(bf16[16,160,128]{2,1,0:T(8,128)(2,1)} %bitcast.20), calls=%async_computation.2 | async-start | bytes 1310720 | tf_op jit(solution)/shard_map/all_to_all | solution.py:301
  150.2 3.6 %shard_map.132 = (bf16[160,16,128]{2,1,0:T(8,128)(2,1)}, bf16[160,16,128]{2,1,0:T(8,128)(2,1)}) custom-call(bf16[320,512]{1,0:T(8,128)(2,1)} %get-tuple-element.44.gelu, bf16[512,2048]{1,0:T(8,128)(2,1)} %get-tuple-element.45.down), custom_call_target="tpu_custom_call" | custom-call | flops 100000000 | bytes 3735552 | tf_op jit(solution)/shard_map/pallas_call | solution.py:39
  153.8 1.9 collective-permute-start.11
  155.7 2.3 %collective-permute-done.11 = bf16[160,16,128]{2,1,0:T(8,128)(2,1)S(1)} collective-permute-done((bf16[160,16,128]{2,1,0:T(8,128)(2,1)}, bf16[160,16,128]{2,1,0:T(8,128)(2,1)S(1)}, u32[]{:S(2)}, u32[]{:S(2)}) %collective-permute-start.11) | collective-permute-done | bytes 655392 | tf_op jit(solution)/shard_map/ppermute | solution.py:278
  158.0 2.1 %add.72 = bf16[160,16,128]{2,1,0:T(8,128)(2,1)} add(bf16[160,16,128]{2,1,0:T(8,128)(2,1)} %get-tuple-element.46, bf16[160,16,128]{2,1,0:T(8,128)(2,1)S(1)} %collective-permute-done.11) | non-fusion elementwise | flops 327680 | bytes 1966080 | tf_op jit(solution)/shard_map/add | solution.py:326
  160.1 1.6 all-to-all-done.2
  161.7 8.7 %all-to-all-start.1 = ((bf16[16,160,128]{2,1,0:T(8,128)(2,1)}), bf16[16,160,128]{2,1,0:T(8,128)(2,1)S(1)}, u32[]{:S(2)}, u32[]{:S(2)}) async-start(bf16[16,160,128]{2,1,0:T(8,128)(2,1)} %bitcast.17), calls=%async_computation.1 | async-start | bytes 1310720 | tf_op jit(solution)/shard_map/all_to_all | solution.py:301
  170.4 8.5 %shard_map.134 = (bf16[128,2048]{1,0:T(8,128)(2,1)}, bf16[128,2048]{1,0:T(8,128)(2,1)}, bf16[128,2048]{1,0:T(8,128)(2,1)}, f32[2,2,16,2048]{3,2,1,0:T(8,128)}, b...) custom-call(s32[2,128]{1,0:T(2,128)} %bitcast.71, bf16[4,640,128]{2,1,0:T(8,128)(2,1)} %bitcast.58, ...), custom_call_target="tpu_custom_call" | custom-call | flops 100000000 | bytes 7734272 | tf_op jit(solution)/shard_map/pallas_call | solution.py:39
  178.9 2.4 %collective-permute-start.13 = (bf16[2,16,2048]{2,1,0:T(8,128)(2,1)}, bf16[2,16,2048]{2,1,0:T(8,128)(2,1)S(1)}, u32[]{:S(2)}, u32[]{:S(2)}) collective-permute-start(bf16[2,16,2048]{2,1,0:T(8,128)(2,1)} %get-tuple-element.55), channel_id=1, source_target_pairs={{0,1},{1,2},{2,3},{3,4},{4,5},{5,6},{6,7},{7,8},{8,9},{9,10},{10,1... | collective-permute-start | bytes 393224 | tf_op jit(solution)/shard_map/ppermute | solution.py:285
  181.4 2.0 collective-permute-start.14
  183.4 0.0 all-to-all-done.1
  183.4 0.8 copy-done.1
  184.3 2.9 %shard_map.133 = bf16[128,2048]{1,0:T(8,128)(2,1)} custom-call(s32[2,128]{1,0:T(2,128)} %bitcast.72, f32[2,128]{1,0:T(2,128)} %bitcast.74, bf16[4,640,128]{2,1,0:T(8,128)(2,1)} %bitcast.57, f32[128,2048]{1,0:T(8,128)} %get-tuple-element.48.hidden), custom_call_target="tpu_custom_call" | custom-call | flops 100000000 | bytes 2230272 | tf_op jit(solution)/shard_map/pallas_call | solution.py:39
  187.2 0.0 collective-permute-done.13
  187.2 0.7 fusion.6
  187.9 7.9 %collective-permute-done.14 = bf16[2,16,2048]{2,1,0:T(8,128)(2,1)S(1)} collective-permute-done((bf16[2,16,2048]{2,1,0:T(8,128)(2,1)}, bf16[2,16,2048]{2,1,0:T(8,128)(2,1)S(1)}, u32[]{:S(2)}, u32[]{:S(2)}) %collective-permute-start.14) | collective-permute-done | bytes 131104 | tf_op jit(solution)/shard_map/ppermute | solution.py:286
  195.8 0.7 fusion.7
  (42 shorter events, 0.2 us)
Async XLA Ops:
  7.2 64.0 %all-gather.4.cloned.1.call-start = ((), (), s32[]{:S(2)}) async-start(), calls=%async_computation.3 | async-start | bytes 1310720 | tf_op jit(solution)/shard_map/all_gather | solution.py:343
  8.2 41.0 %copy-start.18 = (s32[1,128]{1,0:T(1,128)S(1)}, s32[1,128]{1,0:T(1,128)}, u32[]{:S(2)}) copy-start(s32[1,128]{1,0:T(1,128)} %param.14) | copy-start | bytes 1540
  8.2 41.0 %copy-start.19 = (s32[1,128]{1,0:T(1,128)S(1)}, s32[1,128]{1,0:T(1,128)}, u32[]{:S(2)}) copy-start(s32[1,128]{1,0:T(1,128)} %param.13) | copy-start | bytes 1540
  9.9 22.5 %copy-start.3 = (bf16[256,512]{1,0:T(8,128)(2,1)S(1)}, bf16[256,512]{1,0:T(8,128)(2,1)}, u32[]{:S(2)}) copy-start(bf16[256,512]{1,0:T(8,128)(2,1)} %pad_maximum_fusion.1.refs_0_) | copy-start | bytes 786436
  11.0 13.0 %collective-permute-start = (bf16[2,16,2048]{2,1,0:T(8,128)(2,1)S(1)}, bf16[2,16,2048]{2,1,0:T(8,128)(2,1)S(1)}, u32[]{:S(2)}, u32[]{:S(2)}) collective-permute-start(bf16[2,16,2048]{2,1,0:T(8,128)(2,1)S(1)} %pad_maximum_fusion.2), channel_id=1, source_target_pairs={{0,1},{1,2},{2,3},{3,4},{4,5},{5,6},{6,7},{7,8},{8,9},{9,10},{10,1... | collective-permute-start | bytes 393224 | tf_op jit(solution)/shard_map/ppermute | solution.py:285
  20.0 12.4 %collective-permute-start.1 = (bf16[2,16,2048]{2,1,0:T(8,128)(2,1)S(1)}, bf16[2,16,2048]{2,1,0:T(8,128)(2,1)S(1)}, u32[]{:S(2)}, u32[]{:S(2)}) collective-permute-start(bf16[2,16,2048]{2,1,0:T(8,128)(2,1)S(1)} %pad_maximum_fusion.3), channel_id=1, source_target_pairs={{1,0},{2,1},{3,2},{4,3},{5,4},{6,5},{7,6},{8,7},{9,8},{10,9},{11,1... | collective-permute-start | bytes 393224 | tf_op jit(solution)/shard_map/ppermute | solution.py:286
  23.9 25.9 %copy-start.11 = (bf16[2,16,2048]{2,1,0:T(8,128)(2,1)}, bf16[2,16,2048]{2,1,0:T(8,128)(2,1)S(1)}, u32[]{:S(2)}) copy-start(bf16[2,16,2048]{2,1,0:T(8,128)(2,1)S(1)} %collective-permute-done.halo_lo) | copy-start | bytes 393220
  32.4 17.4 %copy-start.12 = (bf16[2,16,2048]{2,1,0:T(8,128)(2,1)}, bf16[2,16,2048]{2,1,0:T(8,128)(2,1)S(1)}, u32[]{:S(2)}) copy-start(bf16[2,16,2048]{2,1,0:T(8,128)(2,1)S(1)} %collective-permute-done.1.halo_hi) | copy-start | bytes 393220
  32.4 9.4 %collective-permute-start.3 = (bf16[256,512]{1,0:T(8,128)(2,1)S(1)}, bf16[256,512]{1,0:T(8,128)(2,1)S(1)}, u32[]{:S(2)}, u32[]{:S(2)}) collective-permute-start(bf16[256,512]{1,0:T(8,128)(2,1)S(1)} %copy-done.3), channel_id=1, source_target_pairs={{0,96},{32,0},{64,32},{96,64},{1,97},{33,1},{65,33},{97,65},{2,98}... | collective-permute-start | bytes 786440 | tf_op jit(solution)/shard_map/ppermute | solution.py:278
  37.1 10.2 %collective-permute-start.2 = (bf16[256,512]{1,0:T(8,128)(2,1)S(1)}, bf16[256,512]{1,0:T(8,128)(2,1)S(1)}, u32[]{:S(2)}, u32[]{:S(2)}) collective-permute-start(bf16[256,512]{1,0:T(8,128)(2,1)S(1)} %copy-done.3), channel_id=1, source_target_pairs={{0,32},{32,64},{64,96},{96,0},{1,33},{33,65},{65,97},{97,1},{2,34}... | collective-permute-start | bytes 786440 | tf_op jit(solution)/shard_map/ppermute | solution.py:278
  41.8 16.1 %copy-start.8 = (bf16[256,512]{1,0:T(8,128)(2,1)}, bf16[256,512]{1,0:T(8,128)(2,1)S(1)}, u32[]{:S(2)}) copy-start(bf16[256,512]{1,0:T(8,128)(2,1)S(1)} %collective-permute-done.3.refs_2_) | copy-start | bytes 786436
  41.8 16.1 %collective-permute-start.5 = (bf16[128,512]{1,0:T(8,128)(2,1)S(1)}, bf16[128,512]{1,0:T(8,128)(2,1)S(1)}, u32[]{:S(2)}, u32[]{:S(2)}) collective-permute-start(bf16[128,512]{1,0:T(8,128)(2,1)S(1)} %slice.69), channel_id=1, source_target_pairs={{0,96},{32,0},{64,32},{96,64},{1,97},{33,1},{65,33},{97,65},{2,98}... | collective-permute-start | bytes 393224 | tf_op jit(solution)/shard_map/ppermute | solution.py:278
  47.2 10.6 %copy-start.9 = (bf16[256,512]{1,0:T(8,128)(2,1)}, bf16[256,512]{1,0:T(8,128)(2,1)S(1)}, u32[]{:S(2)}) copy-start(bf16[256,512]{1,0:T(8,128)(2,1)S(1)} %collective-permute-done.2.refs_1_) | copy-start | bytes 786436
  47.3 10.6 %collective-permute-start.4 = (bf16[128,512]{1,0:T(8,128)(2,1)S(1)}, bf16[128,512]{1,0:T(8,128)(2,1)S(1)}, u32[]{:S(2)}, u32[]{:S(2)}) collective-permute-start(bf16[128,512]{1,0:T(8,128)(2,1)S(1)} %slice.68), channel_id=1, source_target_pairs={{0,32},{32,64},{64,96},{96,0},{1,33},{33,65},{65,97},{97,1},{2,34}... | collective-permute-start | bytes 393224 | tf_op jit(solution)/shard_map/ppermute | solution.py:278
  57.9 13.3 %copy-start.16 = (bf16[128,512]{1,0:T(8,128)(2,1)}, bf16[128,512]{1,0:T(8,128)(2,1)S(1)}, u32[]{:S(2)}) copy-start(bf16[128,512]{1,0:T(8,128)(2,1)S(1)} %collective-permute-done.5.refs_4_) | copy-start | bytes 393220
  57.9 13.3 %copy-start.17 = (bf16[128,512]{1,0:T(8,128)(2,1)}, bf16[128,512]{1,0:T(8,128)(2,1)S(1)}, u32[]{:S(2)}) copy-start(bf16[128,512]{1,0:T(8,128)(2,1)S(1)} %collective-permute-done.4.refs_3_) | copy-start | bytes 393220
  71.2 10.4 %copy-start.10 = (bf16[1024,512]{1,0:T(8,128)(2,1)S(1)}, bf16[1024,512]{1,0:T(8,128)(2,1)}, u32[]{:S(2)}) copy-start(bf16[1024,512]{1,0:T(8,128)(2,1)} %all-gather.4.cloned.1.call-done) | copy-start | bytes 3145732
  71.2 32.6 %all-to-all-start = ((bf16[16,320,128]{2,1,0:T(8,128)(2,1)}), bf16[16,320,128]{2,1,0:T(8,128)(2,1)S(1)}, u32[]{:S(2)}, u32[]{:S(2)}) async-start(bf16[16,320,128]{2,1,0:T(8,128)(2,1)} %bitcast.63), calls=%async_computation | async-start | bytes 2621440 | tf_op jit(solution)/shard_map/all_to_all | solution.py:301
  81.5 42.5 %all-gather.6.cloned.1.call-start = ((), (), s32[]{:S(2)}) async-start(), calls=%async_computation.4 | async-start | bytes 1310720 | tf_op jit(solution)/shard_map/all_gather | solution.py:373
  82.4 41.7 %copy-start.4 = (bf16[512,512]{1,0:T(8,128)(2,1)}, bf16[512,512]{1,0:T(8,128)(2,1)S(1)}, u32[]{:S(2)}) copy-start(bf16[512,512]{1,0:T(8,128)(2,1)S(1)} %pad_maximum_fusion.refs_5_) | copy-start | bytes 1572868
  82.4 14.5 %collective-permute-start.7 = (bf16[512,512]{1,0:T(8,128)(2,1)S(1)}, bf16[512,512]{1,0:T(8,128)(2,1)S(1)}, u32[]{:S(2)}, u32[]{:S(2)}) collective-permute-start(bf16[512,512]{1,0:T(8,128)(2,1)S(1)} %pad_maximum_fusion.refs_5_), channel_id=1, source_target_pairs={{0,96},{32,0},{64,32},{96,64},{1,97},{33,1},{65,33},{97,65},{2,98}... | collective-permute-start | bytes 1572872 | tf_op jit(solution)/shard_map/ppermute | solution.py:278
  86.8 15.1 %collective-permute-start.6 = (bf16[512,512]{1,0:T(8,128)(2,1)S(1)}, bf16[512,512]{1,0:T(8,128)(2,1)S(1)}, u32[]{:S(2)}, u32[]{:S(2)}) collective-permute-start(bf16[512,512]{1,0:T(8,128)(2,1)S(1)} %pad_maximum_fusion.refs_5_), channel_id=1, source_target_pairs={{0,32},{32,64},{64,96},{96,0},{1,33},{33,65},{65,97},{97,1},{2,34}... | collective-permute-start | bytes 1572872 | tf_op jit(solution)/shard_map/ppermute | solution.py:278
  96.9 27.2 %copy-start.6 = (bf16[512,512]{1,0:T(8,128)(2,1)}, bf16[512,512]{1,0:T(8,128)(2,1)S(1)}, u32[]{:S(2)}) copy-start(bf16[512,512]{1,0:T(8,128)(2,1)S(1)} %collective-permute-done.7.refs_7_) | copy-start | bytes 1572868
  101.9 22.3 %copy-start.7 = (bf16[512,512]{1,0:T(8,128)(2,1)}, bf16[512,512]{1,0:T(8,128)(2,1)S(1)}, u32[]{:S(2)}) copy-start(bf16[512,512]{1,0:T(8,128)(2,1)S(1)} %collective-permute-done.6.refs_6_) | copy-start | bytes 1572868
  103.8 1.1 copy-start
  107.6 16.5 %collective-permute-start.8 = (bf16[320,2048]{1,0:T(8,128)(2,1)}, bf16[320,2048]{1,0:T(8,128)(2,1)S(1)}, u32[]{:S(2)}, u32[]{:S(2)}) collective-permute-start(bf16[320,2048]{1,0:T(8,128)(2,1)} %shard_map.130.rows_own), channel_id=1, source_target_pairs={{0,1},{1,0},{2,3},{3,2},{4,5},{5,4},{6,7},{7,6},{8,9},{9,8},{10,11... | collective-permute-start | bytes 3932168 | tf_op jit(solution)/shard_map/ppermute | solution.py:278
  109.9 10.7 %collective-permute-start.10 = (bf16[256,512]{1,0:T(8,128)(2,1)S(1)}, bf16[256,512]{1,0:T(8,128)(2,1)S(1)}, u32[]{:S(2)}, u32[]{:S(2)}) collective-permute-start(bf16[256,512]{1,0:T(8,128)(2,1)S(1)} %slice.71), channel_id=1, source_target_pairs={{0,96},{32,0},{64,32},{96,64},{1,97},{33,1},{65,33},{97,65},{2,98}... | collective-permute-start | bytes 786440 | tf_op jit(solution)/shard_map/ppermute | solution.py:278
  113.9 10.2 %collective-permute-start.9 = (bf16[256,512]{1,0:T(8,128)(2,1)S(1)}, bf16[256,512]{1,0:T(8,128)(2,1)S(1)}, u32[]{:S(2)}, u32[]{:S(2)}) collective-permute-start(bf16[256,512]{1,0:T(8,128)(2,1)S(1)} %slice.70), channel_id=1, source_target_pairs={{0,32},{32,64},{64,96},{96,0},{1,33},{33,65},{65,97},{97,1},{2,34}... | collective-permute-start | bytes 786440 | tf_op jit(solution)/shard_map/ppermute | solution.py:278
  120.6 3.5 %copy-start.14 = (bf16[256,512]{1,0:T(8,128)(2,1)}, bf16[256,512]{1,0:T(8,128)(2,1)S(1)}, u32[]{:S(2)}) copy-start(bf16[256,512]{1,0:T(8,128)(2,1)S(1)} %collective-permute-done.10.refs_9_) | copy-start | bytes 786436
  124.1 0.7 copy-start.15
  124.1 1.3 copy-start.5
  132.4 5.5 %collective-permute-start.12 = (bf16[160,16,128]{2,1,0:T(8,128)(2,1)}, bf16[160,16,128]{2,1,0:T(8,128)(2,1)S(1)}, u32[]{:S(2)}, u32[]{:S(2)}) collective-permute-start(bf16[160,16,128]{2,1,0:T(8,128)(2,1)} %get-tuple-element.50), channel_id=1, source_target_pairs={{0,1},{1,0},{2,3},{3,2},{4,5},{5,4},{6,7},{7,6},{8,9},{9,8},{10,11... | collective-permute-start | bytes 1966088 | tf_op jit(solution)/shard_map/ppermute | solution.py:278
  139.9 21.8 %all-to-all-start.2 = ((bf16[16,160,128]{2,1,0:T(8,128)(2,1)}), bf16[16,160,128]{2,1,0:T(8,128)(2,1)S(1)}, u32[]{:S(2)}, u32[]{:S(2)}) async-start(bf16[16,160,128]{2,1,0:T(8,128)(2,1)} %bitcast.20), calls=%async_computation.2 | async-start | bytes 1310720 | tf_op jit(solution)/shard_map/all_to_all | solution.py:301
  153.8 4.2 %collective-permute-start.11 = (bf16[160,16,128]{2,1,0:T(8,128)(2,1)}, bf16[160,16,128]{2,1,0:T(8,128)(2,1)S(1)}, u32[]{:S(2)}, u32[]{:S(2)}) collective-permute-start(bf16[160,16,128]{2,1,0:T(8,128)(2,1)} %get-tuple-element.47), channel_id=1, source_target_pairs={{0,1},{1,0},{2,3},{3,2},{4,5},{5,4},{6,7},{7,6},{8,9},{9,8},{10,11... | collective-permute-start | bytes 1966088 | tf_op jit(solution)/shard_map/ppermute | solution.py:278
  161.7 8.7 %copy-start.2 = (bf16[16,160,128]{2,1,0:T(8,128)(2,1)}, bf16[16,160,128]{2,1,0:T(8,128)(2,1)S(1)}, u32[]{:S(2)}) copy-start(bf16[16,160,128]{2,1,0:T(8,128)(2,1)S(1)} %all-to-all-done.2) | copy-start | bytes 1966084
  161.7 21.7 %all-to-all-start.1 = ((bf16[16,160,128]{2,1,0:T(8,128)(2,1)}), bf16[16,160,128]{2,1,0:T(8,128)(2,1)S(1)}, u32[]{:S(2)}, u32[]{:S(2)}) async-start(bf16[16,160,128]{2,1,0:T(8,128)(2,1)} %bitcast.17), calls=%async_computation.1 | async-start | bytes 1310720 | tf_op jit(solution)/shard_map/all_to_all | solution.py:301
  178.9 8.3 %copy-start.13 = (f32[2,2,16,2048]{3,2,1,0:T(8,128)S(1)}, f32[2,2,16,2048]{3,2,1,0:T(8,128)}, u32[]{:S(2)}) copy-start(f32[2,2,16,2048]{3,2,1,0:T(8,128)} %get-tuple-element.54) | copy-start | bytes 1572868
  178.9 8.3 %collective-permute-start.13 = (bf16[2,16,2048]{2,1,0:T(8,128)(2,1)}, bf16[2,16,2048]{2,1,0:T(8,128)(2,1)S(1)}, u32[]{:S(2)}, u32[]{:S(2)}) collective-permute-start(bf16[2,16,2048]{2,1,0:T(8,128)(2,1)} %get-tuple-element.55), channel_id=1, source_target_pairs={{0,1},{1,2},{2,3},{3,4},{4,5},{5,6},{6,7},{7,8},{8,9},{9,10},{10,1... | collective-permute-start | bytes 393224 | tf_op jit(solution)/shard_map/ppermute | solution.py:285
  181.4 14.4 %collective-permute-start.14 = (bf16[2,16,2048]{2,1,0:T(8,128)(2,1)}, bf16[2,16,2048]{2,1,0:T(8,128)(2,1)S(1)}, u32[]{:S(2)}, u32[]{:S(2)}) collective-permute-start(bf16[2,16,2048]{2,1,0:T(8,128)(2,1)} %get-tuple-element.56), channel_id=1, source_target_pairs={{1,0},{2,1},{3,2},{4,3},{5,4},{6,5},{7,6},{8,7},{9,8},{10,9},{11,1... | collective-permute-start | bytes 393224 | tf_op jit(solution)/shard_map/ppermute | solution.py:286
  183.4 0.9 copy-start.1
Sparse Core Ops, SparseCore 0:
  10.1 61.0 all-gather.3
  88.8 26.4 all-gather.5

commit v4 on v3

--- a/solution.py
+++ b/solution.py
@@ -187,32 +187,22 @@
 
 
 def assemble(place, pieces, up, down):
+    column, before, after, low, high = pieces
     x, zh = place[0], place[1]
 
-    def put(part, block, x, zh):
+    def put(block, x, zh):
         start = pl.multiple_of(((x & 3) * 4 + (zh & 3)) * LANES, LANES)
-        if part == 0:
-            up[pl.ds(start, LANES), :] = block[...]
-        else:
-            for q in range(4):
-                cols = slice(q * LANES, (q + 1) * LANES)
-                down[cols, pl.ds(start, LANES)] = block[:, cols]
-
-    def put_ring(refs, first_zh):
-        own, before, after, low, high = refs
-        count = own.shape[0] // LANES
-        for i in range(count):
-            rows = pl.ds(i * LANES, LANES)
-            for ref, step in ((own, 0), (before, 3), (after, 1)):
-                put(i % 2, ref.at[rows], x + step, first_zh + i // 2)
-            far, j = (low, i) if 2 * i < count else (high, i - count // 2)
-            put(i % 2, far.at[pl.ds(j * LANES, LANES)], x + 2, first_zh + i // 2)
-
-    put_ring(pieces[0:5], zh)
-    put_ring(pieces[5:10], zh + 1)
-    for i in range(4):
-        for part in range(2):
-            put(part, pieces[10].at[i, pl.ds(part * LANES, LANES)], i, zh + 3)
+        up[pl.ds(start, LANES), :] = block[0:LANES, :]
+        for q in range(4):
+            cols = slice(q * LANES, (q + 1) * LANES)
+            down[cols, pl.ds(start, LANES)] = block[LANES : 2 * LANES, cols]
+
+    for i, step_z in enumerate((0, 3, 1, 2)):
+        rows = pl.ds(2 * LANES * i, 2 * LANES)
+        for ref, step_x in ((column, 0), (before, 3), (after, 1)):
+            put(ref.at[rows], x + step_x, zh + step_z)
+        far = (low, high)[i // 2]
+        put(far.at[pl.ds(2 * LANES * (i % 2), 2 * LANES)], x + 2, zh + step_z)
 
 
 def slot_sum(back, scratch):
@@ -308,13 +298,13 @@
     return jnp.concatenate([up_local, turned], axis=0)
 
 
-def ring_sides(block):
-    return shift(block, "x", 1), shift(block, "x", -1)
-
-
-def ring_opposite(before, after):
+def ring_sides(block, axis):
+    return shift(block, axis, 1), shift(block, axis, -1)
+
+
+def ring_opposite(before, after, axis):
     half = before.shape[0] // 2
-    return shift(before[:half], "x", 1), shift(after[half:], "x", -1)
+    return shift(before[:half], axis, 1), shift(after[half:], axis, -1)
 
 
 def slot_rows(got):
@@ -340,14 +330,13 @@
     gates_t = gate_probs[0].T
 
     packed = pack_weights(w_up[0], w_down[0])
-    column = lax.all_gather(packed, "zh", axis=0, tiled=True)
+    sides_z = ring_sides(packed, "zh")
+    far = ring_opposite(*sides_z, "zh")
     halo_lo, halo_hi = neighbours(
         jnp.stack([keys[tokens - HALO :], values[tokens - HALO :]]),
         jnp.stack([keys[:HALO], values[:HALO]]),
     )
-    for_x, halo_lo, halo_hi = lax.optimization_barrier((packed, halo_lo, halo_hi))
-    own_sides = ring_sides(for_x)
-    own_opposite = ring_opposite(*own_sides)
+    dec, sides_z = lax.optimization_barrier((dec, sides_z))
 
     travel = (4, 2 * EXPERTS * TRAVEL_ROWS, LANES)
     sent, hidden, probs = call(
@@ -360,23 +349,14 @@
             pltpu.VMEM(travel[1:], F32),
         ],
     )
-    sent, column, own_sides, own_opposite = lax.optimization_barrier(
-        (sent, column, own_sides, own_opposite)
-    )
+    sent, far = lax.optimization_barrier((sent, far))
     got = exchange(sent.reshape(16, 2 * TRAVEL_ROWS, LANES))
-    block = packed.shape[0]
-    nexts = [
-        lax.dynamic_slice_in_dim(column, (place[1] + step) % 4 * block, block, 0)
-        for step in range(1, 4)
-    ]
-    two, last = jnp.concatenate(nexts[:2], axis=0), nexts[2]
-    last_x = lax.all_gather(last, "x", axis=0)
-    two_sides = ring_sides(two)
-    two_opposite = ring_opposite(*two_sides)
-    got, two_sides = lax.optimization_barrier((got, two_sides))
+    column = jnp.concatenate([packed, *sides_z, *far], axis=0)
+    sides_x = ring_sides(column, "x")
+    got, sides_x = lax.optimization_barrier((got, sides_x))
     own_rows = slot_rows(got)
     other_rows = shift(own_rows, "core", 1)
-    pieces = (packed, *own_sides, *own_opposite, two, *two_sides, *two_opposite, last_x)
+    pieces = (column, *sides_x, *ring_opposite(*sides_x, "x"))
 
     rows, units = own_rows.shape[0], 4 * LANES
     half = (rows // 2, 16, LANES)

time: 205 us -> 202 us (0.985)
  the two profiles are of different devices: /device:TPU:57 before, /device:TPU:89 now
where the time goes in v4:
time: 202 us; the launch traced here: 201 us
  starting transfers between devices  88.9 us (44%)
  waiting for transfers between devices  63.6 us (31%)
  Pallas kernels  32.7 us (16%)
  other arithmetic  7.74 us (4%)
  local copies, waits for them, and re-layouts  6.77 us (3%)
    ppermute x11, waiting for transfers between devices, shift(): lax.ppermute(value, axis, [(i, (i + step) % count) for i in range(count)])  50.8 us
    ppermute x11, starting transfers between devices, shift(): lax.ppermute(value, axis, [(i, (i + step) % count) for i in range(count)])  49.6 us
    pallas_call x6, Pallas kernels, call(): pl.pallas_call(body, out_shape=outs, in_specs=[pl.BlockSpec(memory_space=...  32.7 us
    all_to_all x3, starting transfers between devices, exchange(): lax.all_to_all(sent, axes, split_axis=0, concat_axis=0, axis_index_groups...  23.8 us
    ppermute x2, starting transfers between devices, neighbours(): lax.ppermute(tail, axes, [(i, i + 1) for i in range(count - 1)])  11.6 us
    ppermute x2, waiting for transfers between devices, neighbours(): lax.ppermute(head, axes, [(i + 1, i) for i in range(count - 1)])  11.1 us
    unnamed x36, local copies, waits for them, and re-layouts  4.69 us
    add x2, other arithmetic, send_back(): total = own + shift(other, 'core', 1)  4.2 us
  transfers between devices with their start and end apart: 18, of which 12 were waited for; matrix products, arithmetic and copies ran while one was open for 3% of the time, Pallas kernels for 11%

profile of v4, /device:TPU:89, one launch (start us, length us, event | category | flops | bytes accessed | tf_op | source)
XLA Modules:
  0.0 200.6 jit_solution(3181031483032109800)
XLA Ops:
  0.6 0.0 copy-start.13
  0.6 0.0 copy-start.14
  0.7 1.0 copy.14
  1.7 0.9 pad_maximum_fusion
  2.6 10.7 %collective-permute-start.1 = (bf16[256,512]{1,0:T(8,128)(2,1)S(1)}, bf16[256,512]{1,0:T(8,128)(2,1)S(1)}, u32[]{:S(2)}, u32[]{:S(2)}) collective-permute-start(bf16[256,512]{1,0:T(8,128)(2,1)S(1)} %pad_maximum_fusion), channel_id=1, source_target_pairs={{0,24},{8,0},{16,8},{24,16},{1,25},{9,1},{17,9},{25,17},{2,26},{10... | collective-permute-start | bytes 786440 | tf_op jit(solution)/shard_map/ppermute | solution.py:268
  13.3 1.9 collective-permute-start
  15.2 1.0 fusion.8
  16.2 6.2 %collective-permute-start.2 = (bf16[2,16,2048]{2,1,0:T(8,128)(2,1)S(1)}, bf16[2,16,2048]{2,1,0:T(8,128)(2,1)S(1)}, u32[]{:S(2)}, u32[]{:S(2)}) collective-permute-start(bf16[2,16,2048]{2,1,0:T(8,128)(2,1)S(1)} %pad_maximum_fusion.1), channel_id=1, source_target_pairs={{0,1},{1,2},{2,3},{3,4},{4,5},{5,6},{6,7},{7,8},{8,9},{9,10},{10,1... | collective-permute-start | bytes 393224 | tf_op jit(solution)/shard_map/ppermute | solution.py:275
  22.4 1.9 collective-permute-start.3
  24.4 4.1 %collective-permute-done.1 = bf16[256,512]{1,0:T(8,128)(2,1)S(1)} collective-permute-done((bf16[256,512]{1,0:T(8,128)(2,1)S(1)}, bf16[256,512]{1,0:T(8,128)(2,1)S(1)}, u32[]{:S(2)}, u32[]{:S(2)}) %collective-permute-start.1) | collective-permute-done | bytes 262176 | tf_op jit(solution)/shard_map/ppermute | solution.py:268
  28.5 12.6 %collective-permute-start.5 = (bf16[128,512]{1,0:T(8,128)(2,1)S(1)}, bf16[128,512]{1,0:T(8,128)(2,1)S(1)}, u32[]{:S(2)}, u32[]{:S(2)}) collective-permute-start(bf16[128,512]{1,0:T(8,128)(2,1)S(1)} %slice.69), channel_id=1, source_target_pairs={{0,24},{8,0},{16,8},{24,16},{1,25},{9,1},{17,9},{25,17},{2,26},{10... | collective-permute-start | bytes 393224 | tf_op jit(solution)/shard_map/ppermute | solution.py:268
  41.1 2.7 %collective-permute-done = bf16[256,512]{1,0:T(8,128)(2,1)S(1)} collective-permute-done((bf16[256,512]{1,0:T(8,128)(2,1)S(1)}, bf16[256,512]{1,0:T(8,128)(2,1)S(1)}, u32[]{:S(2)}, u32[]{:S(2)}) %collective-permute-start) | collective-permute-done | bytes 262176 | tf_op jit(solution)/shard_map/ppermute | solution.py:268
  43.8 2.0 collective-permute-start.4
  45.8 0.0 copy-done.13
  45.8 0.0 copy-done.14
  45.8 0.6 add_subtract_fusion.bounds
  46.4 0.0 collective-permute-done.2.halo_lo
  46.4 0.8 collective-permute-done.3.halo_hi
  47.2 0.0 copy-done.7
  47.3 0.7 copy-done.8
  47.9 8.0 %shard_map.129 = (bf16[4,1280,128]{2,1,0:T(8,128)(2,1)}, f32[128,2048]{1,0:T(8,128)}, f32[16,160,128]{2,1,0:T(8,128)}) custom-call(s32[2,128]{1,0:T(2,128)} %bitcast.72, f32[2,128]{1,0:T(2,128)} %bitcast.75, s32[2,128]{1,0:T(2,128)} %add_subtract_fusion.bounds, bf16[128,2048]{1,0:T(8,128)(2,1)} %bitcast.61, bf16[128,2048]{1,0:T(8,128)(2,1)} %bitcast.63, ...), custom_call_target="tpu_custom_call" | custom-call | flops 100000000 | bytes 6032384 | tf_op jit(solution)/shard_map/pallas_call | solution.py:39
  55.9 0.0 collective-permute-done.5
  55.9 4.8 %collective-permute-done.4 = bf16[128,512]{1,0:T(8,128)(2,1)S(1)} collective-permute-done((bf16[128,512]{1,0:T(8,128)(2,1)S(1)}, bf16[128,512]{1,0:T(8,128)(2,1)S(1)}, u32[]{:S(2)}, u32[]{:S(2)}) %collective-permute-start.4) | collective-permute-done | bytes 131104 | tf_op jit(solution)/shard_map/ppermute | solution.py:268
  60.8 7.7 %all-to-all-start = ((bf16[16,320,128]{2,1,0:T(8,128)(2,1)}), bf16[16,320,128]{2,1,0:T(8,128)(2,1)S(1)}, u32[]{:S(2)}, u32[]{:S(2)}) async-start(bf16[16,320,128]{2,1,0:T(8,128)(2,1)} %bitcast.65), calls=%async_computation | async-start | bytes 2621440 | tf_op jit(solution)/shard_map/all_to_all | solution.py:291
  68.6 4.4 %collective-permute-start.7 = (bf16[1024,512]{1,0:T(8,128)(2,1)S(1)}, bf16[1024,512]{1,0:T(8,128)(2,1)S(1)}, u32[]{:S(2)}, u32[]{:S(2)}) collective-permute-start(bf16[1024,512]{1,0:T(8,128)(2,1)S(1)} %constant_dynamic-update-slice_fusion.refs_0_), channel_id=1, source_target_pairs={{0,96},{32,0},{64,32},{96,64},{1,97},{33,1},{65,33},{97,65},{2,98}... | collective-permute-start | bytes 3145736 | tf_op jit(solution)/shard_map/ppermute | solution.py:268
  73.0 1.9 collective-permute-start.6
  74.9 17.6 %collective-permute-done.7.refs_2_ = bf16[1024,512]{1,0:T(8,128)(2,1)S(1)} collective-permute-done((bf16[1024,512]{1,0:T(8,128)(2,1)S(1)}, bf16[1024,512]{1,0:T(8,128)(2,1)S(1)}, u32[]{:S(2)}, u32[]{:S(2)}) %collective-permute-start.7) | collective-permute-done | bytes 1048608 | tf_op jit(solution)/shard_map/ppermute | solution.py:268
  92.5 5.0 %collective-permute-done.6.refs_1_ = bf16[1024,512]{1,0:T(8,128)(2,1)S(1)} collective-permute-done((bf16[1024,512]{1,0:T(8,128)(2,1)S(1)}, bf16[1024,512]{1,0:T(8,128)(2,1)S(1)}, u32[]{:S(2)}, u32[]{:S(2)}) %collective-permute-start.6) | collective-permute-done | bytes 1048608 | tf_op jit(solution)/shard_map/ppermute | solution.py:268
  97.6 0.0 all-to-all-done.got
  97.6 1.1 copy-done
  98.7 2.6 %shard_map.130.rows_own = bf16[320,2048]{1,0:T(8,128)(2,1)} custom-call(bf16[16,320,128]{2,1,0:T(8,128)(2,1)} %copy-done), custom_call_target="tpu_custom_call" | custom-call | flops 100000000 | bytes 2621440 | tf_op jit(solution)/shard_map/pallas_call | solution.py:39
  101.4 6.0 %collective-permute-start.8 = (bf16[320,2048]{1,0:T(8,128)(2,1)}, bf16[320,2048]{1,0:T(8,128)(2,1)S(1)}, u32[]{:S(2)}, u32[]{:S(2)}) collective-permute-start(bf16[320,2048]{1,0:T(8,128)(2,1)} %shard_map.130.rows_own), channel_id=1, source_target_pairs={{0,1},{1,0},{2,3},{3,2},{4,5},{5,4},{6,7},{7,6},{8,9},{9,8},{10,11... | collective-permute-start | bytes 3932168 | tf_op jit(solution)/shard_map/ppermute | solution.py:268
  107.4 1.9 collective-permute-start.10
  109.3 3.4 %collective-permute-start.9 = (bf16[512,512]{1,0:T(8,128)(2,1)S(1)}, bf16[512,512]{1,0:T(8,128)(2,1)S(1)}, u32[]{:S(2)}, u32[]{:S(2)}) collective-permute-start(bf16[512,512]{1,0:T(8,128)(2,1)S(1)} %slice.58), channel_id=1, source_target_pairs={{0,32},{32,64},{64,96},{96,0},{1,33},{33,65},{65,97},{97,1},{2,34}... | collective-permute-start | bytes 1572872 | tf_op jit(solution)/shard_map/ppermute | solution.py:268
  112.7 0.7 pad_add_fusion.place
  113.4 9.5 %collective-permute-done.10.refs_4_ = bf16[512,512]{1,0:T(8,128)(2,1)S(1)} collective-permute-done((bf16[512,512]{1,0:T(8,128)(2,1)S(1)}, bf16[512,512]{1,0:T(8,128)(2,1)S(1)}, u32[]{:S(2)}, u32[]{:S(2)}) %collective-permute-start.10) | collective-permute-done | bytes 524320 | tf_op jit(solution)/shard_map/ppermute | solution.py:268
  122.9 3.1 %collective-permute-done.9.refs_3_ = bf16[512,512]{1,0:T(8,128)(2,1)S(1)} collective-permute-done((bf16[512,512]{1,0:T(8,128)(2,1)S(1)}, bf16[512,512]{1,0:T(8,128)(2,1)S(1)}, u32[]{:S(2)}, u32[]{:S(2)}) %collective-permute-start.9) | collective-permute-done | bytes 524320 | tf_op jit(solution)/shard_map/ppermute | solution.py:268
  126.0 0.0 collective-permute-done.8.rows_other
  126.0 0.0 copy-done.3
  126.0 0.8 copy-done.12
  126.8 1.2 copy-done.6
  128.0 7.0 %shard_map.131 = (bf16[160,16,128]{2,1,0:T(8,128)(2,1)}, bf16[160,16,128]{2,1,0:T(8,128)(2,1)}, bf16[320,512]{1,0:T(8,128)(2,1)}, bf16[2048,512]{1,0:T(8,128)(2,1)}, bf16[512,2048]{1,0:T(8,128)(2,1)}) custom-call(s32[2]{0:T(128)} %pad_add_fusion.place, bf16[320,2048]{1,0:T(8,128)(2,1)} %shard_map.130.rows_own, bf16[320,2048]{1,0:T(8,128)(2,1)} %copy-done.6, ...), custom_call_target="tpu_custom_call" | custom-call | flops 100000000 | bytes 12648456 | tf_op jit(solution)/shard_map/pallas_call | solution.py:39
  134.9 2.7 %collective-permute-start.12 = (bf16[160,16,128]{2,1,0:T(8,128)(2,1)}, bf16[160,16,128]{2,1,0:T(8,128)(2,1)S(1)}, u32[]{:S(2)}, u32[]{:S(2)}) collective-permute-start(bf16[160,16,128]{2,1,0:T(8,128)(2,1)} %get-tuple-element.44), channel_id=1, source_target_pairs={{0,1},{1,0},{2,3},{3,2},{4,5},{5,4},{6,7},{7,6},{8,9},{9,8},{10,11... | collective-permute-start | bytes 1966088 | tf_op jit(solution)/shard_map/ppermute | solution.py:268
  137.6 1.9 collective-permute-done.12
  139.6 2.1 %add.36 = bf16[160,16,128]{2,1,0:T(8,128)(2,1)} add(bf16[160,16,128]{2,1,0:T(8,128)(2,1)} %get-tuple-element.43, bf16[160,16,128]{2,1,0:T(8,128)(2,1)S(1)} %collective-permute-done.12) | non-fusion elementwise | flops 327680 | bytes 1966080 | tf_op jit(solution)/shard_map/add | solution.py:316
  141.7 7.5 %all-to-all-start.2 = ((bf16[16,160,128]{2,1,0:T(8,128)(2,1)}), bf16[16,160,128]{2,1,0:T(8,128)(2,1)S(1)}, u32[]{:S(2)}, u32[]{:S(2)}) async-start(bf16[16,160,128]{2,1,0:T(8,128)(2,1)} %bitcast.19), calls=%async_computation.2 | async-start | bytes 1310720 | tf_op jit(solution)/shard_map/all_to_all | solution.py:291
  149.2 3.6 %shard_map.132 = (bf16[160,16,128]{2,1,0:T(8,128)(2,1)}, bf16[160,16,128]{2,1,0:T(8,128)(2,1)}) custom-call(bf16[320,512]{1,0:T(8,128)(2,1)} %get-tuple-element.38.gelu, bf16[512,2048]{1,0:T(8,128)(2,1)} %get-tuple-element.39.down), custom_call_target="tpu_custom_call" | custom-call | flops 100000000 | bytes 3735552 | tf_op jit(solution)/shard_map/pallas_call | solution.py:39
  152.7 2.3 %collective-permute-start.11 = (bf16[160,16,128]{2,1,0:T(8,128)(2,1)}, bf16[160,16,128]{2,1,0:T(8,128)(2,1)S(1)}, u32[]{:S(2)}, u32[]{:S(2)}) collective-permute-start(bf16[160,16,128]{2,1,0:T(8,128)(2,1)} %get-tuple-element.41), channel_id=1, source_target_pairs={{0,1},{1,0},{2,3},{3,2},{4,5},{5,4},{6,7},{7,6},{8,9},{9,8},{10,11... | collective-permute-start | bytes 1966088 | tf_op jit(solution)/shard_map/ppermute | solution.py:268
  155.0 1.9 collective-permute-done.11
  156.9 2.1 %add.35 = bf16[160,16,128]{2,1,0:T(8,128)(2,1)} add(bf16[160,16,128]{2,1,0:T(8,128)(2,1)} %get-tuple-element.40, bf16[160,16,128]{2,1,0:T(8,128)(2,1)S(1)} %collective-permute-done.11) | non-fusion elementwise | flops 327680 | bytes 1966080 | tf_op jit(solution)/shard_map/add | solution.py:316
  159.0 1.6 all-to-all-done.2
  160.7 8.6 %all-to-all-start.1 = ((bf16[16,160,128]{2,1,0:T(8,128)(2,1)}), bf16[16,160,128]{2,1,0:T(8,128)(2,1)S(1)}, u32[]{:S(2)}, u32[]{:S(2)}) async-start(bf16[16,160,128]{2,1,0:T(8,128)(2,1)} %bitcast.16), calls=%async_computation.1 | async-start | bytes 1310720 | tf_op jit(solution)/shard_map/all_to_all | solution.py:291
  169.3 0.0 copy-done.2
  169.3 8.5 %shard_map.134 = (bf16[128,2048]{1,0:T(8,128)(2,1)}, bf16[128,2048]{1,0:T(8,128)(2,1)}, bf16[128,2048]{1,0:T(8,128)(2,1)}, f32[2,2,16,2048]{3,2,1,0:T(8,128)}, b...) custom-call(s32[2,128]{1,0:T(2,128)} %bitcast.73, bf16[4,640,128]{2,1,0:T(8,128)(2,1)} %bitcast.60, ...), custom_call_target="tpu_custom_call" | custom-call | flops 100000000 | bytes 7734272 | tf_op jit(solution)/shard_map/pallas_call | solution.py:39
  177.8 5.4 %collective-permute-start.13 = (bf16[2,16,2048]{2,1,0:T(8,128)(2,1)}, bf16[2,16,2048]{2,1,0:T(8,128)(2,1)S(1)}, u32[]{:S(2)}, u32[]{:S(2)}) collective-permute-start(bf16[2,16,2048]{2,1,0:T(8,128)(2,1)} %get-tuple-element.49), channel_id=1, source_target_pairs={{0,1},{1,2},{2,3},{3,4},{4,5},{5,6},{6,7},{7,8},{8,9},{9,10},{10,1... | collective-permute-start | bytes 393224 | tf_op jit(solution)/shard_map/ppermute | solution.py:275
  183.2 1.9 collective-permute-start.14
  185.1 0.0 all-to-all-done.1
  185.1 0.8 copy-done.1
  186.0 2.9 %shard_map.133 = bf16[128,2048]{1,0:T(8,128)(2,1)} custom-call(s32[2,128]{1,0:T(2,128)} %bitcast.74, f32[2,128]{1,0:T(2,128)} %bitcast.76, bf16[4,640,128]{2,1,0:T(8,128)(2,1)} %bitcast.59, f32[128,2048]{1,0:T(8,128)} %get-tuple-element.42.hidden), custom_call_target="tpu_custom_call" | custom-call | flops 100000000 | bytes 2230272 | tf_op jit(solution)/shard_map/pallas_call | solution.py:39
  188.9 0.0 collective-permute-done.13
  188.9 0.0 copy-done.9
  188.9 0.7 fusion.6
  189.6 10.3 %collective-permute-done.14 = bf16[2,16,2048]{2,1,0:T(8,128)(2,1)S(1)} collective-permute-done((bf16[2,16,2048]{2,1,0:T(8,128)(2,1)}, bf16[2,16,2048]{2,1,0:T(8,128)(2,1)S(1)}, u32[]{:S(2)}, u32[]{:S(2)}) %collective-permute-start.14) | collective-permute-done | bytes 131104 | tf_op jit(solution)/shard_map/ppermute | solution.py:276
  199.9 0.7 fusion.7
  (30 shorter events, 0.3 us)
Async XLA Ops:
  0.6 45.2 %copy-start.13 = (s32[1,128]{1,0:T(1,128)S(1)}, s32[1,128]{1,0:T(1,128)}, u32[]{:S(2)}) copy-start(s32[1,128]{1,0:T(1,128)} %param.14) | copy-start | bytes 1540
  0.6 45.2 %copy-start.14 = (s32[1,128]{1,0:T(1,128)S(1)}, s32[1,128]{1,0:T(1,128)}, u32[]{:S(2)}) copy-start(s32[1,128]{1,0:T(1,128)} %param.13) | copy-start | bytes 1540
  2.6 25.9 %collective-permute-start.1 = (bf16[256,512]{1,0:T(8,128)(2,1)S(1)}, bf16[256,512]{1,0:T(8,128)(2,1)S(1)}, u32[]{:S(2)}, u32[]{:S(2)}) collective-permute-start(bf16[256,512]{1,0:T(8,128)(2,1)S(1)} %pad_maximum_fusion), channel_id=1, source_target_pairs={{0,24},{8,0},{16,8},{24,16},{1,25},{9,1},{17,9},{25,17},{2,26},{10... | collective-permute-start | bytes 786440 | tf_op jit(solution)/shard_map/ppermute | solution.py:268
  13.3 30.5 %collective-permute-start = (bf16[256,512]{1,0:T(8,128)(2,1)S(1)}, bf16[256,512]{1,0:T(8,128)(2,1)S(1)}, u32[]{:S(2)}, u32[]{:S(2)}) collective-permute-start(bf16[256,512]{1,0:T(8,128)(2,1)S(1)} %pad_maximum_fusion), channel_id=1, source_target_pairs={{0,8},{8,16},{16,24},{24,0},{1,9},{9,17},{17,25},{25,1},{2,10},{10... | collective-permute-start | bytes 786440 | tf_op jit(solution)/shard_map/ppermute | solution.py:268
  16.2 30.2 %collective-permute-start.2 = (bf16[2,16,2048]{2,1,0:T(8,128)(2,1)S(1)}, bf16[2,16,2048]{2,1,0:T(8,128)(2,1)S(1)}, u32[]{:S(2)}, u32[]{:S(2)}) collective-permute-start(bf16[2,16,2048]{2,1,0:T(8,128)(2,1)S(1)} %pad_maximum_fusion.1), channel_id=1, source_target_pairs={{0,1},{1,2},{2,3},{3,4},{4,5},{5,6},{6,7},{7,8},{8,9},{9,10},{10,1... | collective-permute-start | bytes 393224 | tf_op jit(solution)/shard_map/ppermute | solution.py:275
  22.4 24.8 %collective-permute-start.3 = (bf16[2,16,2048]{2,1,0:T(8,128)(2,1)S(1)}, bf16[2,16,2048]{2,1,0:T(8,128)(2,1)S(1)}, u32[]{:S(2)}, u32[]{:S(2)}) collective-permute-start(bf16[2,16,2048]{2,1,0:T(8,128)(2,1)S(1)} %pad_maximum_fusion.2), channel_id=1, source_target_pairs={{1,0},{2,1},{3,2},{4,3},{5,4},{6,5},{7,6},{8,7},{9,8},{10,9},{11,1... | collective-permute-start | bytes 393224 | tf_op jit(solution)/shard_map/ppermute | solution.py:276
  28.5 27.4 %collective-permute-start.5 = (bf16[128,512]{1,0:T(8,128)(2,1)S(1)}, bf16[128,512]{1,0:T(8,128)(2,1)S(1)}, u32[]{:S(2)}, u32[]{:S(2)}) collective-permute-start(bf16[128,512]{1,0:T(8,128)(2,1)S(1)} %slice.69), channel_id=1, source_target_pairs={{0,24},{8,0},{16,8},{24,16},{1,25},{9,1},{17,9},{25,17},{2,26},{10... | collective-permute-start | bytes 393224 | tf_op jit(solution)/shard_map/ppermute | solution.py:268
  43.8 16.9 %collective-permute-start.4 = (bf16[128,512]{1,0:T(8,128)(2,1)S(1)}, bf16[128,512]{1,0:T(8,128)(2,1)S(1)}, u32[]{:S(2)}, u32[]{:S(2)}) collective-permute-start(bf16[128,512]{1,0:T(8,128)(2,1)S(1)} %slice.68), channel_id=1, source_target_pairs={{0,8},{8,16},{16,24},{24,0},{1,9},{9,17},{17,25},{25,1},{2,10},{10... | collective-permute-start | bytes 393224 | tf_op jit(solution)/shard_map/ppermute | solution.py:268
  46.4 0.9 copy-start.7
  47.2 0.7 copy-start.8
  60.8 7.7 %copy-start.10 = (bf16[1,128,512]{2,1,0:T(8,128)(2,1)S(1)}, bf16[1,128,512]{2,1,0:T(8,128)(2,1)}, u32[]{:S(2)}) copy-start(bf16[1,128,512]{2,1,0:T(8,128)(2,1)} %param.17) | copy-start | bytes 393220
  60.8 36.8 %all-to-all-start = ((bf16[16,320,128]{2,1,0:T(8,128)(2,1)}), bf16[16,320,128]{2,1,0:T(8,128)(2,1)S(1)}, u32[]{:S(2)}, u32[]{:S(2)}) async-start(bf16[16,320,128]{2,1,0:T(8,128)(2,1)} %bitcast.65), calls=%async_computation | async-start | bytes 2621440 | tf_op jit(solution)/shard_map/all_to_all | solution.py:291
  68.6 24.0 %copy-start.5 = (bf16[1024,512]{1,0:T(8,128)(2,1)}, bf16[1024,512]{1,0:T(8,128)(2,1)S(1)}, u32[]{:S(2)}) copy-start(bf16[1024,512]{1,0:T(8,128)(2,1)S(1)} %constant_dynamic-update-slice_fusion.refs_0_) | copy-start | bytes 3145732
  68.6 24.0 %collective-permute-start.7 = (bf16[1024,512]{1,0:T(8,128)(2,1)S(1)}, bf16[1024,512]{1,0:T(8,128)(2,1)S(1)}, u32[]{:S(2)}, u32[]{:S(2)}) collective-permute-start(bf16[1024,512]{1,0:T(8,128)(2,1)S(1)} %constant_dynamic-update-slice_fusion.refs_0_), channel_id=1, source_target_pairs={{0,96},{32,0},{64,32},{96,64},{1,97},{33,1},{65,33},{97,65},{2,98}... | collective-permute-start | bytes 3145736 | tf_op jit(solution)/shard_map/ppermute | solution.py:268
  73.0 24.6 %collective-permute-start.6 = (bf16[1024,512]{1,0:T(8,128)(2,1)S(1)}, bf16[1024,512]{1,0:T(8,128)(2,1)S(1)}, u32[]{:S(2)}, u32[]{:S(2)}) collective-permute-start(bf16[1024,512]{1,0:T(8,128)(2,1)S(1)} %constant_dynamic-update-slice_fusion.refs_0_), channel_id=1, source_target_pairs={{0,32},{32,64},{64,96},{96,0},{1,33},{33,65},{65,97},{97,1},{2,34}... | collective-permute-start | bytes 3145736 | tf_op jit(solution)/shard_map/ppermute | solution.py:268
  92.5 33.5 %copy-start.3 = (bf16[1024,512]{1,0:T(8,128)(2,1)}, bf16[1024,512]{1,0:T(8,128)(2,1)S(1)}, u32[]{:S(2)}) copy-start(bf16[1024,512]{1,0:T(8,128)(2,1)S(1)} %collective-permute-done.7.refs_2_) | copy-start | bytes 3145732
  97.6 28.4 %copy-start.4 = (bf16[1024,512]{1,0:T(8,128)(2,1)}, bf16[1024,512]{1,0:T(8,128)(2,1)S(1)}, u32[]{:S(2)}) copy-start(bf16[1024,512]{1,0:T(8,128)(2,1)S(1)} %collective-permute-done.6.refs_1_) | copy-start | bytes 3145732
  97.6 1.1 copy-start
  101.4 24.6 %collective-permute-start.8 = (bf16[320,2048]{1,0:T(8,128)(2,1)}, bf16[320,2048]{1,0:T(8,128)(2,1)S(1)}, u32[]{:S(2)}, u32[]{:S(2)}) collective-permute-start(bf16[320,2048]{1,0:T(8,128)(2,1)} %shard_map.130.rows_own), channel_id=1, source_target_pairs={{0,1},{1,0},{2,3},{3,2},{4,5},{5,4},{6,7},{7,6},{8,9},{9,8},{10,11... | collective-permute-start | bytes 3932168 | tf_op jit(solution)/shard_map/ppermute | solution.py:268
  107.4 15.4 %collective-permute-start.10 = (bf16[512,512]{1,0:T(8,128)(2,1)S(1)}, bf16[512,512]{1,0:T(8,128)(2,1)S(1)}, u32[]{:S(2)}, u32[]{:S(2)}) collective-permute-start(bf16[512,512]{1,0:T(8,128)(2,1)S(1)} %slice.59), channel_id=1, source_target_pairs={{0,96},{32,0},{64,32},{96,64},{1,97},{33,1},{65,33},{97,65},{2,98}... | collective-permute-start | bytes 1572872 | tf_op jit(solution)/shard_map/ppermute | solution.py:268
  109.3 16.6 %collective-permute-start.9 = (bf16[512,512]{1,0:T(8,128)(2,1)S(1)}, bf16[512,512]{1,0:T(8,128)(2,1)S(1)}, u32[]{:S(2)}, u32[]{:S(2)}) collective-permute-start(bf16[512,512]{1,0:T(8,128)(2,1)S(1)} %slice.58), channel_id=1, source_target_pairs={{0,32},{32,64},{64,96},{96,0},{1,33},{33,65},{65,97},{97,1},{2,34}... | collective-permute-start | bytes 1572872 | tf_op jit(solution)/shard_map/ppermute | solution.py:268
  122.9 3.2 %copy-start.11 = (bf16[512,512]{1,0:T(8,128)(2,1)}, bf16[512,512]{1,0:T(8,128)(2,1)S(1)}, u32[]{:S(2)}) copy-start(bf16[512,512]{1,0:T(8,128)(2,1)S(1)} %collective-permute-done.10.refs_4_) | copy-start | bytes 1572868
  126.0 0.8 copy-start.12
  126.8 1.2 copy-start.6
  134.9 4.6 %collective-permute-start.12 = (bf16[160,16,128]{2,1,0:T(8,128)(2,1)}, bf16[160,16,128]{2,1,0:T(8,128)(2,1)S(1)}, u32[]{:S(2)}, u32[]{:S(2)}) collective-permute-start(bf16[160,16,128]{2,1,0:T(8,128)(2,1)} %get-tuple-element.44), channel_id=1, source_target_pairs={{0,1},{1,0},{2,3},{3,2},{4,5},{5,4},{6,7},{7,6},{8,9},{9,8},{10,11... | collective-permute-start | bytes 1966088 | tf_op jit(solution)/shard_map/ppermute | solution.py:268
  141.7 19.0 %all-to-all-start.2 = ((bf16[16,160,128]{2,1,0:T(8,128)(2,1)}), bf16[16,160,128]{2,1,0:T(8,128)(2,1)S(1)}, u32[]{:S(2)}, u32[]{:S(2)}) async-start(bf16[16,160,128]{2,1,0:T(8,128)(2,1)} %bitcast.19), calls=%async_computation.2 | async-start | bytes 1310720 | tf_op jit(solution)/shard_map/all_to_all | solution.py:291
  152.7 4.2 %collective-permute-start.11 = (bf16[160,16,128]{2,1,0:T(8,128)(2,1)}, bf16[160,16,128]{2,1,0:T(8,128)(2,1)S(1)}, u32[]{:S(2)}, u32[]{:S(2)}) collective-permute-start(bf16[160,16,128]{2,1,0:T(8,128)(2,1)} %get-tuple-element.41), channel_id=1, source_target_pairs={{0,1},{1,0},{2,3},{3,2},{4,5},{5,4},{6,7},{7,6},{8,9},{9,8},{10,11... | collective-permute-start | bytes 1966088 | tf_op jit(solution)/shard_map/ppermute | solution.py:268
  160.7 8.6 %copy-start.2 = (bf16[16,160,128]{2,1,0:T(8,128)(2,1)}, bf16[16,160,128]{2,1,0:T(8,128)(2,1)S(1)}, u32[]{:S(2)}) copy-start(bf16[16,160,128]{2,1,0:T(8,128)(2,1)S(1)} %all-to-all-done.2) | copy-start | bytes 1966084
  160.7 24.5 %all-to-all-start.1 = ((bf16[16,160,128]{2,1,0:T(8,128)(2,1)}), bf16[16,160,128]{2,1,0:T(8,128)(2,1)S(1)}, u32[]{:S(2)}, u32[]{:S(2)}) async-start(bf16[16,160,128]{2,1,0:T(8,128)(2,1)} %bitcast.16), calls=%async_computation.1 | async-start | bytes 1310720 | tf_op jit(solution)/shard_map/all_to_all | solution.py:291
  177.8 11.1 %copy-start.9 = (f32[2,2,16,2048]{3,2,1,0:T(8,128)S(1)}, f32[2,2,16,2048]{3,2,1,0:T(8,128)}, u32[]{:S(2)}) copy-start(f32[2,2,16,2048]{3,2,1,0:T(8,128)} %get-tuple-element.48) | copy-start | bytes 1572868
  177.8 11.1 %collective-permute-start.13 = (bf16[2,16,2048]{2,1,0:T(8,128)(2,1)}, bf16[2,16,2048]{2,1,0:T(8,128)(2,1)S(1)}, u32[]{:S(2)}, u32[]{:S(2)}) collective-permute-start(bf16[2,16,2048]{2,1,0:T(8,128)(2,1)} %get-tuple-element.49), channel_id=1, source_target_pairs={{0,1},{1,2},{2,3},{3,4},{4,5},{5,6},{6,7},{7,8},{8,9},{9,10},{10,1... | collective-permute-start | bytes 393224 | tf_op jit(solution)/shard_map/ppermute | solution.py:275
  183.2 16.7 %collective-permute-start.14 = (bf16[2,16,2048]{2,1,0:T(8,128)(2,1)}, bf16[2,16,2048]{2,1,0:T(8,128)(2,1)S(1)}, u32[]{:S(2)}, u32[]{:S(2)}) collective-permute-start(bf16[2,16,2048]{2,1,0:T(8,128)(2,1)} %get-tuple-element.50), channel_id=1, source_target_pairs={{1,0},{2,1},{3,2},{4,3},{5,4},{6,5},{7,6},{8,7},{9,8},{10,9},{11,1... | collective-permute-start | bytes 393224 | tf_op jit(solution)/shard_map/ppermute | solution.py:276
  185.1 0.8 copy-start.1

commit v5 on v4

--- a/solution.py
+++ b/solution.py
@@ -355,8 +355,10 @@
     sides_x = ring_sides(column, "x")
     got, sides_x = lax.optimization_barrier((got, sides_x))
     own_rows = slot_rows(got)
-    other_rows = shift(own_rows, "core", 1)
-    pieces = (column, *sides_x, *ring_opposite(*sides_x, "x"))
+    opposite = ring_opposite(*sides_x, "x")
+    to_swap, opposite = lax.optimization_barrier((own_rows, opposite))
+    other_rows = shift(to_swap, "core", 1)
+    pieces = (column, *sides_x, *opposite)
 
     rows, units = own_rows.shape[0], 4 * LANES
     half = (rows // 2, 16, LANES)

time: 202 us -> 198 us (0.980)
  the two profiles are of different devices: /device:TPU:89 before, /device:TPU:57 now
where the time goes in v5:
time: 198 us; the launch traced here: 197 us
  starting transfers between devices  94.8 us (48%)
  waiting for transfers between devices  56.1 us (28%)
  Pallas kernels  32.7 us (17%)
  other arithmetic  7.74 us (4%)
  local copies, waits for them, and re-layouts  4.91 us (2%)
    ppermute x11, starting transfers between devices, shift(): lax.ppermute(value, axis, [(i, (i + step) % count) for i in range(count)])  48.9 us
    ppermute x11, waiting for transfers between devices, shift(): lax.ppermute(value, axis, [(i, (i + step) % count) for i in range(count)])  45.2 us
    pallas_call x6, Pallas kernels, call(): pl.pallas_call(body, out_shape=outs, in_specs=[pl.BlockSpec(memory_space=...  32.7 us
    all_to_all x3, starting transfers between devices, exchange(): lax.all_to_all(sent, axes, split_axis=0, concat_axis=0, axis_index_groups...  32.2 us
    ppermute x2, starting transfers between devices, neighbours(): lax.ppermute(tail, axes, [(i, i + 1) for i in range(count - 1)])  9.8 us
    ppermute x2, waiting for transfers between devices, neighbours(): lax.ppermute(head, axes, [(i + 1, i) for i in range(count - 1)])  9.32 us
    add x2, other arithmetic, send_back(): total = own + shift(other, 'core', 1)  4.2 us
  transfers between devices with their start and end apart: 18, of which 11 were waited for; matrix products, arithmetic and copies ran while one was open for 3% of the time, Pallas kernels for 13%

profile of v5, /device:TPU:57, one launch (start us, length us, event | category | flops | bytes accessed | tf_op | source)
XLA Modules:
  0.0 197.1 jit_solution(4710225462905556208)
XLA Ops:
  0.6 0.0 copy-start.13
  0.6 0.0 copy-start.14
  0.7 1.0 copy.14
  1.7 0.9 pad_maximum_fusion
  2.6 11.6 %collective-permute-start.1 = (bf16[256,512]{1,0:T(8,128)(2,1)S(1)}, bf16[256,512]{1,0:T(8,128)(2,1)S(1)}, u32[]{:S(2)}, u32[]{:S(2)}) collective-permute-start(bf16[256,512]{1,0:T(8,128)(2,1)S(1)} %pad_maximum_fusion), channel_id=1, source_target_pairs={{0,24},{8,0},{16,8},{24,16},{1,25},{9,1},{17,9},{25,17},{2,26},{10... | collective-permute-start | bytes 786440 | tf_op jit(solution)/shard_map/ppermute | solution.py:268
  14.2 1.9 collective-permute-start
  16.1 1.0 fusion.8
  17.1 5.7 %collective-permute-start.2 = (bf16[2,16,2048]{2,1,0:T(8,128)(2,1)S(1)}, bf16[2,16,2048]{2,1,0:T(8,128)(2,1)S(1)}, u32[]{:S(2)}, u32[]{:S(2)}) collective-permute-start(bf16[2,16,2048]{2,1,0:T(8,128)(2,1)S(1)} %pad_maximum_fusion.1), channel_id=1, source_target_pairs={{0,1},{1,2},{2,3},{3,4},{4,5},{5,6},{6,7},{7,8},{8,9},{9,10},{10,1... | collective-permute-start | bytes 393224 | tf_op jit(solution)/shard_map/ppermute | solution.py:275
  22.8 1.9 collective-permute-start.3
  24.7 6.0 %collective-permute-done.1 = bf16[256,512]{1,0:T(8,128)(2,1)S(1)} collective-permute-done((bf16[256,512]{1,0:T(8,128)(2,1)S(1)}, bf16[256,512]{1,0:T(8,128)(2,1)S(1)}, u32[]{:S(2)}, u32[]{:S(2)}) %collective-permute-start.1) | collective-permute-done | bytes 262176 | tf_op jit(solution)/shard_map/ppermute | solution.py:268
  30.8 12.5 %collective-permute-start.5 = (bf16[128,512]{1,0:T(8,128)(2,1)S(1)}, bf16[128,512]{1,0:T(8,128)(2,1)S(1)}, u32[]{:S(2)}, u32[]{:S(2)}) collective-permute-start(bf16[128,512]{1,0:T(8,128)(2,1)S(1)} %slice.69), channel_id=1, source_target_pairs={{0,24},{8,0},{16,8},{24,16},{1,25},{9,1},{17,9},{25,17},{2,26},{10... | collective-permute-start | bytes 393224 | tf_op jit(solution)/shard_map/ppermute | solution.py:268
  43.3 0.0 collective-permute-done
  43.3 1.9 collective-permute-start.4
  45.2 0.0 copy-done.13
  45.2 0.0 copy-done.14
  45.2 0.6 add_subtract_fusion.bounds
  45.8 0.0 collective-permute-done.2.halo_lo
  45.8 0.0 collective-permute-done.3.halo_hi
  45.8 0.0 copy-start.8
  45.8 0.6 copy-done.7
  46.5 0.0 copy-done.8
  46.5 8.0 %shard_map.129 = (bf16[4,1280,128]{2,1,0:T(8,128)(2,1)}, f32[128,2048]{1,0:T(8,128)}, f32[16,160,128]{2,1,0:T(8,128)}) custom-call(s32[2,128]{1,0:T(2,128)} %bitcast.72, f32[2,128]{1,0:T(2,128)} %bitcast.75, s32[2,128]{1,0:T(2,128)} %add_subtract_fusion.bounds, bf16[128,2048]{1,0:T(8,128)(2,1)} %bitcast.61, bf16[128,2048]{1,0:T(8,128)(2,1)} %bitcast.63, ...), custom_call_target="tpu_custom_call" | custom-call | flops 100000000 | bytes 6032384 | tf_op jit(solution)/shard_map/pallas_call | solution.py:39
  54.5 0.0 collective-permute-done.5
  54.5 0.3 collective-permute-done.4
  54.8 15.7 %all-to-all-start = ((bf16[16,320,128]{2,1,0:T(8,128)(2,1)}), bf16[16,320,128]{2,1,0:T(8,128)(2,1)S(1)}, u32[]{:S(2)}, u32[]{:S(2)}) async-start(bf16[16,320,128]{2,1,0:T(8,128)(2,1)} %bitcast.65), calls=%async_computation | async-start | bytes 2621440 | tf_op jit(solution)/shard_map/all_to_all | solution.py:291
  70.5 0.0 copy-done.10
  70.7 0.0 copy-start.5
  70.7 4.5 %collective-permute-start.7 = (bf16[1024,512]{1,0:T(8,128)(2,1)S(1)}, bf16[1024,512]{1,0:T(8,128)(2,1)S(1)}, u32[]{:S(2)}, u32[]{:S(2)}) collective-permute-start(bf16[1024,512]{1,0:T(8,128)(2,1)S(1)} %constant_dynamic-update-slice_fusion.refs_0_), channel_id=1, source_target_pairs={{0,96},{32,0},{64,32},{96,64},{1,97},{33,1},{65,33},{97,65},{2,98}... | collective-permute-start | bytes 3145736 | tf_op jit(solution)/shard_map/ppermute | solution.py:268
  75.1 1.9 collective-permute-start.6
  77.1 19.4 %collective-permute-done.7.refs_2_ = bf16[1024,512]{1,0:T(8,128)(2,1)S(1)} collective-permute-done((bf16[1024,512]{1,0:T(8,128)(2,1)S(1)}, bf16[1024,512]{1,0:T(8,128)(2,1)S(1)}, u32[]{:S(2)}, u32[]{:S(2)}) %collective-permute-start.7) | collective-permute-done | bytes 1048608 | tf_op jit(solution)/shard_map/ppermute | solution.py:268
  96.4 5.0 %collective-permute-done.6.refs_1_ = bf16[1024,512]{1,0:T(8,128)(2,1)S(1)} collective-permute-done((bf16[1024,512]{1,0:T(8,128)(2,1)S(1)}, bf16[1024,512]{1,0:T(8,128)(2,1)S(1)}, u32[]{:S(2)}, u32[]{:S(2)}) %collective-permute-start.6) | collective-permute-done | bytes 1048608 | tf_op jit(solution)/shard_map/ppermute | solution.py:268
  101.5 0.0 all-to-all-done.got
  101.5 1.9 collective-permute-start.9
  103.5 3.4 %collective-permute-start.8 = (bf16[512,512]{1,0:T(8,128)(2,1)S(1)}, bf16[512,512]{1,0:T(8,128)(2,1)S(1)}, u32[]{:S(2)}, u32[]{:S(2)}) collective-permute-start(bf16[512,512]{1,0:T(8,128)(2,1)S(1)} %slice.58), channel_id=1, source_target_pairs={{0,32},{32,64},{64,96},{96,0},{1,33},{33,65},{65,97},{97,1},{2,34}... | collective-permute-start | bytes 1572872 | tf_op jit(solution)/shard_map/ppermute | solution.py:268
  106.8 0.0 copy-done
  106.9 2.6 %shard_map.130.rows_own = bf16[320,2048]{1,0:T(8,128)(2,1)} custom-call(bf16[16,320,128]{2,1,0:T(8,128)(2,1)} %copy-done), custom_call_target="tpu_custom_call" | custom-call | flops 100000000 | bytes 2621440 | tf_op jit(solution)/shard_map/pallas_call | solution.py:39
  109.5 5.0 %collective-permute-done.9.refs_4_ = bf16[512,512]{1,0:T(8,128)(2,1)S(1)} collective-permute-done((bf16[512,512]{1,0:T(8,128)(2,1)S(1)}, bf16[512,512]{1,0:T(8,128)(2,1)S(1)}, u32[]{:S(2)}, u32[]{:S(2)}) %collective-permute-start.9) | collective-permute-done | bytes 524320 | tf_op jit(solution)/shard_map/ppermute | solution.py:268
  114.5 3.1 %collective-permute-done.8.refs_3_ = bf16[512,512]{1,0:T(8,128)(2,1)S(1)} collective-permute-done((bf16[512,512]{1,0:T(8,128)(2,1)S(1)}, bf16[512,512]{1,0:T(8,128)(2,1)S(1)}, u32[]{:S(2)}, u32[]{:S(2)}) %collective-permute-start.8) | collective-permute-done | bytes 524320 | tf_op jit(solution)/shard_map/ppermute | solution.py:268
  117.7 5.2 %collective-permute-start.10 = (bf16[320,2048]{1,0:T(8,128)(2,1)}, bf16[320,2048]{1,0:T(8,128)(2,1)S(1)}, u32[]{:S(2)}, u32[]{:S(2)}) collective-permute-start(bf16[320,2048]{1,0:T(8,128)(2,1)} %shard_map.130.rows_own), channel_id=1, source_target_pairs={{0,1},{1,0},{2,3},{3,2},{4,5},{5,4},{6,7},{7,6},{8,9},{9,8},{10,11... | collective-permute-start | bytes 3932168 | tf_op jit(solution)/shard_map/ppermute | solution.py:268
  122.8 0.7 pad_add_fusion.place
  123.5 2.2 %collective-permute-done.10.rows_other = bf16[320,2048]{1,0:T(8,128)(2,1)S(1)} collective-permute-done((bf16[320,2048]{1,0:T(8,128)(2,1)}, bf16[320,2048]{1,0:T(8,128)(2,1)S(1)}, u32[]{:S(2)}, u32[]{:S(2)}) %collective-permute-start.10) | collective-permute-done | bytes 1310752 | tf_op jit(solution)/shard_map/ppermute | solution.py:268
  125.7 0.0 copy-done.4
  125.7 1.2 copy-done.6
  126.9 7.0 %shard_map.131 = (bf16[160,16,128]{2,1,0:T(8,128)(2,1)}, bf16[160,16,128]{2,1,0:T(8,128)(2,1)}, bf16[320,512]{1,0:T(8,128)(2,1)}, bf16[2048,512]{1,0:T(8,128)(2,1)}, bf16[512,2048]{1,0:T(8,128)(2,1)}) custom-call(s32[2]{0:T(128)} %pad_add_fusion.place, bf16[320,2048]{1,0:T(8,128)(2,1)} %shard_map.130.rows_own, bf16[320,2048]{1,0:T(8,128)(2,1)} %copy-done.6, ...), custom_call_target="tpu_custom_call" | custom-call | flops 100000000 | bytes 12648456 | tf_op jit(solution)/shard_map/pallas_call | solution.py:39
  133.8 2.3 %collective-permute-start.12 = (bf16[160,16,128]{2,1,0:T(8,128)(2,1)}, bf16[160,16,128]{2,1,0:T(8,128)(2,1)S(1)}, u32[]{:S(2)}, u32[]{:S(2)}) collective-permute-start(bf16[160,16,128]{2,1,0:T(8,128)(2,1)} %get-tuple-element.50), channel_id=1, source_target_pairs={{0,1},{1,0},{2,3},{3,2},{4,5},{5,4},{6,7},{7,6},{8,9},{9,8},{10,11... | collective-permute-start | bytes 1966088 | tf_op jit(solution)/shard_map/ppermute | solution.py:268
  136.1 1.9 collective-permute-done.12
  138.1 2.1 %add.36 = bf16[160,16,128]{2,1,0:T(8,128)(2,1)} add(bf16[160,16,128]{2,1,0:T(8,128)(2,1)} %get-tuple-element.49, bf16[160,16,128]{2,1,0:T(8,128)(2,1)S(1)} %collective-permute-done.12) | non-fusion elementwise | flops 327680 | bytes 1966080 | tf_op jit(solution)/shard_map/add | solution.py:316
  140.2 8.2 %all-to-all-start.2 = ((bf16[16,160,128]{2,1,0:T(8,128)(2,1)}), bf16[16,160,128]{2,1,0:T(8,128)(2,1)S(1)}, u32[]{:S(2)}, u32[]{:S(2)}) async-start(bf16[16,160,128]{2,1,0:T(8,128)(2,1)} %bitcast.19), calls=%async_computation.2 | async-start | bytes 1310720 | tf_op jit(solution)/shard_map/all_to_all | solution.py:291
  148.3 3.6 %shard_map.132 = (bf16[160,16,128]{2,1,0:T(8,128)(2,1)}, bf16[160,16,128]{2,1,0:T(8,128)(2,1)}) custom-call(bf16[320,512]{1,0:T(8,128)(2,1)} %get-tuple-element.44.gelu, bf16[512,2048]{1,0:T(8,128)(2,1)} %get-tuple-element.45.down), custom_call_target="tpu_custom_call" | custom-call | flops 100000000 | bytes 3735552 | tf_op jit(solution)/shard_map/pallas_call | solution.py:39
  151.9 1.9 collective-permute-start.11
  153.8 2.3 %collective-permute-done.11 = bf16[160,16,128]{2,1,0:T(8,128)(2,1)S(1)} collective-permute-done((bf16[160,16,128]{2,1,0:T(8,128)(2,1)}, bf16[160,16,128]{2,1,0:T(8,128)(2,1)S(1)}, u32[]{:S(2)}, u32[]{:S(2)}) %collective-permute-start.11) | collective-permute-done | bytes 655392 | tf_op jit(solution)/shard_map/ppermute | solution.py:268
  156.1 2.1 %add.35 = bf16[160,16,128]{2,1,0:T(8,128)(2,1)} add(bf16[160,16,128]{2,1,0:T(8,128)(2,1)} %get-tuple-element.46, bf16[160,16,128]{2,1,0:T(8,128)(2,1)S(1)} %collective-permute-done.11) | non-fusion elementwise | flops 327680 | bytes 1966080 | tf_op jit(solution)/shard_map/add | solution.py:316
  158.2 1.5 all-to-all-done.2
  159.7 8.3 %all-to-all-start.1 = ((bf16[16,160,128]{2,1,0:T(8,128)(2,1)}), bf16[16,160,128]{2,1,0:T(8,128)(2,1)S(1)}, u32[]{:S(2)}, u32[]{:S(2)}) async-start(bf16[16,160,128]{2,1,0:T(8,128)(2,1)} %bitcast.16), calls=%async_computation.1 | async-start | bytes 1310720 | tf_op jit(solution)/shard_map/all_to_all | solution.py:291
  168.1 8.5 %shard_map.134 = (bf16[128,2048]{1,0:T(8,128)(2,1)}, bf16[128,2048]{1,0:T(8,128)(2,1)}, bf16[128,2048]{1,0:T(8,128)(2,1)}, f32[2,2,16,2048]{3,2,1,0:T(8,128)}, b...) custom-call(s32[2,128]{1,0:T(2,128)} %bitcast.73, bf16[4,640,128]{2,1,0:T(8,128)(2,1)} %bitcast.60, ...), custom_call_target="tpu_custom_call" | custom-call | flops 100000000 | bytes 7734272 | tf_op jit(solution)/shard_map/pallas_call | solution.py:39
  176.6 4.1 %collective-permute-start.13 = (bf16[2,16,2048]{2,1,0:T(8,128)(2,1)}, bf16[2,16,2048]{2,1,0:T(8,128)(2,1)S(1)}, u32[]{:S(2)}, u32[]{:S(2)}) collective-permute-start(bf16[2,16,2048]{2,1,0:T(8,128)(2,1)} %get-tuple-element.55), channel_id=1, source_target_pairs={{0,1},{1,2},{2,3},{3,4},{4,5},{5,6},{6,7},{7,8},{8,9},{9,10},{10,1... | collective-permute-start | bytes 393224 | tf_op jit(solution)/shard_map/ppermute | solution.py:275
  180.7 1.9 collective-permute-start.14
  182.7 0.0 all-to-all-done.1
  182.7 0.8 copy-done.1
  183.5 2.9 %shard_map.133 = bf16[128,2048]{1,0:T(8,128)(2,1)} custom-call(s32[2,128]{1,0:T(2,128)} %bitcast.74, f32[2,128]{1,0:T(2,128)} %bitcast.76, bf16[4,640,128]{2,1,0:T(8,128)(2,1)} %bitcast.59, f32[128,2048]{1,0:T(8,128)} %get-tuple-element.48.hidden), custom_call_target="tpu_custom_call" | custom-call | flops 100000000 | bytes 2230272 | tf_op jit(solution)/shard_map/pallas_call | solution.py:39
  186.4 0.0 collective-permute-done.13
  186.5 0.7 fusion.6
  187.1 9.3 %collective-permute-done.14 = bf16[2,16,2048]{2,1,0:T(8,128)(2,1)S(1)} collective-permute-done((bf16[2,16,2048]{2,1,0:T(8,128)(2,1)}, bf16[2,16,2048]{2,1,0:T(8,128)(2,1)S(1)}, u32[]{:S(2)}, u32[]{:S(2)}) %collective-permute-start.14) | collective-permute-done | bytes 131104 | tf_op jit(solution)/shard_map/ppermute | solution.py:276
  196.4 0.7 fusion.7
  (30 shorter events, 0.3 us)
Async XLA Ops:
  0.6 44.6 %copy-start.13 = (s32[1,128]{1,0:T(1,128)S(1)}, s32[1,128]{1,0:T(1,128)}, u32[]{:S(2)}) copy-start(s32[1,128]{1,0:T(1,128)} %param.14) | copy-start | bytes 1540
  0.6 44.6 %copy-start.14 = (s32[1,128]{1,0:T(1,128)S(1)}, s32[1,128]{1,0:T(1,128)}, u32[]{:S(2)}) copy-start(s32[1,128]{1,0:T(1,128)} %param.13) | copy-start | bytes 1540
  2.6 28.1 %collective-permute-start.1 = (bf16[256,512]{1,0:T(8,128)(2,1)S(1)}, bf16[256,512]{1,0:T(8,128)(2,1)S(1)}, u32[]{:S(2)}, u32[]{:S(2)}) collective-permute-start(bf16[256,512]{1,0:T(8,128)(2,1)S(1)} %pad_maximum_fusion), channel_id=1, source_target_pairs={{0,24},{8,0},{16,8},{24,16},{1,25},{9,1},{17,9},{25,17},{2,26},{10... | collective-permute-start | bytes 786440 | tf_op jit(solution)/shard_map/ppermute | solution.py:268
  14.2 29.1 %collective-permute-start = (bf16[256,512]{1,0:T(8,128)(2,1)S(1)}, bf16[256,512]{1,0:T(8,128)(2,1)S(1)}, u32[]{:S(2)}, u32[]{:S(2)}) collective-permute-start(bf16[256,512]{1,0:T(8,128)(2,1)S(1)} %pad_maximum_fusion), channel_id=1, source_target_pairs={{0,8},{8,16},{16,24},{24,0},{1,9},{9,17},{17,25},{25,1},{2,10},{10... | collective-permute-start | bytes 786440 | tf_op jit(solution)/shard_map/ppermute | solution.py:268
  17.1 28.7 %collective-permute-start.2 = (bf16[2,16,2048]{2,1,0:T(8,128)(2,1)S(1)}, bf16[2,16,2048]{2,1,0:T(8,128)(2,1)S(1)}, u32[]{:S(2)}, u32[]{:S(2)}) collective-permute-start(bf16[2,16,2048]{2,1,0:T(8,128)(2,1)S(1)} %pad_maximum_fusion.1), channel_id=1, source_target_pairs={{0,1},{1,2},{2,3},{3,4},{4,5},{5,6},{6,7},{7,8},{8,9},{9,10},{10,1... | collective-permute-start | bytes 393224 | tf_op jit(solution)/shard_map/ppermute | solution.py:275
  22.8 23.0 %collective-permute-start.3 = (bf16[2,16,2048]{2,1,0:T(8,128)(2,1)S(1)}, bf16[2,16,2048]{2,1,0:T(8,128)(2,1)S(1)}, u32[]{:S(2)}, u32[]{:S(2)}) collective-permute-start(bf16[2,16,2048]{2,1,0:T(8,128)(2,1)S(1)} %pad_maximum_fusion.2), channel_id=1, source_target_pairs={{1,0},{2,1},{3,2},{4,3},{5,4},{6,5},{7,6},{8,7},{9,8},{10,9},{11,1... | collective-permute-start | bytes 393224 | tf_op jit(solution)/shard_map/ppermute | solution.py:276
  30.8 23.8 %collective-permute-start.5 = (bf16[128,512]{1,0:T(8,128)(2,1)S(1)}, bf16[128,512]{1,0:T(8,128)(2,1)S(1)}, u32[]{:S(2)}, u32[]{:S(2)}) collective-permute-start(bf16[128,512]{1,0:T(8,128)(2,1)S(1)} %slice.69), channel_id=1, source_target_pairs={{0,24},{8,0},{16,8},{24,16},{1,25},{9,1},{17,9},{25,17},{2,26},{10... | collective-permute-start | bytes 393224 | tf_op jit(solution)/shard_map/ppermute | solution.py:268
  43.3 11.5 %collective-permute-start.4 = (bf16[128,512]{1,0:T(8,128)(2,1)S(1)}, bf16[128,512]{1,0:T(8,128)(2,1)S(1)}, u32[]{:S(2)}, u32[]{:S(2)}) collective-permute-start(bf16[128,512]{1,0:T(8,128)(2,1)S(1)} %slice.68), channel_id=1, source_target_pairs={{0,8},{8,16},{16,24},{24,0},{1,9},{9,17},{17,25},{25,1},{2,10},{10... | collective-permute-start | bytes 393224 | tf_op jit(solution)/shard_map/ppermute | solution.py:268
  45.8 0.7 copy-start.7
  45.8 0.7 copy-start.8
  54.8 15.7 %copy-start.10 = (bf16[1,128,512]{2,1,0:T(8,128)(2,1)S(1)}, bf16[1,128,512]{2,1,0:T(8,128)(2,1)}, u32[]{:S(2)}) copy-start(bf16[1,128,512]{2,1,0:T(8,128)(2,1)} %param.17) | copy-start | bytes 393220
  54.8 46.7 %all-to-all-start = ((bf16[16,320,128]{2,1,0:T(8,128)(2,1)}), bf16[16,320,128]{2,1,0:T(8,128)(2,1)S(1)}, u32[]{:S(2)}, u32[]{:S(2)}) async-start(bf16[16,320,128]{2,1,0:T(8,128)(2,1)} %bitcast.65), calls=%async_computation | async-start | bytes 2621440 | tf_op jit(solution)/shard_map/all_to_all | solution.py:291
  70.7 25.8 %copy-start.5 = (bf16[1024,512]{1,0:T(8,128)(2,1)}, bf16[1024,512]{1,0:T(8,128)(2,1)S(1)}, u32[]{:S(2)}) copy-start(bf16[1024,512]{1,0:T(8,128)(2,1)S(1)} %constant_dynamic-update-slice_fusion.refs_0_) | copy-start | bytes 3145732
  70.7 25.7 %collective-permute-start.7 = (bf16[1024,512]{1,0:T(8,128)(2,1)S(1)}, bf16[1024,512]{1,0:T(8,128)(2,1)S(1)}, u32[]{:S(2)}, u32[]{:S(2)}) collective-permute-start(bf16[1024,512]{1,0:T(8,128)(2,1)S(1)} %constant_dynamic-update-slice_fusion.refs_0_), channel_id=1, source_target_pairs={{0,96},{32,0},{64,32},{96,64},{1,97},{33,1},{65,33},{97,65},{2,98}... | collective-permute-start | bytes 3145736 | tf_op jit(solution)/shard_map/ppermute | solution.py:268
  75.1 26.3 %collective-permute-start.6 = (bf16[1024,512]{1,0:T(8,128)(2,1)S(1)}, bf16[1024,512]{1,0:T(8,128)(2,1)S(1)}, u32[]{:S(2)}, u32[]{:S(2)}) collective-permute-start(bf16[1024,512]{1,0:T(8,128)(2,1)S(1)} %constant_dynamic-update-slice_fusion.refs_0_), channel_id=1, source_target_pairs={{0,32},{32,64},{64,96},{96,0},{1,33},{33,65},{65,97},{97,1},{2,34}... | collective-permute-start | bytes 3145736 | tf_op jit(solution)/shard_map/ppermute | solution.py:268
  96.4 29.3 %copy-start.3 = (bf16[1024,512]{1,0:T(8,128)(2,1)}, bf16[1024,512]{1,0:T(8,128)(2,1)S(1)}, u32[]{:S(2)}) copy-start(bf16[1024,512]{1,0:T(8,128)(2,1)S(1)} %collective-permute-done.7.refs_2_) | copy-start | bytes 3145732
  101.5 24.2 %copy-start.4 = (bf16[1024,512]{1,0:T(8,128)(2,1)}, bf16[1024,512]{1,0:T(8,128)(2,1)S(1)}, u32[]{:S(2)}) copy-start(bf16[1024,512]{1,0:T(8,128)(2,1)S(1)} %collective-permute-done.6.refs_1_) | copy-start | bytes 3145732
  101.5 5.4 %copy-start = (bf16[16,320,128]{2,1,0:T(8,128)(2,1)}, bf16[16,320,128]{2,1,0:T(8,128)(2,1)S(1)}, u32[]{:S(2)}) copy-start(bf16[16,320,128]{2,1,0:T(8,128)(2,1)S(1)} %all-to-all-done.got) | copy-start | bytes 3932164
  101.5 13.0 %collective-permute-start.9 = (bf16[512,512]{1,0:T(8,128)(2,1)S(1)}, bf16[512,512]{1,0:T(8,128)(2,1)S(1)}, u32[]{:S(2)}, u32[]{:S(2)}) collective-permute-start(bf16[512,512]{1,0:T(8,128)(2,1)S(1)} %slice.59), channel_id=1, source_target_pairs={{0,96},{32,0},{64,32},{96,64},{1,97},{33,1},{65,33},{97,65},{2,98}... | collective-permute-start | bytes 1572872 | tf_op jit(solution)/shard_map/ppermute | solution.py:268
  103.5 14.2 %collective-permute-start.8 = (bf16[512,512]{1,0:T(8,128)(2,1)S(1)}, bf16[512,512]{1,0:T(8,128)(2,1)S(1)}, u32[]{:S(2)}, u32[]{:S(2)}) collective-permute-start(bf16[512,512]{1,0:T(8,128)(2,1)S(1)} %slice.58), channel_id=1, source_target_pairs={{0,32},{32,64},{64,96},{96,0},{1,33},{33,65},{65,97},{97,1},{2,34}... | collective-permute-start | bytes 1572872 | tf_op jit(solution)/shard_map/ppermute | solution.py:268
  114.5 11.2 %copy-start.11 = (bf16[512,512]{1,0:T(8,128)(2,1)}, bf16[512,512]{1,0:T(8,128)(2,1)S(1)}, u32[]{:S(2)}) copy-start(bf16[512,512]{1,0:T(8,128)(2,1)S(1)} %collective-permute-done.9.refs_4_) | copy-start | bytes 1572868
  117.7 8.0 %copy-start.12 = (bf16[512,512]{1,0:T(8,128)(2,1)}, bf16[512,512]{1,0:T(8,128)(2,1)S(1)}, u32[]{:S(2)}) copy-start(bf16[512,512]{1,0:T(8,128)(2,1)S(1)} %collective-permute-done.8.refs_3_) | copy-start | bytes 1572868
  117.7 8.0 %collective-permute-start.10 = (bf16[320,2048]{1,0:T(8,128)(2,1)}, bf16[320,2048]{1,0:T(8,128)(2,1)S(1)}, u32[]{:S(2)}, u32[]{:S(2)}) collective-permute-start(bf16[320,2048]{1,0:T(8,128)(2,1)} %shard_map.130.rows_own), channel_id=1, source_target_pairs={{0,1},{1,0},{2,3},{3,2},{4,5},{5,4},{6,7},{7,6},{8,9},{9,8},{10,11... | collective-permute-start | bytes 3932168 | tf_op jit(solution)/shard_map/ppermute | solution.py:268
  125.7 1.2 copy-start.6
  133.8 4.2 %collective-permute-start.12 = (bf16[160,16,128]{2,1,0:T(8,128)(2,1)}, bf16[160,16,128]{2,1,0:T(8,128)(2,1)S(1)}, u32[]{:S(2)}, u32[]{:S(2)}) collective-permute-start(bf16[160,16,128]{2,1,0:T(8,128)(2,1)} %get-tuple-element.50), channel_id=1, source_target_pairs={{0,1},{1,0},{2,3},{3,2},{4,5},{5,4},{6,7},{7,6},{8,9},{9,8},{10,11... | collective-permute-start | bytes 1966088 | tf_op jit(solution)/shard_map/ppermute | solution.py:268
  140.2 19.6 %all-to-all-start.2 = ((bf16[16,160,128]{2,1,0:T(8,128)(2,1)}), bf16[16,160,128]{2,1,0:T(8,128)(2,1)S(1)}, u32[]{:S(2)}, u32[]{:S(2)}) async-start(bf16[16,160,128]{2,1,0:T(8,128)(2,1)} %bitcast.19), calls=%async_computation.2 | async-start | bytes 1310720 | tf_op jit(solution)/shard_map/all_to_all | solution.py:291
  151.9 4.2 %collective-permute-start.11 = (bf16[160,16,128]{2,1,0:T(8,128)(2,1)}, bf16[160,16,128]{2,1,0:T(8,128)(2,1)S(1)}, u32[]{:S(2)}, u32[]{:S(2)}) collective-permute-start(bf16[160,16,128]{2,1,0:T(8,128)(2,1)} %get-tuple-element.47), channel_id=1, source_target_pairs={{0,1},{1,0},{2,3},{3,2},{4,5},{5,4},{6,7},{7,6},{8,9},{9,8},{10,11... | collective-permute-start | bytes 1966088 | tf_op jit(solution)/shard_map/ppermute | solution.py:268
  159.7 8.3 %copy-start.2 = (bf16[16,160,128]{2,1,0:T(8,128)(2,1)}, bf16[16,160,128]{2,1,0:T(8,128)(2,1)S(1)}, u32[]{:S(2)}) copy-start(bf16[16,160,128]{2,1,0:T(8,128)(2,1)S(1)} %all-to-all-done.2) | copy-start | bytes 1966084
  159.7 22.9 %all-to-all-start.1 = ((bf16[16,160,128]{2,1,0:T(8,128)(2,1)}), bf16[16,160,128]{2,1,0:T(8,128)(2,1)S(1)}, u32[]{:S(2)}, u32[]{:S(2)}) async-start(bf16[16,160,128]{2,1,0:T(8,128)(2,1)} %bitcast.16), calls=%async_computation.1 | async-start | bytes 1310720 | tf_op jit(solution)/shard_map/all_to_all | solution.py:291
  176.6 9.9 %copy-start.9 = (f32[2,2,16,2048]{3,2,1,0:T(8,128)S(1)}, f32[2,2,16,2048]{3,2,1,0:T(8,128)}, u32[]{:S(2)}) copy-start(f32[2,2,16,2048]{3,2,1,0:T(8,128)} %get-tuple-element.54) | copy-start | bytes 1572868
  176.6 9.8 %collective-permute-start.13 = (bf16[2,16,2048]{2,1,0:T(8,128)(2,1)}, bf16[2,16,2048]{2,1,0:T(8,128)(2,1)S(1)}, u32[]{:S(2)}, u32[]{:S(2)}) collective-permute-start(bf16[2,16,2048]{2,1,0:T(8,128)(2,1)} %get-tuple-element.55), channel_id=1, source_target_pairs={{0,1},{1,2},{2,3},{3,4},{4,5},{5,6},{6,7},{7,8},{8,9},{9,10},{10,1... | collective-permute-start | bytes 393224 | tf_op jit(solution)/shard_map/ppermute | solution.py:275
  180.7 15.7 %collective-permute-start.14 = (bf16[2,16,2048]{2,1,0:T(8,128)(2,1)}, bf16[2,16,2048]{2,1,0:T(8,128)(2,1)S(1)}, u32[]{:S(2)}, u32[]{:S(2)}) collective-permute-start(bf16[2,16,2048]{2,1,0:T(8,128)(2,1)} %get-tuple-element.56), channel_id=1, source_target_pairs={{1,0},{2,1},{3,2},{4,3},{5,4},{6,5},{7,6},{8,7},{9,8},{10,9},{11,1... | collective-permute-start | bytes 393224 | tf_op jit(solution)/shard_map/ppermute | solution.py:276
  182.7 0.8 copy-start.1
